TPU v7x, 256 devices: a whole 4x4x8 slice. The times are simulated.
256 devices in a mesh: sec: 2 (over core), row: 8 (over y, z_lo), col: 16 (over z_hi, x).
Axes of the slice: x: 4, y: 4, z: 8 (z_hi: 4, z_lo: 2; z = z_hi * 2 + z_lo), core: 2. Of those that a mesh axis runs over, the one named last changes fastest.
Arguments:
- anc_inverse: float32 [4096, 4096], P('row', ('sec', 'col')), as said below
- panel: float32 [32768, 4096], P(('sec', 'col'), 'row'), may hold values from -0.375 to 0.375
- diag_inverse: float32 [32768, 512], P(('sec', 'col')), may hold values from -6 to 6
- widths: int32 [64], replicated, may hold values from 1 to 4, as said below
- pattern: int32 [64, 32], replicated, may hold values 0 or 1
Outputs:
- off_inverse: float32 [32768, 4096], P(('sec', 'col'), 'row')
- child_inverse: float32 [32768, 512], P(('sec', 'col'))
Inputs may be any that keep to these rules, and one draw needn't show every extreme that they name: `anc_inverse`: exactly symmetric. `widths`: both 1 and 4 occur in every draw.
All inputs are finite; a program needn't handle non-finite values.
Results may differ from a plain program's by a relative error of at most 0.0003.
Values sent between devices are 32-bit elements; how exact they have to be, the bound alone decides.
No kernel may reach another device: no remote copies, remote signals or barrier semaphores. Data moves between devices by JAX's collectives and lax.ppermute only.
A program may use at most 128 MiB of HBM per device.

v0:
```python
import jax
import jax.numpy as jnp
from jax import lax
from jax.sharding import PartitionSpec as P

B = 128
SW = 512


def mask_rows(values, slot_count, column_mask, block_mask, offset):
    amount = values.shape[1]
    window = lax.dynamic_slice_in_dim(block_mask, offset, amount, 1)
    shaped = (
        values.reshape(slot_count, SW, amount)
        * column_mask.reshape(slot_count, SW, 1)
        * window[:, None, :]
    )
    return shaped.reshape(slot_count * SW, amount)


def local(anc_inverse, panel, diag_inverse, widths, pattern):
    highest = lax.Precision.HIGHEST
    local_rows, rows_here = panel.shape
    slot_count = local_rows // SW
    slot_first = (lax.axis_index("sec") * lax.axis_size("col") + lax.axis_index("col")) * slot_count
    row_offset = lax.axis_index("row") * rows_here
    my_widths = lax.dynamic_slice_in_dim(widths, slot_first, slot_count)
    my_pattern = lax.dynamic_slice_in_dim(pattern, slot_first, slot_count, 0)
    block_mask = jnp.repeat(my_pattern.astype(jnp.float32), B, axis=1)
    position = jnp.arange(SW, dtype=jnp.int32)
    column_mask = (position[None, :] < my_widths[:, None] * B).astype(jnp.float32)
    anc_rows = lax.all_gather(anc_inverse, ("sec", "col"), axis=1, tiled=True)
    local_panel = mask_rows(panel, slot_count, column_mask, block_mask, row_offset)
    masked = mask_rows(
        lax.all_gather(panel, "row", axis=1, tiled=True),
        slot_count,
        column_mask,
        block_mask,
        jnp.int32(0),
    )
    product = lax.dot_general(
        masked,
        anc_rows,
        (((1,), (1,)), ((), ())),
        precision=highest,
        preferred_element_type=jnp.float32,
    )
    product = mask_rows(product, slot_count, column_mask, block_mask, row_offset)
    update = jnp.einsum(
        "jai,jbi->jab",
        product.reshape(slot_count, SW, rows_here),
        local_panel.reshape(slot_count, SW, rows_here),
        precision=highest,
    )
    summed = lax.psum(update.reshape(local_rows, SW), "row")
    pair_mask = column_mask[:, :, None] * column_mask[:, None, :]
    diag_block = (diag_inverse + summed) * pair_mask.reshape(local_rows, SW)
    return (-product, diag_block)


def solution(mesh):
    in_specs = (
        P("row", ("sec", "col")),
        P(("sec", "col"), "row"),
        P(("sec", "col"), None),
        P(),
        P(),
    )
    out_specs = (P(("sec", "col"), "row"), P(("sec", "col"), None))
    return jax.shard_map(local, mesh=mesh, in_specs=in_specs, out_specs=out_specs, check_vma=False)
```

profile of v0, /device:TPU:6, one launch (start us, length us, event | category | flops | bytes accessed | tf_op | source)
XLA Modules:
  0.0 584.7 jit_solution(12280549382512215505)
XLA Ops:
  7.2 0.0 copy-start
  7.2 0.0 copy-start.3
  7.2 0.0 all-gather.3.cloned.1.call-start
  7.2 0.7 all-gather.3.cloned.1.call-update
  7.9 0.0 all-gather.5.cloned.1.call-start
  8.0 0.7 all-gather.5.cloned.1.call-update
  8.7 0.0 all-reduce.2.cloned.1.call-start
  8.7 0.0 copy-done.3
  8.7 0.1 dynamic-slice_multiply_fusion
  8.8 0.1 compare_convert_fusion
  8.9 0.0 copy-done
  8.9 0.1 constant_dynamic-slice_fusion.1
  9.0 0.1 copy.9
  9.1 0.1 broadcast_bitcast_fusion
  9.2 331.8 %all-gather.3.cloned.1.call-done = f32[1024,4096]{1,0:T(8,128)} async-done(((f32[1024,512]{1,0:T(8,128)}), f32[1024,4096]{1,0:T(8,128)}) %all-gather.3.cloned.1.call-update) | async-done | bytes 16777232 | tf_op jit(solution)/shard_map/all_gather | solution.py:35
  341.0 12.0 %bitcast_multiply_fusion = f32[1024,4096]{1,0:T(8,128)} fusion(f32[1024,4096]{1,0:T(8,128)} %all-gather.3.cloned.1.call-done, f32[2,4096]{1,0:T(2,128)S(1)} %bitcast.28, f32[1024]{0:T(1024)S(1)} %bitcast.29), kind=kLoop, calls=%fused_computation | loop fusion | flops 8388608 | bytes 33591296 | tf_op jit(solution)/shard_map/mul | solution.py:14
  353.0 76.8 %all-gather.5.cloned.1.call-done = f32[512,4096]{1,0:T(8,128)} async-done(((f32[512,128]{1,0:T(8,128)}), f32[512,4096]{1,0:T(8,128)}) %all-gather.5.cloned.1.call-update) | async-done | bytes 8388624 | tf_op jit(solution)/shard_map/all_gather | solution.py:32
  429.8 0.0 copy-start.1
  429.8 31.5 %fusion.6 = (f32[2,512,512]{2,1,0:T(8,128)}, f32[2,512,512]{2,1,0:T(8,128)S(1)}) fusion(f32[2,512]{1,0:T(2,128)S(1)} %constant_dynamic-slice_fusion, f32[2,512]{1,0:T(2,128)S(1)} %get-tuple-element.2, f32[2,512,4096]{2,1,0:T(8,128)} %bitcast.24, f32[512,4096]{1,0:T(8,128)} %all-gather.5.cloned.1.call-done), kind=kOutput, calls=%fused_computation.9 | convolution fusion | flops 25771376640 | bytes 29368320 | tf_op jit(solution)/shard_map/dot_general | solution.py:41
  461.2 0.0 copy-done.1
  461.2 5.1 fusion.3
  466.4 0.0 copy-start.2
  466.4 0.0 all-reduce.2.cloned.1.call-update
  466.4 108.4 %all-reduce.2.cloned.1.call-done = f32[1024,512]{1,0:T(8,128)} async-done(((f32[1024,512]{1,0:T(8,128)}), f32[1024,512]{1,0:T(8,128)}) %all-reduce.2.cloned.1.call-update) | async-done | bytes 2097168 | tf_op jit(solution)/shard_map/psum | solution.py:55
  574.9 0.0 copy-done.2
  574.9 3.3 fusion.2
  (4 shorter events, 0.1 us)
Async XLA Ops:
  7.2 1.7 copy-start
  7.2 1.6 copy-start.3
  7.2 333.8 %all-gather.3.cloned.1.call-start = ((), (), s32[]{:S(2)}) async-start(), calls=%async_computation | async-start | bytes 18874368 | tf_op jit(solution)/shard_map/all_gather | solution.py:35
  7.9 421.8 %all-gather.5.cloned.1.call-start = ((), (), s32[]{:S(2)}) async-start(), calls=%async_computation.1 | async-start | bytes 8650752 | tf_op jit(solution)/shard_map/all_gather | solution.py:32
  8.7 566.2 %all-reduce.2.cloned.1.call-start = ((), (), s32[]{:S(2)}) async-start(), calls=%async_computation.2 | async-start | bytes 4194304 | tf_op jit(solution)/shard_map/psum | solution.py:55
  429.8 31.5 %copy-start.1 = (f32[1024,512]{1,0:T(8,128)S(1)}, f32[1024,512]{1,0:T(8,128)}, u32[]{:S(2)}) copy-start(f32[1024,512]{1,0:T(8,128)} %param.6) | copy-start | bytes 6291460
  466.4 108.5 %copy-start.2 = (f32[1024,512]{1,0:T(8,128)S(1)}, f32[1024,512]{1,0:T(8,128)}, u32[]{:S(2)}) copy-start(f32[1024,512]{1,0:T(8,128)} %param.7) | copy-start | bytes 6291460
Sparse Core Ops, SparseCore 0:
  9.8 331.1 all-gather.2
  343.5 86.2 all-gather.4
  466.5 108.2 all-reduce.1
where the time goes:
time: 586 us; the launch traced here: 585 us
  waiting for transfers between devices  518 us (88%)
  matrix products  36.6 us (6%)
  other arithmetic  15.4 us (3%)
  between operations  13.8 us (2%)
    all_gather x1, waiting for transfers between devices, local(): lax.all_gather(panel, 'row', axis=1, tiled=True)  332 us
    psum x1, waiting for transfers between devices, local(): summed = lax.psum(update.reshape(local_rows, SW), 'row')  108 us
    all_gather x1, waiting for transfers between devices, local(): anc_rows = lax.all_gather(anc_inverse, ('sec', 'col'), axis=1, tiled=True)  76.8 us
    dot_general x1, matrix products, local(): lax.dot_general(masked, anc_rows, (((1,), (1,)), ((), ())), precision=hig...  31.5 us
    mul x1, other arithmetic, mask_rows(): values.reshape(slot_count, SW, amount)  12 us
  transfers between devices with their start and end apart: 3, of which 3 were waited for; matrix products, arithmetic and copies ran while one was open for 2% of the time, Pallas kernels for 0%

commit v1 on v0

v1 whole, which is shorter than its diff:
```python
import functools

import jax
import jax.numpy as jnp
from jax import lax
from jax.experimental import pallas as pl
from jax.experimental.pallas import tpu as pltpu
from jax.sharding import Mesh, PartitionSpec as P

B = 128
SW = 512
WIDE = 2048
LIMIT = 18 * 2**20
ROW = ("y", "zl")
Z = ("zl", "zh")
DIRECTIONS = (0, 3, 1, 2)

VMEM = pl.BlockSpec(memory_space=pltpu.VMEM)
SMEM = pl.BlockSpec(memory_space=pltpu.SMEM)
F32 = jnp.float32
BF16 = jnp.bfloat16


def call(kernel, out_shape, specs, out_specs=None, scratch=(), aliases=None):
    single = not isinstance(out_shape, (tuple, list))
    return pl.pallas_call(
        kernel,
        out_shape=out_shape,
        in_specs=specs,
        out_specs=out_specs if out_specs is not None else (VMEM if single else [VMEM] * len(out_shape)),
        scratch_shapes=list(scratch),
        input_output_aliases=aliases or {},
        compiler_params=pltpu.CompilerParams(vmem_limit_bytes=LIMIT),
        cost_estimate=pl.CostEstimate(flops=1024, bytes_accessed=1024, transcendentals=0),
    )


def struct(shape, dtype=F32):
    return jax.ShapeDtypeStruct(shape, dtype)


def z_rounds():
    even = [
        {0: 0, 2: 1, 4: 4, 6: 5},
        {6: 0, 0: 1, 2: 4, 4: 5},
        {2: 0, 4: 1, 6: 4, 0: 5},
        {4: 0, 6: 1, 0: 4, 2: 5},
    ]
    rounds = []
    table = {}
    for k, pairs in enumerate(even):
        pairs = {**pairs, **{(3 - t) % 8: (3 - s) % 8 for t, s in pairs.items()}}
        rounds.append([((s % 2) * 4 + s // 2, (t % 2) * 4 + t // 2) for t, s in pairs.items()])
        for t, s in pairs.items():
            table[t, int(s % 2 == t % 2), (s // 2) // 2] = k
    return rounds, table


def step(value, axis, k, n=4):
    return lax.ppermute(value, axis, [(i, (i + k) % n) for i in range(n)])


def split(value):
    high = value.astype(BF16)
    return high, (value - high.astype(F32)).astype(BF16)


def dot3(a, b):
    dims = (((1,), (1,)), ((), ()))
    mul = functools.partial(lax.dot_general, dimension_numbers=dims, preferred_element_type=F32)
    return mul(a[0], b[0]) + (mul(a[0], b[1]) + mul(a[1], b[0]))


def meta_kernel(ids, widths, pattern, out):
    core, y, zl, zh, x = (ids[i] for i in range(5))
    first = ((core * 4 + zh) * 4 + x) * 2
    for child in range(2):
        for d, shift in enumerate(DIRECTIONS):
            block = ((y + shift) % 4 * 2 + zl) * 4
            for k in range(4):
                value = pattern[first + child, block + k].astype(F32)
                out[child : child + 1, (d * 4 + k) * B : (d * 4 + k + 1) * B] = jnp.full((1, B), value)
        out[2 + child : 3 + child, :] = jnp.full((1, WIDE), (widths[first + child] * B).astype(F32))
        block = (y * 2 + 1 - zl) * 4
        for k in range(4):
            value = pattern[first + child, block + k].astype(F32)
            out[4 + child : 5 + child, k * B : (k + 1) * B] = jnp.full((1, B), value)
        out[4 + child : 5 + child, SW:] = jnp.zeros((1, WIDE - SW), F32)
    out[6:8, :] = jnp.zeros((2, WIDE), F32)


def column_mask(meta, child):
    position = lax.broadcasted_iota(jnp.int32, (SW, B), 0).astype(F32)
    return (position < meta[2 + child : 3 + child, :B]).astype(F32)


def select_kernel(table, ids, r0, r1, r2, r3, other, own):
    z = ids[3] * 2 + ids[2]
    for role, out in enumerate((other, own)):
        for k in range(2):
            place = jnp.int32(0)
            for at in range(8):
                place = jnp.where(z == at, table[at, role, k], place)
            for i, source in enumerate((r0, r1, r2, r3)):

                @pl.when(place == i)
                def _():
                    out[k] = source[...]


def join_kernel(piece, left, right, top, bottom, out):
    out[0], out[1], out[2] = piece[...], left[...], right[...]
    out[3, 0], out[3, 1] = top[...], bottom[...]


def prepare_kernel(ids, mine, theirs, high, low):
    core, y, x = ids[0], ids[1], ids[4]
    for d, shift in enumerate(DIRECTIONS):
        block = (y + shift) % 4
        here = block // 2 == core
        for k in range(4):
            away = (k - x + 4) % 4
            at = jnp.where(away == 0, 0, jnp.where(away == 3, 1, jnp.where(away == 1, 2, 3)))
            columns = slice((d * 4 + k) * B, (d * 4 + k + 1) * B)

            def put(source):
                high[:, columns], low[:, columns] = split(source[at, block % 2])

            pl.when(here)(lambda: put(mine))
            pl.when(jnp.logical_not(here))(lambda: put(theirs))


def product_kernel(child, own, left, right, top, bottom, high, low, meta, out, phigh, plow):
    rows = own.shape[0]
    half = rows // 2
    mask = column_mask(meta, child)
    for d, source in enumerate((own, left, right, None)):
        for k in range(4):
            at = (d * 4 + k) * B
            lanes = slice(at, at + B)
            here = slice(k * B, (k + 1) * B)
            if source is None:
                parts = ((top, 0, half), (bottom, half, rows))
            else:
                parts = ((source, 0, rows),)
            for ref, low_row, high_row in parts:
                value = ref[:, here] * mask[low_row:high_row] * meta[child : child + 1, lanes]
                phigh[low_row:high_row, lanes], plow[low_row:high_row, lanes] = split(value)
    for n in range(0, 512, 256):
        b = (high[n : n + 256, :], low[n : n + 256, :])
        for r in range(0, rows, 256):
            out[r : r + 256, n : n + 256] = dot3((phigh[r : r + 256, :], plow[r : r + 256, :]), b)


def lower_blocks(update, pairs):
    at = 0
    for a in range(4):
        value = None
        for left, right in pairs:
            term = dot3([v[a * B : (a + 1) * B] for v in left], [v[: (a + 1) * B] for v in right])
            value = term if value is None else value + term
        for b in range(a + 1):
            update[at * B : (at + 1) * B, :] = value[:, b * B : (b + 1) * B]
            at += 1


def masked(child, panel, meta, row):
    wide = jnp.concatenate([column_mask(meta, child)] * 4, axis=1)
    return panel[...] * wide * meta[row : row + 1, :SW]


def finish_kernel(child, mine, received, panel, meta, *refs):
    wide = jnp.concatenate([column_mask(meta, child)] * 4, axis=1)
    product = (mine[...] + received[...]) * wide * meta[child : child + 1, :SW]
    if child == 0:
        off, update = refs
        lower_blocks(update, [(split(product), split(masked(child, panel, meta, child)))])
    else:
        off = refs[-1]
    off[...] = -product


def update_kernel(child, mine, theirs, panel, across, meta, update):
    lower_blocks(
        update,
        [
            (split(mine[...]), split(masked(child, panel, meta, child))),
            (split(theirs[...]), split(masked(child, across, meta, 4 + child))),
        ],
    )


def sum_kernel(parts, out):
    total = parts[0]
    for k in range(1, 8):
        total += parts[k]
    for k in range(8):
        out[k] = total


def child_kernel(parts, diag, meta, out):
    at = 0
    for child in range(2):
        across = lax.broadcasted_iota(jnp.int32, (1, SW), 1).astype(F32) < meta[2 + child : 3 + child, :SW]
        across = across.astype(F32)
        mask = column_mask(meta, child)
        for a in range(4):
            for b in range(a + 1):
                block = parts[at]
                at += 1
                for (i, j), value in {(b, a): block.T, (a, b): block}.items():
                    lines = slice(child * SW + i * B, child * SW + (i + 1) * B)
                    lanes = slice(j * B, (j + 1) * B)
                    rows = mask[i * B : (i + 1) * B]
                    out[lines, lanes] = (diag[lines, lanes] + value) * rows * across[:, lanes]


def after(value, *before):
    if not before:
        return value
    return lax.optimization_barrier((value, *before))[0]


def local(anc_inverse, panel, diag_inverse, widths, pattern):
    names = ("core", "y", "zl", "zh", "x")
    ids = jnp.stack([lax.axis_index(n) for n in names]).astype(jnp.int32)
    parts = [panel[:SW], panel[SW:]]

    def send_direct(i):
        return step(parts[i], "y", 1), step(parts[i], "y", -1)

    def send_relay(left, right):
        half = SW // 2
        return step(left[:half], "y", 1), step(right[half:], "y", -1)

    rounds, table = z_rounds()
    direct = [send_direct(0)]
    got = [lax.ppermute(anc_inverse, Z, pairs) for pairs in rounds]
    direct.append(send_direct(1))
    across = step(parts[1], "zl", 1, 2)
    relay = [send_relay(*direct[0]), send_relay(*direct[1])]

    got[0] = after(got[0], *direct[0])
    piece = struct((2, 512, B))
    pieces = call(functools.partial(select_kernel, table), (piece, piece), [SMEM] + [VMEM] * 4)(ids, *got)
    meta = call(meta_kernel, struct((8, WIDE)), [SMEM] * 3)(ids, widths, pattern)

    def gather(value, before, far, joined, swapped):
        value = after(value, *before)
        left, right = step(value, "x", 1), step(value, "x", -1)
        top, bottom = step(after(left[0], *far), "x", 1), step(after(right[1], *far), "x", -1)
        top = after(top, *joined)
        mine = call(join_kernel, struct((4, 2, 512, B)), [VMEM] * 5)(value, left, right, top, bottom)
        theirs = after(step(mine, "core", 1, 2), *swapped)
        pair = struct((512, WIDE), BF16)
        return call(prepare_kernel, (pair, pair), [SMEM, VMEM, VMEM])(ids, mine, theirs), (left, right)

    other, before = gather(pieces[0], (), relay[0], (across,), ())
    own, _ = gather(pieces[1], before, (), direct[1], relay[1])

    def product(child, anc):
        return call(
            functools.partial(product_kernel, child),
            struct((SW, SW)),
            [VMEM] * 8,
            scratch=[pltpu.VMEM((SW, WIDE), BF16)] * 2,
        )(parts[child], *direct[child], *relay[child], *anc, meta)

    theirs = [product(0, other)]
    received = [step(theirs[0], "zl", 1, 2)]
    parts[1] = after(parts[1], theirs[0])
    theirs.append(product(1, other))
    received.append(step(theirs[1], "zl", 1, 2))
    mine = [product(child, own) for child in range(2)]

    packed = struct((10 * B, B))
    params = dict(
        grid=(1,),
        compiler_params=pltpu.CompilerParams(vmem_limit_bytes=LIMIT),
        cost_estimate=pl.CostEstimate(flops=1024, bytes_accessed=1024, transcendentals=0),
    )

    def block(child):
        return pl.BlockSpec((SW, SW), lambda g: (child, 0))

    anywhere = pl.BlockSpec(memory_space=pl.ANY)
    off, first = pl.pallas_call(
        functools.partial(finish_kernel, 0),
        out_shape=(struct(panel.shape), packed),
        in_specs=[VMEM, VMEM, block(0), VMEM],
        out_specs=[block(0), VMEM],
        **params,
    )(mine[0], received[0], panel, meta)
    second = call(functools.partial(update_kernel, 1), packed, [VMEM] * 5)(
        mine[1], theirs[1], parts[1], across, meta
    )
    off = pl.pallas_call(
        functools.partial(finish_kernel, 1),
        out_shape=struct(panel.shape),
        in_specs=[VMEM, VMEM, block(1), VMEM, anywhere],
        out_specs=block(1),
        input_output_aliases={4: 0},
        **params,
    )(mine[1], received[1], panel, meta, off)

    def swap(value):
        return lax.all_to_all(value, ROW, 0, 0, tiled=True)

    shape = (8, 20 * B // 8, B)
    spread = swap(jnp.concatenate([first, second], axis=0).reshape(shape))
    spread = after(spread, received[1])
    summed = swap(call(sum_kernel, struct(shape), [VMEM])(spread)).reshape(20, B, B)
    out = call(child_kernel, struct(diag_inverse.shape), [VMEM] * 3)(summed, diag_inverse, meta)
    return off, out


def solution(mesh):
    fine = Mesh(mesh.devices.reshape(2, 4, 2, 4, 4), ("core", "y", "zl", "zh", "x"))
    group = ("core", "zh", "x")
    in_specs = (P(ROW, group), P(group, ROW), P(group, None), P(), P())
    out_specs = (P(group, ROW), P(group, None))
    return jax.shard_map(local, mesh=fine, in_specs=in_specs, out_specs=out_specs, check_vma=False)
```

time: 586 us -> 235 us (0.40)
  waiting for transfers between devices: 518 us -> 111 us
  starting transfers between devices: 0.11 us -> 64.2 us
  Pallas kernels: 0 us -> 42.5 us
  matrix products: 36.6 us -> 0 us
  other arithmetic: 15.4 us -> 1.14 us
  between operations: 13.8 us -> 1.21 us
  local copies, waits for them, and re-layouts: 0.29 us -> 10.8 us
    all_gather x2 -> x0, waiting for transfers between devices: 409 us -> none  [the longest x1 332 us: local(): lax.all_gather(panel, 'row', axis=1, tiled=True)]
    psum x1 -> x0, waiting for transfers between devices: 108 us -> none  [local(): summed = lax.psum(update.reshape(local_rows, SW), 'row')]
    ppermute x0 -> x25, waiting for transfers between devices: none -> 97 us  [the longest x21 87.6 us: step(): return lax.ppermute(value, axis, [(i, (i + k) % n) for i in range(n)])]
    ppermute x0 -> x25, starting transfers between devices: none -> 54 us  [the longest x21 42.3 us: step(): return lax.ppermute(value, axis, [(i, (i + k) % n) for i in range(n)])]
    pallas_call x0 -> x15, Pallas kernels: none -> 42.5 us  [the longest x4 19.8 us: product(): call(functools.partial(product_kernel, child), struct((SW, SW)), [VMEM] *...]
    dot_general x2 -> x0, matrix products: 36.6 us -> none  [the longest x1 31.5 us: local(): lax.dot_general(masked, anc_rows, (((1,), (1,)), ((), ())), precision=hig...]
    mul x3 -> x0, other arithmetic: 15.3 us -> none  [the longest x1 12 us: mask_rows(): values.reshape(slot_count, SW, amount)]
    all_to_all x0 -> x2, waiting for transfers between devices: none -> 14.5 us  [swap(): return lax.all_to_all(value, ROW, 0, 0, tiled=True)]
  transfers between devices with their start and end apart: 3 -> 27, of which waited for: 3 -> 17; matrix products, arithmetic and copies ran while one was open for 2% -> 1% of each run, Pallas kernels for 0% -> 15%
where the time goes in v1:
time: 235 us; the launch traced here: 231 us
  waiting for transfers between devices  111 us (47%)
  starting transfers between devices  64.2 us (27%)
  Pallas kernels  42.5 us (18%)
  local copies, waits for them, and re-layouts  10.8 us (5%)
    ppermute x21, waiting for transfers between devices, step(): return lax.ppermute(value, axis, [(i, (i + k) % n) for i in range(n)])  87.6 us
    ppermute x21, starting transfers between devices, step(): return lax.ppermute(value, axis, [(i, (i + k) % n) for i in range(n)])  42.3 us
    pallas_call x4, Pallas kernels, product(): call(functools.partial(product_kernel, child), struct((SW, SW)), [VMEM] *...  19.8 us
    all_to_all x2, waiting for transfers between devices, swap(): return lax.all_to_all(value, ROW, 0, 0, tiled=True)  14.5 us
    ppermute x4, starting transfers between devices, local(): got = [lax.ppermute(anc_inverse, Z, pairs) for pairs in rounds]  11.7 us
    all_to_all x2, starting transfers between devices, swap(): return lax.all_to_all(value, ROW, 0, 0, tiled=True)  10.2 us
    ppermute x4, waiting for transfers between devices, local(): got = [lax.ppermute(anc_inverse, Z, pairs) for pairs in rounds]  9.37 us
    unnamed x41, local copies, waits for them, and re-layouts  7.78 us
  transfers between devices with their start and end apart: 27, of which 17 were waited for; matrix products, arithmetic and copies ran while one was open for 1% of the time, Pallas kernels for 15%

profile of v1, /device:TPU:6, one launch (start us, length us, event | category | flops | bytes accessed | tf_op | source)
XLA Modules:
  0.0 231.3 jit_solution(1606354549847423457)
XLA Ops:
  0.6 1.7 fusion
  2.3 1.7 collective-permute-start
  4.0 1.7 collective-permute-start.1
  7.3 7.7 %collective-permute-start.5 = (f32[512,128]{1,0:T(8,128)}, f32[512,128]{1,0:T(8,128)}, u32[]{:S(2)}, u32[]{:S(2)}) collective-permute-start(f32[512,128]{1,0:T(8,128)} %param.5), channel_id=1, source_target_pairs={{0,12},{16,0},{8,4},{24,8},{20,24},{4,20},{28,16},{12,28},{1,13},{... | collective-permute-start | bytes 786440 | tf_op jit(solution)/shard_map/ppermute | solution.py:238
  15.0 2.5 %collective-permute-start.7 = (f32[512,128]{1,0:T(8,128)}, f32[512,128]{1,0:T(8,128)}, u32[]{:S(2)}, u32[]{:S(2)}) collective-permute-start(f32[512,128]{1,0:T(8,128)} %param.5), channel_id=1, source_target_pairs={{0,8},{16,12},{8,0},{24,4},{20,28},{4,24},{28,20},{12,16},{1,9},{1... | collective-permute-start | bytes 786440 | tf_op jit(solution)/shard_map/ppermute | solution.py:238
  17.5 11.1 %collective-permute-done.left = f32[512,512]{1,0:T(8,128)S(1)} collective-permute-done((f32[512,512]{1,0:T(8,128)S(1)}, f32[512,512]{1,0:T(8,128)S(1)}, u32[]{:S(2)}, u32[]{:S(2)}) %collective-permute-start) | collective-permute-done | bytes 1048608 | tf_op jit(solution)/shard_map/ppermute | solution.py:60
  28.7 9.4 %collective-permute-done.6.r2 = f32[512,128]{1,0:T(8,128)} collective-permute-done((f32[512,128]{1,0:T(8,128)}, f32[512,128]{1,0:T(8,128)}, u32[]{:S(2)}, u32[]{:S(2)}) %collective-permute-start.6) | collective-permute-done | bytes 262176 | tf_op jit(solution)/shard_map/ppermute | solution.py:238
  39.9 4.6 %collective-permute-start.11 = (f32[512,512]{1,0:T(8,128)S(1)}, f32[512,512]{1,0:T(8,128)S(1)}, u32[]{:S(2)}, u32[]{:S(2)}) collective-permute-start(f32[512,512]{1,0:T(8,128)S(1)} %get-tuple-element.26.own.panel), channel_id=1, source_target_pairs={{0,16},{16,0},{1,17},{17,1},{2,18},{18,2},{3,19},{19,3},{4,20},{20... | collective-permute-start | bytes 3145736 | tf_op jit(solution)/shard_map/ppermute | solution.py:60
  45.7 3.3 %collective-permute-start.3 = (f32[256,512]{1,0:T(8,128)S(1)}, f32[256,512]{1,0:T(8,128)S(1)}, u32[]{:S(2)}, u32[]{:S(2)}) collective-permute-start(f32[256,512]{1,0:T(8,128)S(1)} %slice.41), channel_id=1, source_target_pairs={{0,96},{32,0},{64,32},{96,64},{1,97},{33,1},{65,33},{97,65},{2,98}... | collective-permute-start | bytes 1572872 | tf_op jit(solution)/shard_map/ppermute | solution.py:60
  51.8 5.0 %collective-permute-done.2.top = f32[256,512]{1,0:T(8,128)S(1)} collective-permute-done((f32[256,512]{1,0:T(8,128)S(1)}, f32[256,512]{1,0:T(8,128)S(1)}, u32[]{:S(2)}, u32[]{:S(2)}) %collective-permute-start.2) | collective-permute-done | bytes 524320 | tf_op jit(solution)/shard_map/ppermute | solution.py:60
  62.6 1.7 collective-permute-start.18
  66.2 2.4 %collective-permute-start.15 = (f32[512,512]{1,0:T(8,128)S(1)}, f32[512,512]{1,0:T(8,128)S(1)}, u32[]{:S(2)}, u32[]{:S(2)}) collective-permute-start(f32[512,512]{1,0:T(8,128)S(1)} %get-tuple-element.26.own.panel), channel_id=1, source_target_pairs={{0,96},{32,0},{64,32},{96,64},{1,97},{33,1},{65,33},{97,65},{2,98}... | collective-permute-start | bytes 3145736 | tf_op jit(solution)/shard_map/ppermute | solution.py:60
  70.8 2.6 %collective-permute-done.18.left = f32[2,512,128]{2,1,0:T(8,128)S(1)} collective-permute-done((f32[2,512,128]{2,1,0:T(8,128)S(1)}, f32[2,512,128]{2,1,0:T(8,128)S(1)}, u32[]{:S(2)}, u32[]{:S(2)}) %collective-permute-start.18) | collective-permute-done | bytes 524320 | tf_op jit(solution)/shard_map/ppermute | solution.py:60
  73.4 3.8 %collective-permute-start.20 = (f32[512,128]{1,0:T(8,128)S(1)}, f32[512,128]{1,0:T(8,128)S(1)}, u32[]{:S(2)}, u32[]{:S(2)}) collective-permute-start(f32[512,128]{1,0:T(8,128)S(1)} %slice_bitcast_fusion.1), channel_id=1, source_target_pairs={{0,1},{1,2},{2,3},{3,0},{4,5},{5,6},{6,7},{7,4},{8,9},{9,10},{10,1... | collective-permute-start | bytes 786440 | tf_op jit(solution)/shard_map/ppermute | solution.py:60
  77.2 8.7 %collective-permute-done.19.right = f32[2,512,128]{2,1,0:T(8,128)S(1)} collective-permute-done((f32[2,512,128]{2,1,0:T(8,128)S(1)}, f32[2,512,128]{2,1,0:T(8,128)S(1)}, u32[]{:S(2)}, u32[]{:S(2)}) %collective-permute-start.19) | collective-permute-done | bytes 524320 | tf_op jit(solution)/shard_map/ppermute | solution.py:60
  86.1 1.9 collective-permute-done.15.right
  89.0 6.1 %collective-permute-done.21.bottom = f32[512,128]{1,0:T(8,128)S(1)} collective-permute-done((f32[512,128]{1,0:T(8,128)S(1)}, f32[512,128]{1,0:T(8,128)S(1)}, u32[]{:S(2)}, u32[]{:S(2)}) %collective-permute-start.21) | collective-permute-done | bytes 262176 | tf_op jit(solution)/shard_map/ppermute | solution.py:60
  97.9 3.7 %shard_map.70 = (bf16[512,2048]{1,0:T(8,128)(2,1)S(1)}, bf16[512,2048]{1,0:T(8,128)(2,1)S(1)}) custom-call(s32[5]{0:T(128)S(1)} %stack.23.ids, f32[4,2,512,128]{3,2,1,0:T(8,128)} %shard_map.69.mine, f32[4,2,512,128]{3,2,1,0:T(8,128)} %collective-permute-done.13.theirs), custom_call_target="tpu_custom_call" | custom-call | flops 1024 | bytes 1024 | tf_op jit(solution)/shard_map/pallas_call | solution.py:256
  101.6 5.6 %shard_map.72 = f32[512,512]{1,0:T(8,128)S(1)} custom-call(f32[512,512]{1,0:T(8,128)S(1)} %get-tuple-element.36.own, f32[512,512]{1,0:T(8,128)S(1)} %collective-permute-done.left, f32[512,512]{1,0:T(8,128)} %collective-permute-done.1.right, f32[256,512]{1,0:T(8,128)S(1)} %copy-done.10, f32[256,512]{1,0:T(8,128)S(1)} %copy-done.12, ...), custom_call_target="tpu_custom_call" | custom-call | flops 1024 | bytes 1024 | tf_op jit(solution)/shard_map/pallas_call | solution.py:262
  108.7 13.8 %collective-permute-start.17 = (f32[256,512]{1,0:T(8,128)S(1)}, f32[256,512]{1,0:T(8,128)S(1)}, u32[]{:S(2)}, u32[]{:S(2)}) collective-permute-start(f32[256,512]{1,0:T(8,128)S(1)} %slice.45), channel_id=1, source_target_pairs={{0,96},{32,0},{64,32},{96,64},{1,97},{33,1},{65,33},{97,65},{2,98}... | collective-permute-start | bytes 1572872 | tf_op jit(solution)/shard_map/ppermute | solution.py:60
  123.0 11.3 %collective-permute-done.17.bottom = f32[256,512]{1,0:T(8,128)S(1)} collective-permute-done((f32[256,512]{1,0:T(8,128)S(1)}, f32[256,512]{1,0:T(8,128)S(1)}, u32[]{:S(2)}, u32[]{:S(2)}) %collective-permute-start.17) | collective-permute-done | bytes 524320 | tf_op jit(solution)/shard_map/ppermute | solution.py:60
  134.3 4.2 %shard_map.76.theirs = f32[512,512]{1,0:T(8,128)S(1)} custom-call(f32[512,512]{1,0:T(8,128)S(1)} %get-tuple-element.26.own.panel, f32[512,512]{1,0:T(8,128)S(1)} %copy-done.4, f32[512,512]{1,0:T(8,128)S(1)} %copy-done.6, f32[256,512]{1,0:T(8,128)S(1)} %collective-permute-done.16.top, f32[256,512]{1,0:T(8,128)S(1)} %collective-permute-done.17.bottom, ...), custom_call_target="tpu_custom_call" | custom-call | flops 1024 | bytes 1024 | tf_op jit(solution)/shard_map/pallas_call | solution.py:262
  138.5 4.0 %shard_map.74 = (bf16[512,2048]{1,0:T(8,128)(2,1)S(1)}, bf16[512,2048]{1,0:T(8,128)(2,1)S(1)}) custom-call(s32[5]{0:T(128)S(1)} %stack.23.ids, f32[4,2,512,128]{3,2,1,0:T(8,128)} %shard_map.73.mine, f32[4,2,512,128]{3,2,1,0:T(8,128)} %collective-permute-done.22.theirs), custom_call_target="tpu_custom_call" | custom-call | flops 1024 | bytes 1024 | tf_op jit(solution)/shard_map/pallas_call | solution.py:256
  142.5 4.2 %shard_map.75.mine = f32[512,512]{1,0:T(8,128)S(1)} custom-call(f32[512,512]{1,0:T(8,128)S(1)} %get-tuple-element.26.own.panel, f32[512,512]{1,0:T(8,128)S(1)} %copy-done.4, f32[512,512]{1,0:T(8,128)S(1)} %copy-done.6, f32[256,512]{1,0:T(8,128)S(1)} %collective-permute-done.16.top, f32[256,512]{1,0:T(8,128)S(1)} %collective-permute-done.17.bottom, ...), custom_call_target="tpu_custom_call" | custom-call | flops 1024 | bytes 1024 | tf_op jit(solution)/shard_map/pallas_call | solution.py:262
  146.7 5.8 %shard_map.77.mine = f32[512,512]{1,0:T(8,128)S(1)} custom-call(f32[512,512]{1,0:T(8,128)S(1)} %get-tuple-element.36.own, f32[512,512]{1,0:T(8,128)S(1)} %collective-permute-done.left, f32[512,512]{1,0:T(8,128)} %collective-permute-done.1.right, f32[256,512]{1,0:T(8,128)S(1)} %copy-done.10, f32[256,512]{1,0:T(8,128)S(1)} %copy-done.12, ...), custom_call_target="tpu_custom_call" | custom-call | flops 1024 | bytes 1024 | tf_op jit(solution)/shard_map/pallas_call | solution.py:262
  152.6 2.6 %shard_map.80 = f32[1280,128]{1,0:T(8,128)S(1)} custom-call(f32[512,512]{1,0:T(8,128)S(1)} %shard_map.75.mine, f32[512,512]{1,0:T(8,128)S(1)} %shard_map.76.theirs, f32[512,512]{1,0:T(8,128)S(1)} %get-tuple-element.26.own.panel, f32[512,512]{1,0:T(8,128)S(1)} %copy-done.15, f32[8,2048]{1,0:T(8,128)S(1)} %shard_map.71.meta), custom_call_target="tpu_custom_call" | custom-call | flops 1024 | bytes 1024 | tf_op jit(solution)/shard_map/pallas_call | solution.py:294
  158.0 5.9 %all-to-all-start = ((f32[8,320,128]{2,1,0:T(8,128)}), f32[8,320,128]{2,1,0:T(8,128)}, u32[]{:S(2)}, u32[]{:S(2)}) async-start(f32[8,320,128]{2,1,0:T(8,128)} %bitcast.15), calls=%async_computation | async-start | bytes 2621440 | tf_op jit(solution)/shard_map/all_to_all | solution.py:307
  163.8 2.0 collective-permute-start.23
  165.9 36.1 %collective-permute-done.23.received = f32[512,512]{1,0:T(8,128)S(1)} collective-permute-done((f32[512,512]{1,0:T(8,128)}, f32[512,512]{1,0:T(8,128)S(1)}, u32[]{:S(2)}, u32[]{:S(2)}) %collective-permute-start.23) | collective-permute-done | bytes 1048608 | tf_op jit(solution)/shard_map/ppermute | solution.py:60
  205.4 4.3 %all-to-all-start.1 = ((f32[8,320,128]{2,1,0:T(8,128)}), f32[8,320,128]{2,1,0:T(8,128)}, u32[]{:S(2)}, u32[]{:S(2)}) async-start(f32[8,320,128]{2,1,0:T(8,128)} %copy-done.7), calls=%async_computation.1 | async-start | bytes 2621440 | tf_op jit(solution)/shard_map/all_to_all | solution.py:307
  212.1 14.5 %all-to-all-done.1 = f32[8,320,128]{2,1,0:T(8,128)} async-done(((f32[8,320,128]{2,1,0:T(8,128)}), f32[8,320,128]{2,1,0:T(8,128)}, u32[]{:S(2)}, u32[]{:S(2)}) %all-to-all-start.1) | async-done | bytes 1310752 | tf_op jit(solution)/shard_map/all_to_all | solution.py:307
  228.2 2.9 %shard_map.82 = f32[1024,512]{1,0:T(8,128)} custom-call(f32[20,128,128]{2,1,0:T(8,128)} %bitcast.10.parts, f32[1024,512]{1,0:T(8,128)S(1)} %copy-done.13, f32[8,2048]{1,0:T(8,128)S(1)} %shard_map.71.meta), custom_call_target="tpu_custom_call" | custom-call | flops 1024 | bytes 1024 | tf_op jit(solution)/shard_map/pallas_call | solution.py:313
  (89 shorter events, 33.7 us)
Async XLA Ops:
  2.3 26.3 %collective-permute-start = (f32[512,512]{1,0:T(8,128)S(1)}, f32[512,512]{1,0:T(8,128)S(1)}, u32[]{:S(2)}, u32[]{:S(2)}) collective-permute-start(f32[512,512]{1,0:T(8,128)S(1)} %get-tuple-element.36.own), channel_id=1, source_target_pairs={{0,32},{32,64},{64,96},{96,0},{1,33},{33,65},{65,97},{97,1},{2,34}... | collective-permute-start | bytes 3145736 | tf_op jit(solution)/shard_map/ppermute | solution.py:60
  4.0 24.7 %collective-permute-start.1 = (f32[512,512]{1,0:T(8,128)S(1)}, f32[512,512]{1,0:T(8,128)}, u32[]{:S(2)}, u32[]{:S(2)}) collective-permute-start(f32[512,512]{1,0:T(8,128)S(1)} %get-tuple-element.36.own), channel_id=1, source_target_pairs={{0,96},{32,0},{64,32},{96,64},{1,97},{33,1},{65,33},{97,65},{2,98}... | collective-permute-start | bytes 3145736 | tf_op jit(solution)/shard_map/ppermute | solution.py:60
  5.7 9.3 %collective-permute-start.4 = (f32[512,128]{1,0:T(8,128)}, f32[512,128]{1,0:T(8,128)S(1)}, u32[]{:S(2)}, u32[]{:S(2)}) collective-permute-start(f32[512,128]{1,0:T(8,128)} %param.5), channel_id=1, source_target_pairs={{0,0},{16,4},{8,8},{24,12},{20,20},{4,16},{28,28},{12,24},{1,1},{1... | collective-permute-start | bytes 786440 | tf_op jit(solution)/shard_map/ppermute | solution.py:238
  7.3 21.5 %collective-permute-start.5 = (f32[512,128]{1,0:T(8,128)}, f32[512,128]{1,0:T(8,128)}, u32[]{:S(2)}, u32[]{:S(2)}) collective-permute-start(f32[512,128]{1,0:T(8,128)} %param.5), channel_id=1, source_target_pairs={{0,12},{16,0},{8,4},{24,8},{20,24},{4,20},{28,16},{12,28},{1,13},{... | collective-permute-start | bytes 786440 | tf_op jit(solution)/shard_map/ppermute | solution.py:238
  15.0 23.1 %collective-permute-start.6 = (f32[512,128]{1,0:T(8,128)}, f32[512,128]{1,0:T(8,128)}, u32[]{:S(2)}, u32[]{:S(2)}) collective-permute-start(f32[512,128]{1,0:T(8,128)} %param.5), channel_id=1, source_target_pairs={{0,4},{16,8},{8,12},{24,0},{20,16},{4,28},{28,24},{12,20},{1,5},{1... | collective-permute-start | bytes 786440 | tf_op jit(solution)/shard_map/ppermute | solution.py:238
  15.0 23.1 %collective-permute-start.7 = (f32[512,128]{1,0:T(8,128)}, f32[512,128]{1,0:T(8,128)}, u32[]{:S(2)}, u32[]{:S(2)}) collective-permute-start(f32[512,128]{1,0:T(8,128)} %param.5), channel_id=1, source_target_pairs={{0,8},{16,12},{8,0},{24,4},{20,28},{4,24},{28,20},{12,16},{1,9},{1... | collective-permute-start | bytes 786440 | tf_op jit(solution)/shard_map/ppermute | solution.py:238
  39.4 12.4 %collective-permute-start.8 = (f32[2,512,128]{2,1,0:T(8,128)S(1)}, f32[2,512,128]{2,1,0:T(8,128)S(1)}, u32[]{:S(2)}, u32[]{:S(2)}) collective-permute-start(f32[2,512,128]{2,1,0:T(8,128)S(1)} %get-tuple-element.20.piece), channel_id=1, source_target_pairs={{0,1},{1,2},{2,3},{3,0},{4,5},{5,6},{6,7},{7,4},{8,9},{9,10},{10,1... | collective-permute-start | bytes 1572872 | tf_op jit(solution)/shard_map/ppermute | solution.py:60
  39.9 25.3 %collective-permute-start.11 = (f32[512,512]{1,0:T(8,128)S(1)}, f32[512,512]{1,0:T(8,128)S(1)}, u32[]{:S(2)}, u32[]{:S(2)}) collective-permute-start(f32[512,512]{1,0:T(8,128)S(1)} %get-tuple-element.26.own.panel), channel_id=1, source_target_pairs={{0,16},{16,0},{1,17},{17,1},{2,18},{18,2},{3,19},{19,3},{4,20},{20... | collective-permute-start | bytes 3145736 | tf_op jit(solution)/shard_map/ppermute | solution.py:60
  44.5 12.2 %collective-permute-start.2 = (f32[256,512]{1,0:T(8,128)S(1)}, f32[256,512]{1,0:T(8,128)S(1)}, u32[]{:S(2)}, u32[]{:S(2)}) collective-permute-start(f32[256,512]{1,0:T(8,128)S(1)} %slice.40), channel_id=1, source_target_pairs={{0,32},{32,64},{64,96},{96,0},{1,33},{33,65},{65,97},{97,1},{2,34}... | collective-permute-start | bytes 1572872 | tf_op jit(solution)/shard_map/ppermute | solution.py:60
  45.7 11.5 %collective-permute-start.3 = (f32[256,512]{1,0:T(8,128)S(1)}, f32[256,512]{1,0:T(8,128)S(1)}, u32[]{:S(2)}, u32[]{:S(2)}) collective-permute-start(f32[256,512]{1,0:T(8,128)S(1)} %slice.41), channel_id=1, source_target_pairs={{0,96},{32,0},{64,32},{96,64},{1,97},{33,1},{65,33},{97,65},{2,98}... | collective-permute-start | bytes 1572872 | tf_op jit(solution)/shard_map/ppermute | solution.py:60
  49.0 12.0 %collective-permute-start.9 = (f32[2,512,128]{2,1,0:T(8,128)S(1)}, f32[2,512,128]{2,1,0:T(8,128)S(1)}, u32[]{:S(2)}, u32[]{:S(2)}) collective-permute-start(f32[2,512,128]{2,1,0:T(8,128)S(1)} %get-tuple-element.20.piece), channel_id=1, source_target_pairs={{0,3},{1,0},{2,1},{3,2},{4,7},{5,4},{6,5},{7,6},{8,11},{9,8},{10,9... | collective-permute-start | bytes 1572872 | tf_op jit(solution)/shard_map/ppermute | solution.py:60
  56.8 8.4 %copy-start.9 = (f32[256,512]{1,0:T(8,128)}, f32[256,512]{1,0:T(8,128)S(1)}, u32[]{:S(2)}) copy-start(f32[256,512]{1,0:T(8,128)S(1)} %collective-permute-done.2.top) | copy-start | bytes 1572868
  58.0 10.6 %collective-permute-start.10 = (f32[512,128]{1,0:T(8,128)S(1)}, f32[512,128]{1,0:T(8,128)S(1)}, u32[]{:S(2)}, u32[]{:S(2)}) collective-permute-start(f32[512,128]{1,0:T(8,128)S(1)} %slice_bitcast_fusion.3), channel_id=1, source_target_pairs={{0,1},{1,2},{2,3},{3,0},{4,5},{5,6},{6,7},{7,4},{8,9},{9,10},{10,1... | collective-permute-start | bytes 786440 | tf_op jit(solution)/shard_map/ppermute | solution.py:60
  61.0 7.7 %collective-permute-start.12 = (f32[512,128]{1,0:T(8,128)S(1)}, f32[512,128]{1,0:T(8,128)S(1)}, u32[]{:S(2)}, u32[]{:S(2)}) collective-permute-start(f32[512,128]{1,0:T(8,128)S(1)} %slice_bitcast_fusion.2), channel_id=1, source_target_pairs={{0,3},{1,0},{2,1},{3,2},{4,7},{5,4},{6,5},{7,6},{8,11},{9,8},{10,9... | collective-permute-start | bytes 786440 | tf_op jit(solution)/shard_map/ppermute | solution.py:60
  62.6 10.8 %collective-permute-start.18 = (f32[2,512,128]{2,1,0:T(8,128)S(1)}, f32[2,512,128]{2,1,0:T(8,128)S(1)}, u32[]{:S(2)}, u32[]{:S(2)}) collective-permute-start(f32[2,512,128]{2,1,0:T(8,128)S(1)} %get-tuple-element.28.piece), channel_id=1, source_target_pairs={{0,1},{1,2},{2,3},{3,0},{4,5},{5,6},{6,7},{7,4},{8,9},{9,10},{10,1... | collective-permute-start | bytes 1572872 | tf_op jit(solution)/shard_map/ppermute | solution.py:60
  64.3 21.7 %collective-permute-start.14 = (f32[512,512]{1,0:T(8,128)S(1)}, f32[512,512]{1,0:T(8,128)S(1)}, u32[]{:S(2)}, u32[]{:S(2)}) collective-permute-start(f32[512,512]{1,0:T(8,128)S(1)} %get-tuple-element.26.own.panel), channel_id=1, source_target_pairs={{0,32},{32,64},{64,96},{96,0},{1,33},{33,65},{65,97},{97,1},{2,34}... | collective-permute-start | bytes 3145736 | tf_op jit(solution)/shard_map/ppermute | solution.py:60
  66.2 21.8 %collective-permute-start.15 = (f32[512,512]{1,0:T(8,128)S(1)}, f32[512,512]{1,0:T(8,128)S(1)}, u32[]{:S(2)}, u32[]{:S(2)}) collective-permute-start(f32[512,512]{1,0:T(8,128)S(1)} %get-tuple-element.26.own.panel), channel_id=1, source_target_pairs={{0,96},{32,0},{64,32},{96,64},{1,97},{33,1},{65,33},{97,65},{2,98}... | collective-permute-start | bytes 3145736 | tf_op jit(solution)/shard_map/ppermute | solution.py:60
  70.1 27.8 %collective-permute-start.13 = (f32[4,2,512,128]{3,2,1,0:T(8,128)}, f32[4,2,512,128]{3,2,1,0:T(8,128)}, u32[]{:S(2)}, u32[]{:S(2)}) collective-permute-start(f32[4,2,512,128]{3,2,1,0:T(8,128)} %shard_map.69.mine), channel_id=1, source_target_pairs={{0,128},{128,0},{1,129},{129,1},{2,130},{130,2},{3,131},{131,3},{4... | collective-permute-start | bytes 6291464 | tf_op jit(solution)/shard_map/ppermute | solution.py:60
  70.4 15.5 %collective-permute-start.19 = (f32[2,512,128]{2,1,0:T(8,128)S(1)}, f32[2,512,128]{2,1,0:T(8,128)S(1)}, u32[]{:S(2)}, u32[]{:S(2)}) collective-permute-start(f32[2,512,128]{2,1,0:T(8,128)S(1)} %get-tuple-element.28.piece), channel_id=1, source_target_pairs={{0,3},{1,0},{2,1},{3,2},{4,7},{5,4},{6,5},{7,6},{8,11},{9,8},{10,9... | collective-permute-start | bytes 1572872 | tf_op jit(solution)/shard_map/ppermute | solution.py:60
  73.4 14.6 %collective-permute-start.20 = (f32[512,128]{1,0:T(8,128)S(1)}, f32[512,128]{1,0:T(8,128)S(1)}, u32[]{:S(2)}, u32[]{:S(2)}) collective-permute-start(f32[512,128]{1,0:T(8,128)S(1)} %slice_bitcast_fusion.1), channel_id=1, source_target_pairs={{0,1},{1,2},{2,3},{3,0},{4,5},{5,6},{6,7},{7,4},{8,9},{9,10},{10,1... | collective-permute-start | bytes 786440 | tf_op jit(solution)/shard_map/ppermute | solution.py:60
  86.0 10.6 %copy-start.19 = (s32[64,32]{0,1:T(8,128)S(1)}, s32[64,32]{0,1:T(8,128)}, u32[]{:S(2)}) copy-start(s32[64,32]{0,1:T(8,128)} %param.9) | copy-start | bytes 24580
  86.0 10.7 %copy-start.18 = (s32[64]{0:T(128)S(1)}, s32[64]{0:T(128)}, u32[]{:S(2)}) copy-start(s32[64]{0:T(128)} %widths.1) | copy-start | bytes 772
  86.0 9.1 %collective-permute-start.21 = (f32[512,128]{1,0:T(8,128)S(1)}, f32[512,128]{1,0:T(8,128)S(1)}, u32[]{:S(2)}, u32[]{:S(2)}) collective-permute-start(f32[512,128]{1,0:T(8,128)S(1)} %slice_bitcast_fusion), channel_id=1, source_target_pairs={{0,3},{1,0},{2,1},{3,2},{4,7},{5,4},{6,5},{7,6},{8,11},{9,8},{10,9... | collective-permute-start | bytes 786440 | tf_op jit(solution)/shard_map/ppermute | solution.py:60
  96.6 41.9 %collective-permute-start.22 = (f32[4,2,512,128]{3,2,1,0:T(8,128)}, f32[4,2,512,128]{3,2,1,0:T(8,128)}, u32[]{:S(2)}, u32[]{:S(2)}) collective-permute-start(f32[4,2,512,128]{3,2,1,0:T(8,128)} %shard_map.73.mine), channel_id=1, source_target_pairs={{0,128},{128,0},{1,129},{129,1},{2,130},{130,2},{3,131},{131,3},{4... | collective-permute-start | bytes 6291464 | tf_op jit(solution)/shard_map/ppermute | solution.py:60
  107.2 48.0 %collective-permute-start.24 = (f32[512,512]{1,0:T(8,128)S(1)}, f32[512,512]{1,0:T(8,128)S(1)}, u32[]{:S(2)}, u32[]{:S(2)}) collective-permute-start(f32[512,512]{1,0:T(8,128)S(1)} %shard_map.72), channel_id=1, source_target_pairs={{0,16},{16,0},{1,17},{17,1},{2,18},{18,2},{3,19},{19,3},{4,20},{20... | collective-permute-start | bytes 3145736 | tf_op jit(solution)/shard_map/ppermute | solution.py:60
  107.4 15.6 %collective-permute-start.16 = (f32[256,512]{1,0:T(8,128)S(1)}, f32[256,512]{1,0:T(8,128)S(1)}, u32[]{:S(2)}, u32[]{:S(2)}) collective-permute-start(f32[256,512]{1,0:T(8,128)S(1)} %slice.44), channel_id=1, source_target_pairs={{0,32},{32,64},{64,96},{96,0},{1,33},{33,65},{65,97},{97,1},{2,34}... | collective-permute-start | bytes 1572872 | tf_op jit(solution)/shard_map/ppermute | solution.py:60
  108.7 25.5 %collective-permute-start.17 = (f32[256,512]{1,0:T(8,128)S(1)}, f32[256,512]{1,0:T(8,128)S(1)}, u32[]{:S(2)}, u32[]{:S(2)}) collective-permute-start(f32[256,512]{1,0:T(8,128)S(1)} %slice.45), channel_id=1, source_target_pairs={{0,96},{32,0},{64,32},{96,64},{1,97},{33,1},{65,33},{97,65},{2,98}... | collective-permute-start | bytes 1572872 | tf_op jit(solution)/shard_map/ppermute | solution.py:60
  138.5 14.1 %copy-start.8 = (f32[512,512]{1,0:T(8,128)}, f32[512,512]{1,0:T(8,128)S(1)}, u32[]{:S(2)}) copy-start(f32[512,512]{1,0:T(8,128)S(1)} %shard_map.76.theirs) | copy-start | bytes 3145732
  158.0 45.0 %all-to-all-start = ((f32[8,320,128]{2,1,0:T(8,128)}), f32[8,320,128]{2,1,0:T(8,128)}, u32[]{:S(2)}, u32[]{:S(2)}) async-start(f32[8,320,128]{2,1,0:T(8,128)} %bitcast.15), calls=%async_computation | async-start | bytes 2621440 | tf_op jit(solution)/shard_map/all_to_all | solution.py:307
  163.8 45.9 %copy-start.2 = (f32[512,512]{1,0:T(8,128)S(1)}, f32[512,512]{1,0:T(8,128)}, u32[]{:S(2)}) copy-start(f32[512,512]{1,0:T(8,128)} %copy-done.1) | copy-start | bytes 3145732
  163.8 38.1 %collective-permute-start.23 = (f32[512,512]{1,0:T(8,128)}, f32[512,512]{1,0:T(8,128)S(1)}, u32[]{:S(2)}, u32[]{:S(2)}) collective-permute-start(f32[512,512]{1,0:T(8,128)} %copy-done.8), channel_id=1, source_target_pairs={{0,16},{16,0},{1,17},{17,1},{2,18},{18,2},{3,19},{19,3},{4,20},{20... | collective-permute-start | bytes 3145736 | tf_op jit(solution)/shard_map/ppermute | solution.py:60
  205.4 21.2 %all-to-all-start.1 = ((f32[8,320,128]{2,1,0:T(8,128)}), f32[8,320,128]{2,1,0:T(8,128)}, u32[]{:S(2)}, u32[]{:S(2)}) async-start(f32[8,320,128]{2,1,0:T(8,128)} %copy-done.7), calls=%async_computation.1 | async-start | bytes 2621440 | tf_op jit(solution)/shard_map/all_to_all | solution.py:307
  (15 other events, 44.1 us)

commit v2 on v1

v2 whole, which is shorter than its diff:
```python
import functools

import jax
import jax.numpy as jnp
from jax import lax
from jax.experimental import pallas as pl
from jax.experimental.pallas import tpu as pltpu
from jax.sharding import Mesh, PartitionSpec as P

B = 128
SW = 512
WIDE = 2048
LIMIT = 22 * 2**20
ROW = ("y", "zl")
Z = ("zl", "zh")
DIRECTIONS = (0, 3, 1, 2)

VMEM = pl.BlockSpec(memory_space=pltpu.VMEM)
SMEM = pl.BlockSpec(memory_space=pltpu.SMEM)
F32 = jnp.float32
BF16 = jnp.bfloat16


def call(kernel, out_shape, specs, out_specs=None, scratch=(), aliases=None):
    single = not isinstance(out_shape, (tuple, list))
    return pl.pallas_call(
        kernel,
        out_shape=out_shape,
        in_specs=specs,
        out_specs=out_specs if out_specs is not None else (VMEM if single else [VMEM] * len(out_shape)),
        scratch_shapes=list(scratch),
        input_output_aliases=aliases or {},
        compiler_params=pltpu.CompilerParams(vmem_limit_bytes=LIMIT),
        cost_estimate=pl.CostEstimate(flops=1024, bytes_accessed=1024, transcendentals=0),
    )


def struct(shape, dtype=F32):
    return jax.ShapeDtypeStruct(shape, dtype)


def z_rounds():
    even = [
        {0: 0, 2: 1, 4: 4, 6: 5},
        {6: 0, 0: 1, 2: 4, 4: 5},
        {2: 0, 4: 1, 6: 4, 0: 5},
        {4: 0, 6: 1, 0: 4, 2: 5},
    ]
    rounds = []
    table = {}
    for k, pairs in enumerate(even):
        pairs = {**pairs, **{(3 - t) % 8: (3 - s) % 8 for t, s in pairs.items()}}
        rounds.append([((s % 2) * 4 + s // 2, (t % 2) * 4 + t // 2) for t, s in pairs.items()])
        for t, s in pairs.items():
            table[t, int(s % 2 == t % 2), (s // 2) // 2] = k
    return rounds, table


def step(value, axis, k, n=4):
    return lax.ppermute(value, axis, [(i, (i + k) % n) for i in range(n)])


def split(value):
    high = value.astype(BF16)
    return high, (value - high.astype(F32)).astype(BF16)


def dot3(a, b):
    dims = (((1,), (1,)), ((), ()))
    mul = functools.partial(lax.dot_general, dimension_numbers=dims, preferred_element_type=F32)
    return mul(a[0], b[0]) + (mul(a[0], b[1]) + mul(a[1], b[0]))


def meta_kernel(ids, widths, pattern, out):
    core, y, zl, zh, x = (ids[i] for i in range(5))
    first = ((core * 4 + zh) * 4 + x) * 2
    for child in range(2):
        for d, shift in enumerate(DIRECTIONS):
            block = ((y + shift) % 4 * 2 + zl) * 4
            for k in range(4):
                value = pattern[first + child, block + k].astype(F32)
                out[child : child + 1, (d * 4 + k) * B : (d * 4 + k + 1) * B] = jnp.full((1, B), value)
        out[2 + child : 3 + child, :] = jnp.full((1, WIDE), (widths[first + child] * B).astype(F32))
    out[4:8, :] = jnp.zeros((4, WIDE), F32)


def column_mask(meta, child):
    position = lax.broadcasted_iota(jnp.int32, (SW, B), 0).astype(F32)
    return (position < meta[2 + child : 3 + child, :B]).astype(F32)


def prepare_kernel(table, ids, *refs):
    core, y, zl, zh, x = (ids[i] for i in range(5))
    mine, theirs, outs = refs[:5], refs[5:10], refs[10:]
    z = zh * 2 + zl
    for role in range(2):
        high, low = outs[2 * role : 2 * role + 2]
        places = [jnp.int32(0)] * 2
        for k in range(2):
            for at in range(8):
                places[k] = jnp.where(z == at, table[at, role, k], places[k])

        @pl.loop(0, 16)
        def _(i):
            d, k = i // 4, i % 4
            block = (y + jnp.where(d == 0, 0, jnp.where(d == 1, 3, jnp.where(d == 2, 1, 2)))) % 4
            place = jnp.where(block % 2 == 0, places[0], places[1])
            away = (k - x + 4) % 4
            lanes = pl.ds(pl.multiple_of(i * B, B), B)
            for here, pieces in ((block // 2 == core, mine), (block // 2 != core, theirs)):
                held, left, right, top, bottom = pieces
                for when, ref, at in (
                    (away == 0, held, place),
                    (away == 3, left, place),
                    (away == 1, right, place),
                    ((away == 2) & (place < 2), top, place % 2),
                    ((away == 2) & (place >= 2), bottom, place % 2),
                ):

                    @pl.when(here & when)
                    def _():
                        high[:, lanes], low[:, lanes] = split(ref[at])


def product_kernel(child, own, left, right, far, high, low, meta, out, phigh, plow):
    mask = column_mask(meta, child)
    rows = slice(child * SW, (child + 1) * SW)
    for d, source in enumerate((own, left, right, far)):
        for k in range(4):
            lanes = slice((d * 4 + k) * B, (d * 4 + k + 1) * B)
            here = slice(k * B, (k + 1) * B)
            value = source[:, here] if d == 3 else source[rows, here]
            phigh[:, lanes], plow[:, lanes] = split(value * mask * meta[child : child + 1, lanes])
    for n in range(0, 512, 256):
        b = (high[n : n + 256, :], low[n : n + 256, :])
        for r in range(0, SW, 256):
            out[r : r + 256, n : n + 256] = dot3((phigh[r : r + 256, :], plow[r : r + 256, :]), b)


def lower_blocks(update, left, right):
    at = 0
    for a in range(4):
        value = dot3([v[a * B : (a + 1) * B] for v in left], [v[: (a + 1) * B] for v in right])
        for b in range(a + 1):
            update[at * B : (at + 1) * B, :] = value[:, b * B : (b + 1) * B]
            at += 1


def finish_kernel(child, mine, received, panel, meta, *refs):
    off, update = refs[-2:]
    wide = jnp.concatenate([column_mask(meta, child)] * 4, axis=1)
    masks = wide * meta[child : child + 1, :SW]
    product = (mine[...] + received[...]) * masks
    off[...] = -product
    lower_blocks(update, split(product), split(panel[...] * masks))


def sum_kernel(parts, out):
    total = parts[0]
    for k in range(1, 8):
        total += parts[k]
    for k in range(8):
        out[k] = total


def child_kernel(child, parts, diag, meta, *refs):
    out = refs[-1]
    across = lax.broadcasted_iota(jnp.int32, (1, SW), 1).astype(F32) < meta[2 + child : 3 + child, :SW]
    across = across.astype(F32)
    mask = column_mask(meta, child)
    at = 0
    for a in range(4):
        for b in range(a + 1):
            block = parts[at]
            at += 1
            for (i, j), value in {(b, a): block.T, (a, b): block}.items():
                lines, lanes = slice(i * B, (i + 1) * B), slice(j * B, (j + 1) * B)
                out[lines, lanes] = (diag[lines, lanes] + value) * mask[lines] * across[:, lanes]


def after(value, *before):
    return lax.optimization_barrier((value, *before))[0]


def local(anc_inverse, panel, diag_inverse, widths, pattern):
    names = ("core", "y", "zl", "zh", "x")
    ids = jnp.stack([lax.axis_index(n) for n in names]).astype(jnp.int32)
    left, right = step(panel, "y", 1), step(panel, "y", -1)
    far = [step(left[:SW], "y", 1), step(right[SW:], "y", -1)]

    rounds, table = z_rounds()
    held = jnp.stack([lax.ppermute(anc_inverse, Z, pairs) for pairs in rounds])
    before, beyond = step(held, "x", 1), step(held, "x", -1)
    top, bottom = step(before[:2], "x", 1), step(beyond[2:], "x", -1)
    top = after(top, *far)
    pieces = [held, before, beyond, top, bottom]
    theirs = [step(value, "core", 1, 2) for value in pieces]
    anc = call(
        functools.partial(prepare_kernel, table), [struct((SW, WIDE), BF16)] * 4, [SMEM] + [VMEM] * 10
    )(ids, *pieces, *theirs)
    meta = call(meta_kernel, struct((8, WIDE)), [SMEM] * 3)(ids, widths, pattern)

    def product(child, role, panel):
        return call(
            functools.partial(product_kernel, child),
            struct((SW, SW)),
            [VMEM] * 7,
            scratch=[pltpu.VMEM((SW, WIDE), BF16)] * 2,
        )(panel, left, right, far[child], *anc[2 * role : 2 * role + 2], meta)

    sent = [product(0, 0, panel)]
    sent.append(product(1, 0, after(panel, sent[0])))
    received = [step(value, "zl", 1, 2) for value in sent]
    mine = [product(child, 1, after(panel, sent[1])) for child in range(2)]

    def swap(value):
        return lax.all_to_all(value, ROW, 0, 0, tiled=True)

    shape = (8, 10 * B // 8, B)
    off = out = None
    for child in range(2):
        block = pl.BlockSpec((SW, SW), lambda g, child=child: (child, 0))
        anywhere = [] if child == 0 else [pl.BlockSpec(memory_space=pl.ANY)]
        params = dict(
            grid=(1,),
            compiler_params=pltpu.CompilerParams(vmem_limit_bytes=LIMIT),
            cost_estimate=pl.CostEstimate(flops=1024, bytes_accessed=1024, transcendentals=0),
        )
        off, update = pl.pallas_call(
            functools.partial(finish_kernel, child),
            out_shape=(struct(panel.shape), struct((10 * B, B))),
            in_specs=[VMEM, VMEM, block, VMEM] + anywhere,
            out_specs=[block, VMEM],
            input_output_aliases={4: 0} if child else {},
            **params,
        )(mine[child], received[child], panel, meta, *([off] if child else []))
        summed = call(sum_kernel, struct(shape), [VMEM])(swap(update.reshape(shape)))
        summed = swap(summed).reshape(10, B, B)
        out = pl.pallas_call(
            functools.partial(child_kernel, child),
            out_shape=struct(diag_inverse.shape),
            in_specs=[VMEM, block, VMEM] + anywhere,
            out_specs=block,
            input_output_aliases={3: 0} if child else {},
            **params,
        )(summed, diag_inverse, meta, *([out] if child else []))
    return off, out


def solution(mesh):
    fine = Mesh(mesh.devices.reshape(2, 4, 2, 4, 4), ("core", "y", "zl", "zh", "x"))
    group = ("core", "zh", "x")
    in_specs = (P(ROW, group), P(group, ROW), P(group, None), P(), P())
    out_specs = (P(group, ROW), P(group, None))
    return jax.shard_map(local, mesh=fine, in_specs=in_specs, out_specs=out_specs, check_vma=False)
```

time: 235 us -> 220 us (0.936)
  starting transfers between devices: 64.2 us -> 40.3 us
  waiting for transfers between devices: 111 us -> 125 us
  Pallas kernels: 42.5 us -> 33.9 us
  local copies, waits for them, and re-layouts: 10.8 us -> 15.1 us
    ppermute x21 -> x15, starting transfers between devices: 42.3 us -> 13 us  [step(): return lax.ppermute(value, axis, [(i, (i + k) % n) for i in range(n)])]
    ppermute x4, waiting for transfers between devices: 9.37 us -> 20.7 us  [local(): held = jnp.stack([lax.ppermute(anc_inverse, Z, pairs) for pairs in rounds])]
    all_to_all x2 -> x4, waiting for transfers between devices: 14.5 us -> 24.4 us  [swap(): return lax.all_to_all(value, ROW, 0, 0, tiled=True)]
    ppermute x21 -> x15, waiting for transfers between devices: 87.6 us -> 79.8 us  [step(): return lax.ppermute(value, axis, [(i, (i + k) % n) for i in range(n)])]
    pallas_call x10 -> x7, Pallas kernels: 21.5 us -> 15.8 us  [the longest x1 8.42 us: local(): call(functools.partial(prepare_kernel, table), [struct((SW, WIDE), BF16)]...]
    all_to_all x2 -> x4, starting transfers between devices: 10.2 us -> 15.6 us  [swap(): return lax.all_to_all(value, ROW, 0, 0, tiled=True)]
    unnamed x41, local copies, waits for them, and re-layouts: 7.78 us -> 12.7 us
    pallas_call x4, Pallas kernels: 19.8 us -> 16.9 us  [product(): call(functools.partial(product_kernel, child), struct((SW, SW)), [VMEM] *...]
  transfers between devices with their start and end apart: 27 -> 23, of which waited for: 17 -> 13; matrix products, arithmetic and copies ran while one was open for 1% -> 2% of each run, Pallas kernels for 15% -> 9%
where the time goes in v2:
time: 220 us; the launch traced here: 216 us
  waiting for transfers between devices  125 us (57%)
  starting transfers between devices  40.3 us (18%)
  Pallas kernels  33.9 us (15%)
  local copies, waits for them, and re-layouts  15.1 us (7%)
    ppermute x15, waiting for transfers between devices, step(): return lax.ppermute(value, axis, [(i, (i + k) % n) for i in range(n)])  79.8 us
    all_to_all x4, waiting for transfers between devices, swap(): return lax.all_to_all(value, ROW, 0, 0, tiled=True)  24.4 us
    ppermute x4, waiting for transfers between devices, local(): held = jnp.stack([lax.ppermute(anc_inverse, Z, pairs) for pairs in rounds])  20.7 us
    pallas_call x4, Pallas kernels, product(): call(functools.partial(product_kernel, child), struct((SW, SW)), [VMEM] *...  16.9 us
    all_to_all x4, starting transfers between devices, swap(): return lax.all_to_all(value, ROW, 0, 0, tiled=True)  15.6 us
    ppermute x15, starting transfers between devices, step(): return lax.ppermute(value, axis, [(i, (i + k) % n) for i in range(n)])  13 us
    unnamed x41, local copies, waits for them, and re-layouts  12.7 us
    ppermute x4, starting transfers between devices, local(): held = jnp.stack([lax.ppermute(anc_inverse, Z, pairs) for pairs in rounds])  11.7 us
  transfers between devices with their start and end apart: 23, of which 13 were waited for; matrix products, arithmetic and copies ran while one was open for 2% of the time, Pallas kernels for 9%

profile of v2, /device:TPU:6, one launch (start us, length us, event | category | flops | bytes accessed | tf_op | source)
XLA Modules:
  0.0 216.2 jit_solution(16054060175623917719)
XLA Ops:
  0.6 3.1 %collective-permute-start.1 = (f32[1024,512]{1,0:T(8,128)}, f32[1024,512]{1,0:T(8,128)S(1)}, u32[]{:S(2)}, u32[]{:S(2)}) collective-permute-start(f32[1024,512]{1,0:T(8,128)} %panel.3), channel_id=1, source_target_pairs={{0,96},{32,0},{64,32},{96,64},{1,97},{33,1},{65,33},{97,65},{2,98}... | collective-permute-start | bytes 6291464 | tf_op jit(solution)/shard_map/ppermute | solution.py:60
  3.7 1.6 collective-permute-start.3
  5.3 7.7 %collective-permute-start.4 = (f32[512,128]{1,0:T(8,128)}, f32[512,128]{1,0:T(8,128)S(1)}, u32[]{:S(2)}, u32[]{:S(2)}) collective-permute-start(f32[512,128]{1,0:T(8,128)} %param.5), channel_id=1, source_target_pairs={{0,12},{16,0},{8,4},{24,8},{20,24},{4,20},{28,16},{12,28},{1,13},{... | collective-permute-start | bytes 786440 | tf_op jit(solution)/shard_map/ppermute | solution.py:192
  13.0 2.4 %collective-permute-start.6 = (f32[512,128]{1,0:T(8,128)}, f32[512,128]{1,0:T(8,128)S(1)}, u32[]{:S(2)}, u32[]{:S(2)}) collective-permute-start(f32[512,128]{1,0:T(8,128)} %param.5), channel_id=1, source_target_pairs={{0,8},{16,12},{8,0},{24,4},{20,28},{4,24},{28,20},{12,16},{1,9},{1... | collective-permute-start | bytes 786440 | tf_op jit(solution)/shard_map/ppermute | solution.py:192
  15.5 6.6 %collective-permute-done.4 = f32[512,128]{1,0:T(8,128)S(1)} collective-permute-done((f32[512,128]{1,0:T(8,128)}, f32[512,128]{1,0:T(8,128)S(1)}, u32[]{:S(2)}, u32[]{:S(2)}) %collective-permute-start.4) | collective-permute-done | bytes 262176 | tf_op jit(solution)/shard_map/ppermute | solution.py:192
  22.1 14.1 %collective-permute-done.5 = f32[512,128]{1,0:T(8,128)S(1)} collective-permute-done((f32[512,128]{1,0:T(8,128)}, f32[512,128]{1,0:T(8,128)S(1)}, u32[]{:S(2)}, u32[]{:S(2)}) %collective-permute-start.5) | collective-permute-done | bytes 262176 | tf_op jit(solution)/shard_map/ppermute | solution.py:192
  39.2 22.0 %collective-permute-done.7.refs_1_ = f32[4,512,128]{2,1,0:T(8,128)} collective-permute-done((f32[4,512,128]{2,1,0:T(8,128)}, f32[4,512,128]{2,1,0:T(8,128)}, u32[]{:S(2)}, u32[]{:S(2)}) %collective-permute-start.7) | collective-permute-done | bytes 1048608 | tf_op jit(solution)/shard_map/ppermute | solution.py:60
  62.3 1.8 collective-permute-start.9
  66.6 2.7 %collective-permute-start.10 = (f32[512,512]{1,0:T(8,128)S(1)}, f32[512,512]{1,0:T(8,128)S(1)}, u32[]{:S(2)}, u32[]{:S(2)}) collective-permute-start(f32[512,512]{1,0:T(8,128)S(1)} %slice.18), channel_id=1, source_target_pairs={{0,96},{32,0},{64,32},{96,64},{1,97},{33,1},{65,33},{97,65},{2,98}... | collective-permute-start | bytes 3145736 | tf_op jit(solution)/shard_map/ppermute | solution.py:60
  71.0 3.0 %collective-permute-done.9.refs_3_ = f32[2,512,128]{2,1,0:T(8,128)} collective-permute-done((f32[2,512,128]{2,1,0:T(8,128)S(1)}, f32[2,512,128]{2,1,0:T(8,128)}, u32[]{:S(2)}, u32[]{:S(2)}) %collective-permute-start.9) | collective-permute-done | bytes 524320 | tf_op jit(solution)/shard_map/ppermute | solution.py:60
  74.1 8.6 %collective-permute-done.11.refs_4_ = f32[2,512,128]{2,1,0:T(8,128)} collective-permute-done((f32[2,512,128]{2,1,0:T(8,128)S(1)}, f32[2,512,128]{2,1,0:T(8,128)}, u32[]{:S(2)}, u32[]{:S(2)}) %collective-permute-start.11) | collective-permute-done | bytes 524320 | tf_op jit(solution)/shard_map/ppermute | solution.py:60
  82.7 6.4 %collective-permute-done.10.far = f32[512,512]{1,0:T(8,128)S(1)} collective-permute-done((f32[512,512]{1,0:T(8,128)S(1)}, f32[512,512]{1,0:T(8,128)S(1)}, u32[]{:S(2)}, u32[]{:S(2)}) %collective-permute-start.10) | collective-permute-done | bytes 1048608 | tf_op jit(solution)/shard_map/ppermute | solution.py:60
  89.1 4.7 %collective-permute-done.2.far = f32[512,512]{1,0:T(8,128)S(1)} collective-permute-done((f32[512,512]{1,0:T(8,128)S(1)}, f32[512,512]{1,0:T(8,128)S(1)}, u32[]{:S(2)}, u32[]{:S(2)}) %collective-permute-start.2) | collective-permute-done | bytes 1048608 | tf_op jit(solution)/shard_map/ppermute | solution.py:60
  97.0 8.4 %shard_map.68 = (bf16[512,2048]{1,0:T(8,128)(2,1)S(1)}, bf16[512,2048]{1,0:T(8,128)(2,1)S(1)}, bf16[512,2048]{1,0:T(8,128)(2,1)S(1)}, bf16[512,2048]{1,0:T(8,128)(2,1)S(1)}) custom-call(s32[5]{0:T(128)S(1)} %stack.38.ids, f32[4,512,128]{2,1,0:T(8,128)} %pad_maximum_fusion.refs_0_, f32[4,512,128]{2,1,0:T(8,128)} %collective-permute-done.7.refs_1_, ...), custom_call_target="tpu_custom_call" | custom-call | flops 1024 | bytes 1024 | tf_op jit(solution)/shard_map/pallas_call | solution.py:198
  105.5 4.3 %shard_map.70 = f32[512,512]{1,0:T(8,128)S(1)} custom-call(f32[1024,512]{1,0:T(8,128)S(1)} %copy-done, f32[1024,512]{1,0:T(8,128)S(1)} %copy-done.5, f32[1024,512]{1,0:T(8,128)S(1)} %copy-done.2, f32[512,512]{1,0:T(8,128)S(1)} %copy-done.13, bf16[512,2048]{1,0:T(8,128)(2,1)S(1)} %get-tuple-element.14.high, bf16[512,2048]{1,0:T(8,128)(2,1)S(1)} %get-tuple-element.15.low, ...), custom_call_target="tpu_custom_call" | custom-call | flops 1024 | bytes 1024 | tf_op jit(solution)/shard_map/pallas_call | solution.py:204
  111.0 4.3 %shard_map.71 = f32[512,512]{1,0:T(8,128)S(1)} custom-call(f32[1024,512]{1,0:T(8,128)S(1)} %copy-done, f32[1024,512]{1,0:T(8,128)S(1)} %copy-done.5, f32[1024,512]{1,0:T(8,128)S(1)} %copy-done.2, f32[512,512]{1,0:T(8,128)S(1)} %collective-permute-done.10.far, bf16[512,2048]{1,0:T(8,128)(2,1)S(1)} %get-tuple-element.14.high, ...), custom_call_target="tpu_custom_call" | custom-call | flops 1024 | bytes 1024 | tf_op jit(solution)/shard_map/pallas_call | solution.py:204
  115.3 4.2 %shard_map.73.mine = f32[512,512]{1,0:T(8,128)S(1)} custom-call(f32[1024,512]{1,0:T(8,128)S(1)} %copy-done, f32[1024,512]{1,0:T(8,128)S(1)} %copy-done.5, f32[1024,512]{1,0:T(8,128)S(1)} %copy-done.2, f32[512,512]{1,0:T(8,128)S(1)} %copy-done.13, bf16[512,2048]{1,0:T(8,128)(2,1)S(1)} %get-tuple-element.18.high, bf16[512,2048]{1,0:T(8,128)(2,1)S(1)} %get-tuple-element.19.low, ...), custom_call_target="tpu_custom_call" | custom-call | flops 1024 | bytes 1024 | tf_op jit(solution)/shard_map/pallas_call | solution.py:204
  119.5 15.4 %collective-permute-done.18.received = f32[512,512]{1,0:T(8,128)S(1)} collective-permute-done((f32[512,512]{1,0:T(8,128)S(1)}, f32[512,512]{1,0:T(8,128)S(1)}, u32[]{:S(2)}, u32[]{:S(2)}) %collective-permute-start.18) | collective-permute-done | bytes 1048608 | tf_op jit(solution)/shard_map/ppermute | solution.py:60
  134.9 1.6 shard_map.74
  137.4 4.2 %all-to-all-start.2 = ((f32[8,160,128]{2,1,0:T(8,128)}), f32[8,160,128]{2,1,0:T(8,128)}, u32[]{:S(2)}, u32[]{:S(2)}) async-start(f32[8,160,128]{2,1,0:T(8,128)} %bitcast.15), calls=%async_computation.2 | async-start | bytes 1310720 | tf_op jit(solution)/shard_map/all_to_all | solution.py:217
  141.6 1.9 collective-permute-start.17
  146.7 1.6 copy-done.9
  148.3 1.6 copy-done.11
  149.9 4.2 %shard_map.72.mine = f32[512,512]{1,0:T(8,128)S(1)} custom-call(f32[1024,512]{1,0:T(8,128)S(1)} %copy-done, f32[1024,512]{1,0:T(8,128)S(1)} %copy-done.6, f32[1024,512]{1,0:T(8,128)S(1)} %copy-done.3, f32[512,512]{1,0:T(8,128)S(1)} %collective-permute-done.10.far, bf16[512,2048]{1,0:T(8,128)(2,1)S(1)} %copy-done.9, bf16[512,2048]{1,0:T(8,128)(2,1)S(1)} %copy-done.11, ...), custom_call_target="tpu_custom_call" | custom-call | flops 1024 | bytes 1024 | tf_op jit(solution)/shard_map/pallas_call | solution.py:204
  154.1 18.8 %collective-permute-done.17.received = f32[512,512]{1,0:T(8,128)S(1)} collective-permute-done((f32[512,512]{1,0:T(8,128)}, f32[512,512]{1,0:T(8,128)S(1)}, u32[]{:S(2)}, u32[]{:S(2)}) %collective-permute-start.17) | collective-permute-done | bytes 1048608 | tf_op jit(solution)/shard_map/ppermute | solution.py:60
  172.9 2.2 %shard_map.75 = (f32[1024,512]{1,0:T(8,128)}, f32[1280,128]{1,0:T(8,128)}) custom-call(f32[512,512]{1,0:T(8,128)S(1)} %shard_map.72.mine, f32[512,512]{1,0:T(8,128)S(1)} %collective-permute-done.17.received, f32[1024,512]{1,0:T(8,128)S(1)} %copy-done, f32[8,2048]{1,0:T(8,128)S(1)} %shard_map.69.meta, ...), custom_call_target="tpu_custom_call", output_to_operand_aliasing={{0}: (4, {})} | custom-call | flops 1024 | bytes 1024 | tf_op jit(solution)/shard_map/pallas_call | solution.py:229
  175.2 4.3 %all-to-all-start = ((f32[8,160,128]{2,1,0:T(8,128)}), f32[8,160,128]{2,1,0:T(8,128)S(1)}, u32[]{:S(2)}, u32[]{:S(2)}) async-start(f32[8,160,128]{2,1,0:T(8,128)} %bitcast.9), calls=%async_computation | async-start | bytes 1310720 | tf_op jit(solution)/shard_map/all_to_all | solution.py:217
  181.5 7.9 %all-to-all-done.parts = f32[8,160,128]{2,1,0:T(8,128)S(1)} async-done(((f32[8,160,128]{2,1,0:T(8,128)}), f32[8,160,128]{2,1,0:T(8,128)S(1)}, u32[]{:S(2)}, u32[]{:S(2)}) %all-to-all-start) | async-done | bytes 655392 | tf_op jit(solution)/shard_map/all_to_all | solution.py:217
  189.3 3.5 %all-to-all-start.3 = ((f32[8,160,128]{2,1,0:T(8,128)}), f32[8,160,128]{2,1,0:T(8,128)S(1)}, u32[]{:S(2)}, u32[]{:S(2)}) async-start(f32[8,160,128]{2,1,0:T(8,128)} %copy-done.14), calls=%async_computation.3 | async-start | bytes 1310720 | tf_op jit(solution)/shard_map/all_to_all | solution.py:217
  193.8 8.4 %all-to-all-done.3 = f32[8,160,128]{2,1,0:T(8,128)S(1)} async-done(((f32[8,160,128]{2,1,0:T(8,128)}), f32[8,160,128]{2,1,0:T(8,128)S(1)}, u32[]{:S(2)}, u32[]{:S(2)}) %all-to-all-start.3) | async-done | bytes 655392 | tf_op jit(solution)/shard_map/all_to_all | solution.py:217
  202.2 3.5 %all-to-all-start.1 = ((f32[8,160,128]{2,1,0:T(8,128)}), f32[8,160,128]{2,1,0:T(8,128)S(1)}, u32[]{:S(2)}, u32[]{:S(2)}) async-start(f32[8,160,128]{2,1,0:T(8,128)} %copy-done.15), calls=%async_computation.1 | async-start | bytes 1310720 | tf_op jit(solution)/shard_map/all_to_all | solution.py:217
  206.9 8.2 %all-to-all-done.1 = f32[8,160,128]{2,1,0:T(8,128)S(1)} async-done(((f32[8,160,128]{2,1,0:T(8,128)}), f32[8,160,128]{2,1,0:T(8,128)S(1)}, u32[]{:S(2)}, u32[]{:S(2)}) %all-to-all-start.1) | async-done | bytes 655392 | tf_op jit(solution)/shard_map/all_to_all | solution.py:217
  (73 shorter events, 22.0 us)
Async XLA Ops:
  0.6 64.6 %collective-permute-start.1 = (f32[1024,512]{1,0:T(8,128)}, f32[1024,512]{1,0:T(8,128)S(1)}, u32[]{:S(2)}, u32[]{:S(2)}) collective-permute-start(f32[1024,512]{1,0:T(8,128)} %panel.3), channel_id=1, source_target_pairs={{0,96},{32,0},{64,32},{96,64},{1,97},{33,1},{65,33},{97,65},{2,98}... | collective-permute-start | bytes 6291464 | tf_op jit(solution)/shard_map/ppermute | solution.py:60
  3.7 65.6 %collective-permute-start = (f32[1024,512]{1,0:T(8,128)}, f32[1024,512]{1,0:T(8,128)S(1)}, u32[]{:S(2)}, u32[]{:S(2)}) collective-permute-start(f32[1024,512]{1,0:T(8,128)} %panel.3), channel_id=1, source_target_pairs={{0,32},{32,64},{64,96},{96,0},{1,33},{33,65},{65,97},{97,1},{2,34}... | collective-permute-start | bytes 6291464 | tf_op jit(solution)/shard_map/ppermute | solution.py:60
  3.7 9.3 %collective-permute-start.3 = (f32[512,128]{1,0:T(8,128)}, f32[512,128]{1,0:T(8,128)S(1)}, u32[]{:S(2)}, u32[]{:S(2)}) collective-permute-start(f32[512,128]{1,0:T(8,128)} %param.5), channel_id=1, source_target_pairs={{0,0},{16,4},{8,8},{24,12},{20,20},{4,16},{28,28},{12,24},{1,1},{1... | collective-permute-start | bytes 786440 | tf_op jit(solution)/shard_map/ppermute | solution.py:192
  5.3 16.7 %collective-permute-start.4 = (f32[512,128]{1,0:T(8,128)}, f32[512,128]{1,0:T(8,128)S(1)}, u32[]{:S(2)}, u32[]{:S(2)}) collective-permute-start(f32[512,128]{1,0:T(8,128)} %param.5), channel_id=1, source_target_pairs={{0,12},{16,0},{8,4},{24,8},{20,24},{4,20},{28,16},{12,28},{1,13},{... | collective-permute-start | bytes 786440 | tf_op jit(solution)/shard_map/ppermute | solution.py:192
  13.0 23.2 %collective-permute-start.5 = (f32[512,128]{1,0:T(8,128)}, f32[512,128]{1,0:T(8,128)S(1)}, u32[]{:S(2)}, u32[]{:S(2)}) collective-permute-start(f32[512,128]{1,0:T(8,128)} %param.5), channel_id=1, source_target_pairs={{0,4},{16,8},{8,12},{24,0},{20,16},{4,28},{28,24},{12,20},{1,5},{1... | collective-permute-start | bytes 786440 | tf_op jit(solution)/shard_map/ppermute | solution.py:192
  13.0 23.2 %collective-permute-start.6 = (f32[512,128]{1,0:T(8,128)}, f32[512,128]{1,0:T(8,128)S(1)}, u32[]{:S(2)}, u32[]{:S(2)}) collective-permute-start(f32[512,128]{1,0:T(8,128)} %param.5), channel_id=1, source_target_pairs={{0,8},{16,12},{8,0},{24,4},{20,28},{4,24},{28,20},{12,16},{1,9},{1... | collective-permute-start | bytes 786440 | tf_op jit(solution)/shard_map/ppermute | solution.py:192
  37.2 24.0 %collective-permute-start.7 = (f32[4,512,128]{2,1,0:T(8,128)}, f32[4,512,128]{2,1,0:T(8,128)}, u32[]{:S(2)}, u32[]{:S(2)}) collective-permute-start(f32[4,512,128]{2,1,0:T(8,128)} %pad_maximum_fusion.refs_0_), channel_id=1, source_target_pairs={{0,1},{1,2},{2,3},{3,0},{4,5},{5,6},{6,7},{7,4},{8,9},{9,10},{10,1... | collective-permute-start | bytes 3145736 | tf_op jit(solution)/shard_map/ppermute | solution.py:60
  37.7 26.4 %collective-permute-start.8 = (f32[4,512,128]{2,1,0:T(8,128)}, f32[4,512,128]{2,1,0:T(8,128)}, u32[]{:S(2)}, u32[]{:S(2)}) collective-permute-start(f32[4,512,128]{2,1,0:T(8,128)} %pad_maximum_fusion.refs_0_), channel_id=1, source_target_pairs={{0,3},{1,0},{2,1},{3,2},{4,7},{5,4},{6,5},{7,6},{8,11},{9,8},{10,9... | collective-permute-start | bytes 3145736 | tf_op jit(solution)/shard_map/ppermute | solution.py:60
  62.3 11.7 %collective-permute-start.9 = (f32[2,512,128]{2,1,0:T(8,128)S(1)}, f32[2,512,128]{2,1,0:T(8,128)}, u32[]{:S(2)}, u32[]{:S(2)}) collective-permute-start(f32[2,512,128]{2,1,0:T(8,128)S(1)} %slice.17), channel_id=1, source_target_pairs={{0,1},{1,2},{2,3},{3,0},{4,5},{5,6},{6,7},{7,4},{8,9},{9,10},{10,1... | collective-permute-start | bytes 1572872 | tf_op jit(solution)/shard_map/ppermute | solution.py:60
  65.2 29.6 %copy-start.19 = (s32[64,32]{0,1:T(8,128)S(1)}, s32[64,32]{0,1:T(8,128)}, u32[]{:S(2)}) copy-start(s32[64,32]{0,1:T(8,128)} %param.9) | copy-start | bytes 24580
  65.2 29.8 %copy-start.18 = (s32[64]{0:T(128)S(1)}, s32[64]{0:T(128)}, u32[]{:S(2)}) copy-start(s32[64]{0:T(128)} %widths.1) | copy-start | bytes 772
  66.6 22.5 %collective-permute-start.10 = (f32[512,512]{1,0:T(8,128)S(1)}, f32[512,512]{1,0:T(8,128)S(1)}, u32[]{:S(2)}, u32[]{:S(2)}) collective-permute-start(f32[512,512]{1,0:T(8,128)S(1)} %slice.18), channel_id=1, source_target_pairs={{0,96},{32,0},{64,32},{96,64},{1,97},{33,1},{65,33},{97,65},{2,98}... | collective-permute-start | bytes 3145736 | tf_op jit(solution)/shard_map/ppermute | solution.py:60
  70.7 23.1 %collective-permute-start.2 = (f32[512,512]{1,0:T(8,128)S(1)}, f32[512,512]{1,0:T(8,128)S(1)}, u32[]{:S(2)}, u32[]{:S(2)}) collective-permute-start(f32[512,512]{1,0:T(8,128)S(1)} %slice.16), channel_id=1, source_target_pairs={{0,32},{32,64},{64,96},{96,0},{1,33},{33,65},{65,97},{97,1},{2,34}... | collective-permute-start | bytes 3145736 | tf_op jit(solution)/shard_map/ppermute | solution.py:60
  70.7 12.0 %collective-permute-start.11 = (f32[2,512,128]{2,1,0:T(8,128)S(1)}, f32[2,512,128]{2,1,0:T(8,128)}, u32[]{:S(2)}, u32[]{:S(2)}) collective-permute-start(f32[2,512,128]{2,1,0:T(8,128)S(1)} %slice.19), channel_id=1, source_target_pairs={{0,3},{1,0},{2,1},{3,2},{4,7},{5,4},{6,5},{7,6},{8,11},{9,8},{10,9... | collective-permute-start | bytes 1572872 | tf_op jit(solution)/shard_map/ppermute | solution.py:60
  71.0 25.2 %collective-permute-start.12 = (f32[4,512,128]{2,1,0:T(8,128)}, f32[4,512,128]{2,1,0:T(8,128)}, u32[]{:S(2)}, u32[]{:S(2)}) collective-permute-start(f32[4,512,128]{2,1,0:T(8,128)} %pad_maximum_fusion.refs_0_), channel_id=1, source_target_pairs={{0,128},{128,0},{1,129},{129,1},{2,130},{130,2},{3,131},{131,3},{4... | collective-permute-start | bytes 3145736 | tf_op jit(solution)/shard_map/ppermute | solution.py:60
  74.0 22.2 %collective-permute-start.13 = (f32[4,512,128]{2,1,0:T(8,128)}, f32[4,512,128]{2,1,0:T(8,128)}, u32[]{:S(2)}, u32[]{:S(2)}) collective-permute-start(f32[4,512,128]{2,1,0:T(8,128)} %collective-permute-done.7.refs_1_), channel_id=1, source_target_pairs={{0,128},{128,0},{1,129},{129,1},{2,130},{130,2},{3,131},{131,3},{4... | collective-permute-start | bytes 3145736 | tf_op jit(solution)/shard_map/ppermute | solution.py:60
  82.7 13.5 %collective-permute-start.14 = (f32[4,512,128]{2,1,0:T(8,128)}, f32[4,512,128]{2,1,0:T(8,128)}, u32[]{:S(2)}, u32[]{:S(2)}) collective-permute-start(f32[4,512,128]{2,1,0:T(8,128)} %collective-permute-done.8.refs_2_), channel_id=1, source_target_pairs={{0,128},{128,0},{1,129},{129,1},{2,130},{130,2},{3,131},{131,3},{4... | collective-permute-start | bytes 3145736 | tf_op jit(solution)/shard_map/ppermute | solution.py:60
  89.1 7.1 %collective-permute-start.16 = (f32[2,512,128]{2,1,0:T(8,128)}, f32[2,512,128]{2,1,0:T(8,128)}, u32[]{:S(2)}, u32[]{:S(2)}) collective-permute-start(f32[2,512,128]{2,1,0:T(8,128)} %collective-permute-done.11.refs_4_), channel_id=1, source_target_pairs={{0,128},{128,0},{1,129},{129,1},{2,130},{130,2},{3,131},{131,3},{4... | collective-permute-start | bytes 1572872 | tf_op jit(solution)/shard_map/ppermute | solution.py:60
  94.8 2.3 %collective-permute-start.15 = (f32[2,512,128]{2,1,0:T(8,128)}, f32[2,512,128]{2,1,0:T(8,128)}, u32[]{:S(2)}, u32[]{:S(2)}) collective-permute-start(f32[2,512,128]{2,1,0:T(8,128)} %collective-permute-done.9.refs_3_), channel_id=1, source_target_pairs={{0,128},{128,0},{1,129},{129,1},{2,130},{130,2},{3,131},{131,3},{4... | collective-permute-start | bytes 1572872 | tf_op jit(solution)/shard_map/ppermute | solution.py:60
  96.1 9.3 %copy-start = (f32[1024,512]{1,0:T(8,128)S(1)}, f32[1024,512]{1,0:T(8,128)}, u32[]{:S(2)}) copy-start(f32[1024,512]{1,0:T(8,128)} %panel.3) | copy-start | bytes 6291460
  96.2 9.3 %copy-start.2 = (f32[1024,512]{1,0:T(8,128)S(1)}, f32[1024,512]{1,0:T(8,128)}, u32[]{:S(2)}) copy-start(f32[1024,512]{1,0:T(8,128)} %copy-done.1) | copy-start | bytes 6291460
  96.2 9.3 %copy-start.5 = (f32[1024,512]{1,0:T(8,128)S(1)}, f32[1024,512]{1,0:T(8,128)}, u32[]{:S(2)}) copy-start(f32[1024,512]{1,0:T(8,128)} %copy-done.4) | copy-start | bytes 6291460
  96.2 9.3 %copy-start.13 = (f32[512,512]{1,0:T(8,128)S(1)}, f32[512,512]{1,0:T(8,128)}, u32[]{:S(2)}) copy-start(f32[512,512]{1,0:T(8,128)} %copy-done.12) | copy-start | bytes 3145732
  105.5 9.8 %copy-start.8 = (bf16[512,2048]{1,0:T(8,128)(2,1)}, bf16[512,2048]{1,0:T(8,128)(2,1)S(1)}, u32[]{:S(2)}) copy-start(bf16[512,2048]{1,0:T(8,128)(2,1)S(1)} %get-tuple-element.18.high) | copy-start | bytes 6291460
  105.5 9.8 %copy-start.10 = (bf16[512,2048]{1,0:T(8,128)(2,1)}, bf16[512,2048]{1,0:T(8,128)(2,1)S(1)}, u32[]{:S(2)}) copy-start(bf16[512,2048]{1,0:T(8,128)(2,1)S(1)} %get-tuple-element.19.low) | copy-start | bytes 6291460
  109.8 25.1 %collective-permute-start.18 = (f32[512,512]{1,0:T(8,128)S(1)}, f32[512,512]{1,0:T(8,128)S(1)}, u32[]{:S(2)}, u32[]{:S(2)}) collective-permute-start(f32[512,512]{1,0:T(8,128)S(1)} %shard_map.70), channel_id=1, source_target_pairs={{0,16},{16,0},{1,17},{17,1},{2,18},{18,2},{3,19},{19,3},{4,20},{20... | collective-permute-start | bytes 3145736 | tf_op jit(solution)/shard_map/ppermute | solution.py:60
  137.4 37.7 %all-to-all-start.2 = ((f32[8,160,128]{2,1,0:T(8,128)}), f32[8,160,128]{2,1,0:T(8,128)}, u32[]{:S(2)}, u32[]{:S(2)}) async-start(f32[8,160,128]{2,1,0:T(8,128)} %bitcast.15), calls=%async_computation.2 | async-start | bytes 1310720 | tf_op jit(solution)/shard_map/all_to_all | solution.py:217
  141.6 31.3 %collective-permute-start.17 = (f32[512,512]{1,0:T(8,128)}, f32[512,512]{1,0:T(8,128)S(1)}, u32[]{:S(2)}, u32[]{:S(2)}) collective-permute-start(f32[512,512]{1,0:T(8,128)} %copy-done.16), channel_id=1, source_target_pairs={{0,16},{16,0},{1,17},{17,1},{2,18},{18,2},{3,19},{19,3},{4,20},{20... | collective-permute-start | bytes 3145736 | tf_op jit(solution)/shard_map/ppermute | solution.py:60
  175.2 14.2 %all-to-all-start = ((f32[8,160,128]{2,1,0:T(8,128)}), f32[8,160,128]{2,1,0:T(8,128)S(1)}, u32[]{:S(2)}, u32[]{:S(2)}) async-start(f32[8,160,128]{2,1,0:T(8,128)} %bitcast.9), calls=%async_computation | async-start | bytes 1310720 | tf_op jit(solution)/shard_map/all_to_all | solution.py:217
  181.5 24.3 %copy-start.7 = (f32[1024,512]{1,0:T(8,128)S(1)}, f32[1024,512]{1,0:T(8,128)}, u32[]{:S(2)}) copy-start(f32[1024,512]{1,0:T(8,128)} %diag.3) | copy-start | bytes 6291460
  189.3 12.9 %all-to-all-start.3 = ((f32[8,160,128]{2,1,0:T(8,128)}), f32[8,160,128]{2,1,0:T(8,128)S(1)}, u32[]{:S(2)}, u32[]{:S(2)}) async-start(f32[8,160,128]{2,1,0:T(8,128)} %copy-done.14), calls=%async_computation.3 | async-start | bytes 1310720 | tf_op jit(solution)/shard_map/all_to_all | solution.py:217
  202.2 12.9 %all-to-all-start.1 = ((f32[8,160,128]{2,1,0:T(8,128)}), f32[8,160,128]{2,1,0:T(8,128)S(1)}, u32[]{:S(2)}, u32[]{:S(2)}) async-start(f32[8,160,128]{2,1,0:T(8,128)} %copy-done.15), calls=%async_computation.1 | async-start | bytes 1310720 | tf_op jit(solution)/shard_map/all_to_all | solution.py:217
  (11 other events, 16.9 us)

commit v3 on v1

--- a/solution.py
+++ b/solution.py
@@ -10,7 +10,7 @@
 B = 128
 SW = 512
 WIDE = 2048
-LIMIT = 18 * 2**20
+LIMIT = 14 * 2**20
 ROW = ("y", "zl")
 Z = ("zl", "zh")
 DIRECTIONS = (0, 3, 1, 2)
@@ -108,48 +108,67 @@
                     out[k] = source[...]
 
 
-def join_kernel(piece, left, right, top, bottom, out):
-    out[0], out[1], out[2] = piece[...], left[...], right[...]
-    out[3, 0], out[3, 1] = top[...], bottom[...]
-
-
-def prepare_kernel(ids, mine, theirs, high, low):
-    core, y, x = ids[0], ids[1], ids[4]
-    for d, shift in enumerate(DIRECTIONS):
-        block = (y + shift) % 4
-        here = block // 2 == core
-        for k in range(4):
-            away = (k - x + 4) % 4
-            at = jnp.where(away == 0, 0, jnp.where(away == 3, 1, jnp.where(away == 1, 2, 3)))
-            columns = slice((d * 4 + k) * B, (d * 4 + k + 1) * B)
-
-            def put(source):
-                high[:, columns], low[:, columns] = split(source[at, block % 2])
-
-            pl.when(here)(lambda: put(mine))
-            pl.when(jnp.logical_not(here))(lambda: put(theirs))
-
-
-def product_kernel(child, own, left, right, top, bottom, high, low, meta, out, phigh, plow):
-    rows = own.shape[0]
-    half = rows // 2
+def each_piece(ids, body):
+    @pl.loop(0, 16)
+    def _(i):
+        d, k = i // 4, i % 4
+        block = (ids[1] + jnp.where(d == 0, 0, jnp.where(d == 1, 3, jnp.where(d == 2, 1, 2)))) % 4
+        body(block, k, pl.ds(pl.multiple_of(i * B, B), B))
+
+
+def sort_pieces_kernel(ids, *refs):
+    mine, theirs, (high, low) = refs[:5], refs[5:10], refs[10:]
+
+    def body(block, k, lanes):
+        away, half = (k - ids[4] + 4) % 4, block % 2
+        for here, pieces in ((block // 2 == ids[0], mine), (block // 2 != ids[0], theirs)):
+            held, left, right, top, bottom = pieces
+            for when, ref, at in (
+                (away == 0, held, half),
+                (away == 3, left, half),
+                (away == 1, right, half),
+                ((away == 2) & (half == 0), top, None),
+                ((away == 2) & (half == 1), bottom, None),
+            ):
+
+                @pl.when(here & when)
+                def _():
+                    high[:, lanes], low[:, lanes] = split(ref[...] if at is None else ref[at])
+
+    each_piece(ids, body)
+
+
+def sort_gathered_kernel(ids, whole, high, low):
+    def body(block, k, lanes):
+        high[:, lanes], low[:, lanes] = split(whole[block // 2 * 4 + k, block % 2])
+
+    each_piece(ids, body)
+
+
+def product_kernel(child, own, left, right, left_tail, right_tail, top, bottom, high, low, meta, *refs):
+    outs, (phigh, plow) = refs[:-2], refs[-2:]
     mask = column_mask(meta, child)
+    rows = slice(child * SW, (child + 1) * SW)
     for d, source in enumerate((own, left, right, None)):
         for k in range(4):
-            at = (d * 4 + k) * B
-            lanes = slice(at, at + B)
+            lanes = slice((d * 4 + k) * B, (d * 4 + k + 1) * B)
             here = slice(k * B, (k + 1) * B)
             if source is None:
-                parts = ((top, 0, half), (bottom, half, rows))
+                value = jnp.concatenate([top[:, here], bottom[:, here]], axis=0)
+            elif d and child:
+                end = (left_tail, right_tail)[d - 1]
+                value = jnp.concatenate([source[SW:, here], end[:, here]], axis=0)
             else:
-                parts = ((source, 0, rows),)
-            for ref, low_row, high_row in parts:
-                value = ref[:, here] * mask[low_row:high_row] * meta[child : child + 1, lanes]
-                phigh[low_row:high_row, lanes], plow[low_row:high_row, lanes] = split(value)
+                value = source[rows, here]
+            phigh[:, lanes], plow[:, lanes] = split(value * mask * meta[child : child + 1, lanes])
     for n in range(0, 512, 256):
         b = (high[n : n + 256, :], low[n : n + 256, :])
-        for r in range(0, rows, 256):
-            out[r : r + 256, n : n + 256] = dot3((phigh[r : r + 256, :], plow[r : r + 256, :]), b)
+        for r in range(0, SW, 256):
+            value = dot3((phigh[r : r + 256, :], plow[r : r + 256, :]), b)
+            if len(outs) == 1:
+                outs[0][r : r + 256, n : n + 256] = value
+            else:
+                outs[r // 256][:, n : n + 256] = value
 
 
 def lower_blocks(update, pairs):
@@ -164,30 +183,24 @@
             at += 1
 
 
-def masked(child, panel, meta, row):
+def finish_kernel(child, mine, *refs):
+    received, (panel, meta), refs = refs[: child + 1], refs[child + 1 : child + 3], refs[child + 3 :]
     wide = jnp.concatenate([column_mask(meta, child)] * 4, axis=1)
-    return panel[...] * wide * meta[row : row + 1, :SW]
-
-
-def finish_kernel(child, mine, received, panel, meta, *refs):
-    wide = jnp.concatenate([column_mask(meta, child)] * 4, axis=1)
-    product = (mine[...] + received[...]) * wide * meta[child : child + 1, :SW]
+    masks = wide * meta[child : child + 1, :SW]
+    product = (mine[...] + jnp.concatenate([ref[...] for ref in received], axis=0)) * masks
     if child == 0:
         off, update = refs
-        lower_blocks(update, [(split(product), split(masked(child, panel, meta, child)))])
+        lower_blocks(update, [(split(product), split(panel[...] * masks))])
     else:
         off = refs[-1]
     off[...] = -product
 
 
-def update_kernel(child, mine, theirs, panel, across, meta, update):
-    lower_blocks(
-        update,
-        [
-            (split(mine[...]), split(masked(child, panel, meta, child))),
-            (split(theirs[...]), split(masked(child, across, meta, 4 + child))),
-        ],
-    )
+def update_kernel(child, mine, sent_top, sent_bottom, panel, across, meta, update):
+    wide = jnp.concatenate([column_mask(meta, child)] * 4, axis=1)
+    own = panel[child * SW : (child + 1) * SW, :] * wide * meta[child : child + 1, :SW]
+    other = across[...] * wide * meta[4 + child : 5 + child, :SW]
+    lower_blocks(update, [(split(mine[...]), split(own)), (split(jnp.concatenate([sent_top[...], sent_bottom[...]], axis=0)), split(other))])
 
 
 def sum_kernel(parts, out):
@@ -216,62 +229,49 @@
 
 
 def after(value, *before):
-    if not before:
-        return value
     return lax.optimization_barrier((value, *before))[0]
 
 
 def local(anc_inverse, panel, diag_inverse, widths, pattern):
     names = ("core", "y", "zl", "zh", "x")
     ids = jnp.stack([lax.axis_index(n) for n in names]).astype(jnp.int32)
-    parts = [panel[:SW], panel[SW:]]
-
-    def send_direct(i):
-        return step(parts[i], "y", 1), step(parts[i], "y", -1)
-
-    def send_relay(left, right):
-        half = SW // 2
-        return step(left[:half], "y", 1), step(right[half:], "y", -1)
+    half, cut = SW // 2, SW + SW // 2
+    head = [step(panel[:cut], "y", k) for k in (1, -1)]
+    tail = [step(panel[cut:], "y", k) for k in (1, -1)]
+    far = [
+        (step(head[0][:half], "y", 1), step(head[1][half:SW], "y", -1)),
+        (step(head[0][SW:cut], "y", 1), step(tail[1], "y", -1)),
+    ]
+    across = step(panel[SW:], "zl", 1, 2)
 
     rounds, table = z_rounds()
-    direct = [send_direct(0)]
     got = [lax.ppermute(anc_inverse, Z, pairs) for pairs in rounds]
-    direct.append(send_direct(1))
-    across = step(parts[1], "zl", 1, 2)
-    relay = [send_relay(*direct[0]), send_relay(*direct[1])]
-
-    got[0] = after(got[0], *direct[0])
-    piece = struct((2, 512, B))
-    pieces = call(functools.partial(select_kernel, table), (piece, piece), [SMEM] + [VMEM] * 4)(ids, *got)
+    got[0] = after(got[0], *head)
+    piece = struct((2, SW, B))
+    held, kept = call(functools.partial(select_kernel, table), (piece, piece), [SMEM] + [VMEM] * 4)(ids, *got)
+    whole = lax.all_gather(kept, ("core", "x"), axis=0)
+    before, beyond = step(held, "x", 1), step(held, "x", -1)
+    top, bottom = step(after(before[0], *far[0]), "x", 1), step(after(beyond[1], *far[0]), "x", -1)
+    top, bottom = after(top, *tail, across), after(bottom, *tail)
+    pieces = [held, before, beyond, top, bottom]
+    pieces += [step(value, "core", 1, 2) for value in pieces]
+    pair = [struct((SW, WIDE), BF16)] * 2
+    other = call(sort_pieces_kernel, pair, [SMEM] + [VMEM] * 10)(ids, *pieces)
     meta = call(meta_kernel, struct((8, WIDE)), [SMEM] * 3)(ids, widths, pattern)
 
-    def gather(value, before, far, joined, swapped):
-        value = after(value, *before)
-        left, right = step(value, "x", 1), step(value, "x", -1)
-        top, bottom = step(after(left[0], *far), "x", 1), step(after(right[1], *far), "x", -1)
-        top = after(top, *joined)
-        mine = call(join_kernel, struct((4, 2, 512, B)), [VMEM] * 5)(value, left, right, top, bottom)
-        theirs = after(step(mine, "core", 1, 2), *swapped)
-        pair = struct((512, WIDE), BF16)
-        return call(prepare_kernel, (pair, pair), [SMEM, VMEM, VMEM])(ids, mine, theirs), (left, right)
-
-    other, before = gather(pieces[0], (), relay[0], (across,), ())
-    own, _ = gather(pieces[1], before, (), direct[1], relay[1])
-
-    def product(child, anc):
+    def product(child, anc, panel, pieces=1):
         return call(
             functools.partial(product_kernel, child),
-            struct((SW, SW)),
-            [VMEM] * 8,
+            [struct((SW // pieces, SW))] * pieces,
+            [VMEM] * 10,
             scratch=[pltpu.VMEM((SW, WIDE), BF16)] * 2,
-        )(parts[child], *direct[child], *relay[child], *anc, meta)
-
-    theirs = [product(0, other)]
-    received = [step(theirs[0], "zl", 1, 2)]
-    parts[1] = after(parts[1], theirs[0])
-    theirs.append(product(1, other))
-    received.append(step(theirs[1], "zl", 1, 2))
-    mine = [product(child, own) for child in range(2)]
+        )(panel, *head, *tail, *far[child], *anc, meta)
+
+    sent = product(0, other, panel)
+    sent += product(1, other, after(panel, sent[0]), 2)
+    received = [step(value, "zl", 1, 2) for value in sent]
+    own = call(sort_gathered_kernel, pair, [SMEM, VMEM])(ids, after(whole, sent[1]))
+    mine = [product(child, own, panel)[0] for child in range(2)]
 
     packed = struct((10 * B, B))
     params = dict(
@@ -279,36 +279,33 @@
         compiler_params=pltpu.CompilerParams(vmem_limit_bytes=LIMIT),
         cost_estimate=pl.CostEstimate(flops=1024, bytes_accessed=1024, transcendentals=0),
     )
-
-    def block(child):
-        return pl.BlockSpec((SW, SW), lambda g: (child, 0))
-
-    anywhere = pl.BlockSpec(memory_space=pl.ANY)
+    blocks = [pl.BlockSpec((SW, SW), lambda g, child=child: (child, 0)) for child in range(2)]
     off, first = pl.pallas_call(
         functools.partial(finish_kernel, 0),
         out_shape=(struct(panel.shape), packed),
-        in_specs=[VMEM, VMEM, block(0), VMEM],
-        out_specs=[block(0), VMEM],
+        in_specs=[VMEM, VMEM, blocks[0], VMEM],
+        out_specs=[blocks[0], VMEM],
         **params,
     )(mine[0], received[0], panel, meta)
-    second = call(functools.partial(update_kernel, 1), packed, [VMEM] * 5)(
-        mine[1], theirs[1], parts[1], across, meta
+    second = call(functools.partial(update_kernel, 1), packed, [VMEM] * 6)(
+        mine[1], *sent[1:], panel, across, meta
     )
     off = pl.pallas_call(
         functools.partial(finish_kernel, 1),
         out_shape=struct(panel.shape),
-        in_specs=[VMEM, VMEM, block(1), VMEM, anywhere],
-        out_specs=block(1),
-        input_output_aliases={4: 0},
+        in_specs=[VMEM] * 3 + [blocks[1], VMEM, pl.BlockSpec(memory_space=pl.ANY)],
+        out_specs=blocks[1],
+        input_output_aliases={5: 0},
         **params,
-    )(mine[1], received[1], panel, meta, off)
+    )(mine[1], *received[1:], panel, meta, off)
 
     def swap(value):
         return lax.all_to_all(value, ROW, 0, 0, tiled=True)
 
     shape = (8, 20 * B // 8, B)
+    second = after(second, received[1])
     spread = swap(jnp.concatenate([first, second], axis=0).reshape(shape))
-    spread = after(spread, received[1])
+    spread = after(spread, received[2])
     summed = swap(call(sum_kernel, struct(shape), [VMEM])(spread)).reshape(20, B, B)
     out = call(child_kernel, struct(diag_inverse.shape), [VMEM] * 3)(summed, diag_inverse, meta)
     return off, out

time: 235 us -> 218 us (0.928); the launches traced: 231 us -> 217 us
  starting transfers between devices: 64.2 us -> 41.2 us
  waiting for transfers between devices: 111 us -> 94.8 us
  between operations: 1.21 us -> 14.4 us
  Pallas kernels: 42.5 us -> 49.2 us
  local copies, waits for them, and re-layouts: 10.8 us -> 16.7 us
    ppermute x21, starting transfers between devices: 42.3 us -> 20.9 us  [step(): return lax.ppermute(value, axis, [(i, (i + k) % n) for i in range(n)])]
    ppermute x4, waiting for transfers between devices: 9.37 us -> 0.01 us  [local(): got = [lax.ppermute(anc_inverse, Z, pairs) for pairs in rounds]]
    ppermute x21, waiting for transfers between devices: 87.6 us -> 80.9 us  [step(): return lax.ppermute(value, axis, [(i, (i + k) % n) for i in range(n)])]
    pallas_call x9 -> x7, Pallas kernels: 32.9 us -> 36.9 us  [the longest x4 26.8 us: product(): call(functools.partial(product_kernel, child), [struct((SW // pieces, SW)...]
    slice x5, local copies, waits for them, and re-layouts: 2.9 us -> 6.01 us  [the longest x1 2.7 us: local(): head = [step(panel[:cut], 'y', k) for k in (1, -1)]]
    unnamed x41 -> x55, local copies, waits for them, and re-layouts: 7.78 us -> 8.64 us
  transfers between devices with their start and end apart: 27 -> 28, of which waited for: 17 -> 12; matrix products, arithmetic and copies ran while one was open for 1% -> 2% of each run, Pallas kernels for 15% -> 19%
where the time goes in v3:
time: 218 us; the launch traced here: 217 us
  waiting for transfers between devices  94.8 us (43%)
  Pallas kernels  49.2 us (23%)
  starting transfers between devices  41.2 us (19%)
  local copies, waits for them, and re-layouts  16.7 us (8%)
  between operations  14.4 us (7%)
    ppermute x21, waiting for transfers between devices, step(): return lax.ppermute(value, axis, [(i, (i + k) % n) for i in range(n)])  80.9 us
    pallas_call x4, Pallas kernels, product(): call(functools.partial(product_kernel, child), [struct((SW // pieces, SW)...  26.8 us
    ppermute x21, starting transfers between devices, step(): return lax.ppermute(value, axis, [(i, (i + k) % n) for i in range(n)])  20.9 us
    all_to_all x2, waiting for transfers between devices, swap(): return lax.all_to_all(value, ROW, 0, 0, tiled=True)  13.9 us
    ppermute x4, starting transfers between devices, local(): got = [lax.ppermute(anc_inverse, Z, pairs) for pairs in rounds]  11.7 us
    unnamed x55, local copies, waits for them, and re-layouts  8.64 us
    all_to_all x2, starting transfers between devices, swap(): return lax.all_to_all(value, ROW, 0, 0, tiled=True)  8.55 us
    pallas_call x1, Pallas kernels, local(): other = call(sort_pieces_kernel, pair, [SMEM] + [VMEM] * 10)(ids, *pieces)  4.36 us
  transfers between devices with their start and end apart: 28, of which 12 were waited for; matrix products, arithmetic and copies ran while one was open for 2% of the time, Pallas kernels for 19%

profile of v3, /device:TPU:6, one launch (start us, length us, event | category | flops | bytes accessed | tf_op | source)
XLA Modules:
  0.0 217.4 jit_solution(4497399279754781281)
XLA Ops:
  7.2 2.7 %slice.26 = f32[768,512]{1,0:T(8,128)} slice(f32[1024,512]{1,0:T(8,128)} %panel.1), slice={[0:768], [0:512]} | slice | bytes 3145728 | tf_op jit(solution)/shard_map/slice | solution.py:239
  13.8 8.6 %collective-permute-start.7 = (f32[512,128]{1,0:T(8,128)S(1)}, f32[512,128]{1,0:T(8,128)S(1)}, u32[]{:S(2)}, u32[]{:S(2)}) collective-permute-start(f32[512,128]{1,0:T(8,128)S(1)} %copy-done.26), channel_id=1, source_target_pairs={{0,12},{16,0},{8,4},{24,8},{20,24},{4,20},{28,16},{12,28},{1,13},{... | collective-permute-start | bytes 786440 | tf_op jit(solution)/shard_map/ppermute | solution.py:248
  22.5 2.5 %collective-permute-start.9 = (f32[512,128]{1,0:T(8,128)S(1)}, f32[512,128]{1,0:T(8,128)S(1)}, u32[]{:S(2)}, u32[]{:S(2)}) collective-permute-start(f32[512,128]{1,0:T(8,128)S(1)} %copy-done.26), channel_id=1, source_target_pairs={{0,8},{16,12},{8,0},{24,4},{20,28},{4,24},{28,20},{12,16},{1,9},{1... | collective-permute-start | bytes 786440 | tf_op jit(solution)/shard_map/ppermute | solution.py:248
  25.0 22.6 %collective-permute-done.left = f32[768,512]{1,0:T(8,128)} collective-permute-done((f32[768,512]{1,0:T(8,128)}, f32[768,512]{1,0:T(8,128)}, u32[]{:S(2)}, u32[]{:S(2)}) %collective-permute-start) | collective-permute-done | bytes 1572896 | tf_op jit(solution)/shard_map/ppermute | solution.py:60
  50.0 2.1 fusion
  53.8 2.0 collective-permute-start.15
  56.8 1.7 collective-permute-start.11
  60.1 2.5 %collective-permute-done.12.refs_1_ = f32[2,512,128]{2,1,0:T(8,128)} collective-permute-done((f32[2,512,128]{2,1,0:T(8,128)}, f32[2,512,128]{2,1,0:T(8,128)}, u32[]{:S(2)}, u32[]{:S(2)}) %collective-permute-start.12) | collective-permute-done | bytes 524320 | tf_op jit(solution)/shard_map/ppermute | solution.py:60
  62.6 2.6 %collective-permute-start.3 = (f32[256,512]{1,0:T(8,128)S(1)}, f32[256,512]{1,0:T(8,128)S(1)}, u32[]{:S(2)}, u32[]{:S(2)}) collective-permute-start(f32[256,512]{1,0:T(8,128)S(1)} %slice.27), channel_id=1, source_target_pairs={{0,96},{32,0},{64,32},{96,64},{1,97},{33,1},{65,33},{97,65},{2,98}... | collective-permute-start | bytes 1572872 | tf_op jit(solution)/shard_map/ppermute | solution.py:60
  66.9 4.8 %collective-permute-done.11.bottom = f32[256,512]{1,0:T(8,128)S(1)} collective-permute-done((f32[256,512]{1,0:T(8,128)S(1)}, f32[256,512]{1,0:T(8,128)S(1)}, u32[]{:S(2)}, u32[]{:S(2)}) %collective-permute-start.11) | collective-permute-done | bytes 524320 | tf_op jit(solution)/shard_map/ppermute | solution.py:60
  71.8 8.5 %collective-permute-done.13.refs_2_ = f32[2,512,128]{2,1,0:T(8,128)} collective-permute-done((f32[2,512,128]{2,1,0:T(8,128)}, f32[2,512,128]{2,1,0:T(8,128)}, u32[]{:S(2)}, u32[]{:S(2)}) %collective-permute-start.13) | collective-permute-done | bytes 524320 | tf_op jit(solution)/shard_map/ppermute | solution.py:60
  81.3 2.1 collective-permute-start.16
  85.1 3.8 %collective-permute-done.14.refs_3_ = f32[512,128]{1,0:T(8,128)S(1)} collective-permute-done((f32[512,128]{1,0:T(8,128)S(1)}, f32[512,128]{1,0:T(8,128)S(1)}, u32[]{:S(2)}, u32[]{:S(2)}) %collective-permute-start.14) | collective-permute-done | bytes 262176 | tf_op jit(solution)/shard_map/ppermute | solution.py:60
  89.0 5.5 %collective-permute-done.16.refs_4_ = f32[512,128]{1,0:T(8,128)} collective-permute-done((f32[512,128]{1,0:T(8,128)S(1)}, f32[512,128]{1,0:T(8,128)}, u32[]{:S(2)}, u32[]{:S(2)}) %collective-permute-start.16) | collective-permute-done | bytes 262176 | tf_op jit(solution)/shard_map/ppermute | solution.py:60
  97.8 4.4 %shard_map.69 = (bf16[512,2048]{1,0:T(8,128)(2,1)S(1)}, bf16[512,2048]{1,0:T(8,128)(2,1)S(1)}) custom-call(s32[5]{0:T(128)S(1)} %stack.23.ids, f32[2,512,128]{2,1,0:T(8,128)} %get-tuple-element.23.refs_0_, f32[2,512,128]{2,1,0:T(8,128)} %collective-permute-done.12.refs_1_, f32[2,512,128]{2,1,0:T(8,128)} %collective-permute-done.13.refs_2_, ...), custom_call_target="tpu_custom_call" | custom-call | flops 1024 | bytes 1024 | tf_op jit(solution)/shard_map/pallas_call | solution.py:259
  102.2 7.1 %shard_map.71 = f32[512,512]{1,0:T(8,128)} custom-call(f32[1024,512]{1,0:T(8,128)S(1)} %copy-done, f32[768,512]{1,0:T(8,128)} %collective-permute-done.left, f32[768,512]{1,0:T(8,128)} %collective-permute-done.1.right, f32[256,512]{1,0:T(8,128)S(1)} %collective-permute-done.2.left_tail, f32[256,512]{1,0:T(8,128)S(1)} %collective-permute-done.3.right_tail, ...), custom_call_target="tpu_custom_call" | custom-call | flops 1024 | bytes 1024 | tf_op jit(solution)/shard_map/pallas_call | solution.py:263
  110.1 2.6 %collective-permute-done.4.top = f32[256,512]{1,0:T(8,128)S(1)} collective-permute-done((f32[256,512]{1,0:T(8,128)}, f32[256,512]{1,0:T(8,128)S(1)}, u32[]{:S(2)}, u32[]{:S(2)}) %collective-permute-start.4) | collective-permute-done | bytes 524320 | tf_op jit(solution)/shard_map/ppermute | solution.py:60
  112.7 7.2 %shard_map.72 = (f32[256,512]{1,0:T(8,128)}, f32[256,512]{1,0:T(8,128)S(1)}) custom-call(f32[1024,512]{1,0:T(8,128)S(1)} %copy-done, f32[768,512]{1,0:T(8,128)} %collective-permute-done.left, f32[768,512]{1,0:T(8,128)} %collective-permute-done.1.right, f32[256,512]{1,0:T(8,128)S(1)} %collective-permute-done.2.left_tail, ...), custom_call_target="tpu_custom_call" | custom-call | flops 1024 | bytes 1024 | tf_op jit(solution)/shard_map/pallas_call | solution.py:263
  121.0 2.2 %copy-done.6 = f32[16,512,128]{2,1,0:T(8,128)S(1)} copy-done((f32[16,512,128]{2,1,0:T(8,128)S(1)}, f32[16,512,128]{2,1,0:T(8,128)}, u32[]{:S(2)}) %copy-start.6) | copy-done | bytes 4194328
  123.2 2.0 shard_map.73
  125.3 6.2 %shard_map.74.mine = f32[512,512]{1,0:T(8,128)S(1)} custom-call(f32[1024,512]{1,0:T(8,128)S(1)} %copy-done, f32[768,512]{1,0:T(8,128)} %collective-permute-done.left, f32[768,512]{1,0:T(8,128)} %collective-permute-done.1.right, f32[256,512]{1,0:T(8,128)S(1)} %copy-done.4, f32[256,512]{1,0:T(8,128)S(1)} %copy-done.2, f32[256,512]{1,0:T(8,128)S(1)} %copy-done.16, ...), custom_call_target="tpu_custom_call" | custom-call | flops 1024 | bytes 1024 | tf_op jit(solution)/shard_map/pallas_call | solution.py:263
  131.6 6.3 %shard_map.75.mine = f32[512,512]{1,0:T(8,128)S(1)} custom-call(f32[1024,512]{1,0:T(8,128)S(1)} %copy-done, f32[768,512]{1,0:T(8,128)} %collective-permute-done.left, f32[768,512]{1,0:T(8,128)} %collective-permute-done.1.right, f32[256,512]{1,0:T(8,128)S(1)} %copy-done.4, f32[256,512]{1,0:T(8,128)S(1)} %copy-done.2, f32[256,512]{1,0:T(8,128)S(1)} %copy-done.9, ...), custom_call_target="tpu_custom_call" | custom-call | flops 1024 | bytes 1024 | tf_op jit(solution)/shard_map/pallas_call | solution.py:263
  137.9 3.6 %shard_map.78 = f32[1280,128]{1,0:T(8,128)S(1)} custom-call(f32[512,512]{1,0:T(8,128)S(1)} %shard_map.74.mine, f32[256,512]{1,0:T(8,128)} %get-tuple-element.31.sent_top, f32[256,512]{1,0:T(8,128)S(1)} %copy-done.21, f32[1024,512]{1,0:T(8,128)S(1)} %copy-done, f32[512,512]{1,0:T(8,128)S(1)} %copy-done.19, f32[8,2048]{1,0:T(8,128)S(1)} %shard_map.70.meta.refs_2_.refs_3_), custom_call_target="tpu_custom_call" | custom-call | flops 1024 | bytes 1024 | tf_op jit(solution)/shard_map/pallas_call | solution.py:290
  141.6 4.4 %collective-permute-done.22.refs_0_ = f32[256,512]{1,0:T(8,128)} collective-permute-done((f32[256,512]{1,0:T(8,128)}, f32[256,512]{1,0:T(8,128)}, u32[]{:S(2)}, u32[]{:S(2)}) %collective-permute-start.22) | collective-permute-done | bytes 524320 | tf_op jit(solution)/shard_map/ppermute | solution.py:60
  145.9 2.9 %shard_map.76 = (f32[1024,512]{1,0:T(8,128)}, f32[1280,128]{1,0:T(8,128)S(1)}) custom-call(f32[512,512]{1,0:T(8,128)S(1)} %shard_map.75.mine, f32[512,512]{1,0:T(8,128)} %collective-permute-done.24.refs_0_, f32[1024,512]{1,0:T(8,128)S(1)} %copy-done, f32[8,2048]{1,0:T(8,128)S(1)} %shard_map.70.meta.refs_2_.refs_3_), custom_call_target="tpu_custom_call" | custom-call | flops 1024 | bytes 1024 | tf_op jit(solution)/shard_map/pallas_call | solution.py:283
  150.0 4.3 %all-to-all-start = ((f32[8,320,128]{2,1,0:T(8,128)}), f32[8,320,128]{2,1,0:T(8,128)}, u32[]{:S(2)}, u32[]{:S(2)}) async-start(f32[8,320,128]{2,1,0:T(8,128)} %bitcast.13), calls=%async_computation | async-start | bytes 2621440 | tf_op jit(solution)/shard_map/all_to_all | solution.py:303
  154.2 1.9 collective-permute-start.23
  156.1 25.1 %collective-permute-done.23.refs_1_ = f32[256,512]{1,0:T(8,128)S(1)} collective-permute-done((f32[256,512]{1,0:T(8,128)}, f32[256,512]{1,0:T(8,128)S(1)}, u32[]{:S(2)}, u32[]{:S(2)}) %collective-permute-start.23) | collective-permute-done | bytes 524320 | tf_op jit(solution)/shard_map/ppermute | solution.py:60
  184.6 4.3 %all-to-all-start.1 = ((f32[8,320,128]{2,1,0:T(8,128)}), f32[8,320,128]{2,1,0:T(8,128)}, u32[]{:S(2)}, u32[]{:S(2)}) async-start(f32[8,320,128]{2,1,0:T(8,128)} %copy-done.5), calls=%async_computation.1 | async-start | bytes 2621440 | tf_op jit(solution)/shard_map/all_to_all | solution.py:303
  189.9 2.2 %shard_map.77 = f32[1024,512]{1,0:T(8,128)} custom-call(f32[512,512]{1,0:T(8,128)S(1)} %shard_map.74.mine, f32[256,512]{1,0:T(8,128)} %collective-permute-done.22.refs_0_, f32[256,512]{1,0:T(8,128)S(1)} %copy-done.23, f32[1024,512]{1,0:T(8,128)S(1)} %copy-done, f32[8,2048]{1,0:T(8,128)S(1)} %shard_map.70.meta.refs_2_.refs_3_, ...), custom_call_target="tpu_custom_call", output_to_operand_aliasing={{}: (5, {})} | custom-call | flops 1024 | bytes 1024 | tf_op jit(solution)/shard_map/pallas_call | solution.py:293
  192.1 13.9 %all-to-all-done.1 = f32[8,320,128]{2,1,0:T(8,128)} async-done(((f32[8,320,128]{2,1,0:T(8,128)}), f32[8,320,128]{2,1,0:T(8,128)}, u32[]{:S(2)}, u32[]{:S(2)}) %all-to-all-start.1) | async-done | bytes 1310752 | tf_op jit(solution)/shard_map/all_to_all | solution.py:303
  207.6 2.9 %shard_map.80 = f32[1024,512]{1,0:T(8,128)} custom-call(f32[20,128,128]{2,1,0:T(8,128)} %bitcast.9.parts, f32[1024,512]{1,0:T(8,128)S(1)} %copy-done.17, f32[8,2048]{1,0:T(8,128)S(1)} %shard_map.70.meta.refs_2_.refs_3_), custom_call_target="tpu_custom_call" | custom-call | flops 1024 | bytes 1024 | tf_op jit(solution)/shard_map/pallas_call | solution.py:310
  (102 shorter events, 27.4 us)
Async XLA Ops:
  7.2 113.8 %all-gather.3.cloned.1.call-start = ((), (), s32[]{:S(2)}) async-start(), calls=%async_computation.2 | async-start | bytes 4718592 | tf_op jit(solution)/shard_map/all_gather | solution.py:252
  9.9 37.7 %collective-permute-start = (f32[768,512]{1,0:T(8,128)}, f32[768,512]{1,0:T(8,128)}, u32[]{:S(2)}, u32[]{:S(2)}) collective-permute-start(f32[768,512]{1,0:T(8,128)} %slice.26), channel_id=1, source_target_pairs={{0,32},{32,64},{64,96},{96,0},{1,33},{33,65},{65,97},{97,1},{2,34}... | collective-permute-start | bytes 4718600 | tf_op jit(solution)/shard_map/ppermute | solution.py:60
  11.5 36.2 %collective-permute-start.1 = (f32[768,512]{1,0:T(8,128)}, f32[768,512]{1,0:T(8,128)}, u32[]{:S(2)}, u32[]{:S(2)}) collective-permute-start(f32[768,512]{1,0:T(8,128)} %slice.26), channel_id=1, source_target_pairs={{0,96},{32,0},{64,32},{96,64},{1,97},{33,1},{65,33},{97,65},{2,98}... | collective-permute-start | bytes 4718600 | tf_op jit(solution)/shard_map/ppermute | solution.py:60
  13.2 9.3 %collective-permute-start.6 = (f32[512,128]{1,0:T(8,128)S(1)}, f32[512,128]{1,0:T(8,128)S(1)}, u32[]{:S(2)}, u32[]{:S(2)}) collective-permute-start(f32[512,128]{1,0:T(8,128)S(1)} %copy-done.26), channel_id=1, source_target_pairs={{0,0},{16,4},{8,8},{24,12},{20,20},{4,16},{28,28},{12,24},{1,1},{1... | collective-permute-start | bytes 786440 | tf_op jit(solution)/shard_map/ppermute | solution.py:248
  13.8 33.8 %collective-permute-start.7 = (f32[512,128]{1,0:T(8,128)S(1)}, f32[512,128]{1,0:T(8,128)S(1)}, u32[]{:S(2)}, u32[]{:S(2)}) collective-permute-start(f32[512,128]{1,0:T(8,128)S(1)} %copy-done.26), channel_id=1, source_target_pairs={{0,12},{16,0},{8,4},{24,8},{20,24},{4,20},{28,16},{12,28},{1,13},{... | collective-permute-start | bytes 786440 | tf_op jit(solution)/shard_map/ppermute | solution.py:248
  22.5 25.2 %collective-permute-start.8 = (f32[512,128]{1,0:T(8,128)S(1)}, f32[512,128]{1,0:T(8,128)S(1)}, u32[]{:S(2)}, u32[]{:S(2)}) collective-permute-start(f32[512,128]{1,0:T(8,128)S(1)} %copy-done.26), channel_id=1, source_target_pairs={{0,4},{16,8},{8,12},{24,0},{20,16},{4,28},{28,24},{12,20},{1,5},{1... | collective-permute-start | bytes 786440 | tf_op jit(solution)/shard_map/ppermute | solution.py:248
  22.5 25.2 %collective-permute-start.9 = (f32[512,128]{1,0:T(8,128)S(1)}, f32[512,128]{1,0:T(8,128)S(1)}, u32[]{:S(2)}, u32[]{:S(2)}) collective-permute-start(f32[512,128]{1,0:T(8,128)S(1)} %copy-done.26), channel_id=1, source_target_pairs={{0,8},{16,12},{8,0},{24,4},{20,28},{4,24},{28,20},{12,16},{1,9},{1... | collective-permute-start | bytes 786440 | tf_op jit(solution)/shard_map/ppermute | solution.py:248
  49.4 13.2 %collective-permute-start.12 = (f32[2,512,128]{2,1,0:T(8,128)}, f32[2,512,128]{2,1,0:T(8,128)}, u32[]{:S(2)}, u32[]{:S(2)}) collective-permute-start(f32[2,512,128]{2,1,0:T(8,128)} %get-tuple-element.23.refs_0_), channel_id=1, source_target_pairs={{0,1},{1,2},{2,3},{3,0},{4,5},{5,6},{6,7},{7,4},{8,9},{9,10},{10,1... | collective-permute-start | bytes 1572872 | tf_op jit(solution)/shard_map/ppermute | solution.py:60
  52.1 13.7 %collective-permute-start.10 = (f32[256,512]{1,0:T(8,128)S(1)}, f32[256,512]{1,0:T(8,128)S(1)}, u32[]{:S(2)}, u32[]{:S(2)}) collective-permute-start(f32[256,512]{1,0:T(8,128)S(1)} %get-tuple-element.40), channel_id=1, source_target_pairs={{0,32},{32,64},{64,96},{96,0},{1,33},{33,65},{65,97},{97,1},{2,34}... | collective-permute-start | bytes 1572872 | tf_op jit(solution)/shard_map/ppermute | solution.py:60
  53.7 40.7 %copy-start.25 = (s32[64,32]{0,1:T(8,128)S(1)}, s32[64,32]{0,1:T(8,128)}, u32[]{:S(2)}) copy-start(s32[64,32]{0,1:T(8,128)} %param.9) | copy-start | bytes 24580
  53.8 40.8 %copy-start.24 = (s32[64]{0:T(128)S(1)}, s32[64]{0:T(128)}, u32[]{:S(2)}) copy-start(s32[64]{0:T(128)} %widths.1) | copy-start | bytes 772
  53.8 29.9 %collective-permute-start.15 = (f32[512,512]{1,0:T(8,128)S(1)}, f32[512,512]{1,0:T(8,128)S(1)}, u32[]{:S(2)}, u32[]{:S(2)}) collective-permute-start(f32[512,512]{1,0:T(8,128)S(1)} %slice.32), channel_id=1, source_target_pairs={{0,16},{16,0},{1,17},{17,1},{2,18},{18,2},{3,19},{19,3},{4,20},{20... | collective-permute-start | bytes 3145736 | tf_op jit(solution)/shard_map/ppermute | solution.py:60
  56.8 14.9 %collective-permute-start.11 = (f32[256,512]{1,0:T(8,128)S(1)}, f32[256,512]{1,0:T(8,128)S(1)}, u32[]{:S(2)}, u32[]{:S(2)}) collective-permute-start(f32[256,512]{1,0:T(8,128)S(1)} %slice.36), channel_id=1, source_target_pairs={{0,96},{32,0},{64,32},{96,64},{1,97},{33,1},{65,33},{97,65},{2,98}... | collective-permute-start | bytes 1572872 | tf_op jit(solution)/shard_map/ppermute | solution.py:60
  58.6 21.7 %collective-permute-start.13 = (f32[2,512,128]{2,1,0:T(8,128)}, f32[2,512,128]{2,1,0:T(8,128)}, u32[]{:S(2)}, u32[]{:S(2)}) collective-permute-start(f32[2,512,128]{2,1,0:T(8,128)} %get-tuple-element.23.refs_0_), channel_id=1, source_target_pairs={{0,3},{1,0},{2,1},{3,2},{4,7},{5,4},{6,5},{7,6},{8,11},{9,8},{10,9... | collective-permute-start | bytes 1572872 | tf_op jit(solution)/shard_map/ppermute | solution.py:60
  62.6 18.6 %collective-permute-start.3 = (f32[256,512]{1,0:T(8,128)S(1)}, f32[256,512]{1,0:T(8,128)S(1)}, u32[]{:S(2)}, u32[]{:S(2)}) collective-permute-start(f32[256,512]{1,0:T(8,128)S(1)} %slice.27), channel_id=1, source_target_pairs={{0,96},{32,0},{64,32},{96,64},{1,97},{33,1},{65,33},{97,65},{2,98}... | collective-permute-start | bytes 1572872 | tf_op jit(solution)/shard_map/ppermute | solution.py:60
  65.8 17.6 %collective-permute-start.2 = (f32[256,512]{1,0:T(8,128)S(1)}, f32[256,512]{1,0:T(8,128)S(1)}, u32[]{:S(2)}, u32[]{:S(2)}) collective-permute-start(f32[256,512]{1,0:T(8,128)S(1)} %slice.27), channel_id=1, source_target_pairs={{0,32},{32,64},{64,96},{96,0},{1,33},{33,65},{65,97},{97,1},{2,34}... | collective-permute-start | bytes 1572872 | tf_op jit(solution)/shard_map/ppermute | solution.py:60
  71.8 23.9 %collective-permute-start.17 = (f32[2,512,128]{2,1,0:T(8,128)}, f32[2,512,128]{2,1,0:T(8,128)}, u32[]{:S(2)}, u32[]{:S(2)}) collective-permute-start(f32[2,512,128]{2,1,0:T(8,128)} %get-tuple-element.23.refs_0_), channel_id=1, source_target_pairs={{0,128},{128,0},{1,129},{129,1},{2,130},{130,2},{3,131},{131,3},{4... | collective-permute-start | bytes 1572872 | tf_op jit(solution)/shard_map/ppermute | solution.py:60
  80.3 8.7 %collective-permute-start.14 = (f32[512,128]{1,0:T(8,128)S(1)}, f32[512,128]{1,0:T(8,128)S(1)}, u32[]{:S(2)}, u32[]{:S(2)}) collective-permute-start(f32[512,128]{1,0:T(8,128)S(1)} %slice_bitcast_fusion.1), channel_id=1, source_target_pairs={{0,1},{1,2},{2,3},{3,0},{4,5},{5,6},{6,7},{7,4},{8,9},{9,10},{10,1... | collective-permute-start | bytes 786440 | tf_op jit(solution)/shard_map/ppermute | solution.py:60
  81.3 31.4 %copy-start.1 = (f32[256,512]{1,0:T(8,128)}, f32[256,512]{1,0:T(8,128)S(1)}, u32[]{:S(2)}) copy-start(f32[256,512]{1,0:T(8,128)S(1)} %collective-permute-done.3.right_tail) | copy-start | bytes 1572868
  81.3 13.1 %collective-permute-start.16 = (f32[512,128]{1,0:T(8,128)S(1)}, f32[512,128]{1,0:T(8,128)}, u32[]{:S(2)}, u32[]{:S(2)}) collective-permute-start(f32[512,128]{1,0:T(8,128)S(1)} %slice_bitcast_fusion), channel_id=1, source_target_pairs={{0,3},{1,0},{2,1},{3,2},{4,7},{5,4},{6,5},{7,6},{8,11},{9,8},{10,9... | collective-permute-start | bytes 786440 | tf_op jit(solution)/shard_map/ppermute | solution.py:60
  83.4 29.3 %copy-start.3 = (f32[256,512]{1,0:T(8,128)}, f32[256,512]{1,0:T(8,128)S(1)}, u32[]{:S(2)}) copy-start(f32[256,512]{1,0:T(8,128)S(1)} %collective-permute-done.2.left_tail) | copy-start | bytes 1572868
  83.4 14.4 %collective-permute-start.18 = (f32[2,512,128]{2,1,0:T(8,128)}, f32[2,512,128]{2,1,0:T(8,128)}, u32[]{:S(2)}, u32[]{:S(2)}) collective-permute-start(f32[2,512,128]{2,1,0:T(8,128)} %collective-permute-done.12.refs_1_), channel_id=1, source_target_pairs={{0,128},{128,0},{1,129},{129,1},{2,130},{130,2},{3,131},{131,3},{4... | collective-permute-start | bytes 1572872 | tf_op jit(solution)/shard_map/ppermute | solution.py:60
  84.7 13.2 %collective-permute-start.19 = (f32[2,512,128]{2,1,0:T(8,128)}, f32[2,512,128]{2,1,0:T(8,128)}, u32[]{:S(2)}, u32[]{:S(2)}) collective-permute-start(f32[2,512,128]{2,1,0:T(8,128)} %collective-permute-done.13.refs_2_), channel_id=1, source_target_pairs={{0,128},{128,0},{1,129},{129,1},{2,130},{130,2},{3,131},{131,3},{4... | collective-permute-start | bytes 1572872 | tf_op jit(solution)/shard_map/ppermute | solution.py:60
  88.9 8.3 %collective-permute-start.20 = (f32[512,128]{1,0:T(8,128)S(1)}, f32[512,128]{1,0:T(8,128)}, u32[]{:S(2)}, u32[]{:S(2)}) collective-permute-start(f32[512,128]{1,0:T(8,128)S(1)} %collective-permute-done.14.refs_3_), channel_id=1, source_target_pairs={{0,128},{128,0},{1,129},{129,1},{2,130},{130,2},{3,131},{131,3},{4... | collective-permute-start | bytes 786440 | tf_op jit(solution)/shard_map/ppermute | solution.py:60
  94.4 3.4 %collective-permute-start.21 = (f32[512,128]{1,0:T(8,128)}, f32[512,128]{1,0:T(8,128)}, u32[]{:S(2)}, u32[]{:S(2)}) collective-permute-start(f32[512,128]{1,0:T(8,128)} %collective-permute-done.16.refs_4_), channel_id=1, source_target_pairs={{0,128},{128,0},{1,129},{129,1},{2,130},{130,2},{3,131},{131,3},{4... | collective-permute-start | bytes 786440 | tf_op jit(solution)/shard_map/ppermute | solution.py:60
  95.7 14.4 %collective-permute-start.5 = (f32[256,512]{1,0:T(8,128)S(1)}, f32[256,512]{1,0:T(8,128)S(1)}, u32[]{:S(2)}, u32[]{:S(2)}) collective-permute-start(f32[256,512]{1,0:T(8,128)S(1)} %collective-permute-done.3.right_tail), channel_id=1, source_target_pairs={{0,96},{32,0},{64,32},{96,64},{1,97},{33,1},{65,33},{97,65},{2,98}... | collective-permute-start | bytes 1572872 | tf_op jit(solution)/shard_map/ppermute | solution.py:60
  97.2 15.5 %collective-permute-start.4 = (f32[256,512]{1,0:T(8,128)}, f32[256,512]{1,0:T(8,128)S(1)}, u32[]{:S(2)}, u32[]{:S(2)}) collective-permute-start(f32[256,512]{1,0:T(8,128)} %get-tuple-element.41), channel_id=1, source_target_pairs={{0,32},{32,64},{64,96},{96,0},{1,33},{33,65},{65,97},{97,1},{2,34}... | collective-permute-start | bytes 1572872 | tf_op jit(solution)/shard_map/ppermute | solution.py:60
  109.4 36.6 %collective-permute-start.24 = (f32[512,512]{1,0:T(8,128)}, f32[512,512]{1,0:T(8,128)}, u32[]{:S(2)}, u32[]{:S(2)}) collective-permute-start(f32[512,512]{1,0:T(8,128)} %shard_map.71), channel_id=1, source_target_pairs={{0,16},{16,0},{1,17},{17,1},{2,18},{18,2},{3,19},{19,3},{4,20},{20... | collective-permute-start | bytes 3145736 | tf_op jit(solution)/shard_map/ppermute | solution.py:60
  120.7 25.2 %collective-permute-start.22 = (f32[256,512]{1,0:T(8,128)}, f32[256,512]{1,0:T(8,128)}, u32[]{:S(2)}, u32[]{:S(2)}) collective-permute-start(f32[256,512]{1,0:T(8,128)} %get-tuple-element.31.sent_top), channel_id=1, source_target_pairs={{0,16},{16,0},{1,17},{17,1},{2,18},{18,2},{3,19},{19,3},{4,20},{20... | collective-permute-start | bytes 1572872 | tf_op jit(solution)/shard_map/ppermute | solution.py:60
  150.0 32.1 %all-to-all-start = ((f32[8,320,128]{2,1,0:T(8,128)}), f32[8,320,128]{2,1,0:T(8,128)}, u32[]{:S(2)}, u32[]{:S(2)}) async-start(f32[8,320,128]{2,1,0:T(8,128)} %bitcast.13), calls=%async_computation | async-start | bytes 2621440 | tf_op jit(solution)/shard_map/all_to_all | solution.py:303
  154.2 27.0 %collective-permute-start.23 = (f32[256,512]{1,0:T(8,128)}, f32[256,512]{1,0:T(8,128)S(1)}, u32[]{:S(2)}, u32[]{:S(2)}) collective-permute-start(f32[256,512]{1,0:T(8,128)} %copy-done.20), channel_id=1, source_target_pairs={{0,16},{16,0},{1,17},{17,1},{2,18},{18,2},{3,19},{19,3},{4,20},{20... | collective-permute-start | bytes 1572872 | tf_op jit(solution)/shard_map/ppermute | solution.py:60
  184.6 21.4 %all-to-all-start.1 = ((f32[8,320,128]{2,1,0:T(8,128)}), f32[8,320,128]{2,1,0:T(8,128)}, u32[]{:S(2)}, u32[]{:S(2)}) async-start(f32[8,320,128]{2,1,0:T(8,128)} %copy-done.5), calls=%async_computation.1 | async-start | bytes 2621440 | tf_op jit(solution)/shard_map/all_to_all | solution.py:303
  (23 other events, 108.7 us)
Sparse Core Ops, SparseCore 0:
  49.5 45.7 all-gather.2

commit v4 on v0

v4 whole, which is shorter than its diff:
```python
import functools

import jax
import jax.numpy as jnp
from jax import lax
from jax.experimental import pallas as pl
from jax.experimental.pallas import tpu as pltpu
from jax.sharding import Mesh, PartitionSpec as P

B = 128
SW = 512
WIDE = 4096
LIMIT = 24 * 2**20
ROW = ("y", "zl")
GROUP = ("core", "zh", "x")
DIRECTIONS = ((0, 0), (3, 0), (1, 0), (0, 1), (3, 1), (1, 1), (2, 0), (2, 1))
CUTS = (0, 192, 352, 512)

VMEM = pl.BlockSpec(memory_space=pltpu.VMEM)
SMEM = pl.BlockSpec(memory_space=pltpu.SMEM)
F32 = jnp.float32
BF16 = jnp.bfloat16


def call(kernel, out_shape, specs, out_specs=None, scratch=(), aliases=None):
    single = not isinstance(out_shape, (tuple, list))
    return pl.pallas_call(
        kernel,
        out_shape=out_shape,
        in_specs=specs,
        out_specs=out_specs if out_specs is not None else (VMEM if single else [VMEM] * len(out_shape)),
        scratch_shapes=list(scratch),
        input_output_aliases=aliases or {},
        compiler_params=pltpu.CompilerParams(vmem_limit_bytes=LIMIT),
        cost_estimate=pl.CostEstimate(flops=1024, bytes_accessed=1024, transcendentals=0),
    )


def struct(shape, dtype=F32):
    return jax.ShapeDtypeStruct(shape, dtype)


def step(value, axis, k, n=4):
    return lax.ppermute(value, axis, [(i, (i + k) % n) for i in range(n)])


def split(value):
    high = value.astype(BF16)
    return high, (value - high.astype(F32)).astype(BF16)


def dot3(a, b):
    dims = (((1,), (1,)), ((), ()))
    mul = functools.partial(lax.dot_general, dimension_numbers=dims, preferred_element_type=F32)
    return mul(a[0], b[0]) + (mul(a[0], b[1]) + mul(a[1], b[0]))


def meta_kernel(ids, widths, pattern, out):
    core, y, zl, zh, x = (ids[i] for i in range(5))
    first = ((core * 4 + zh) * 4 + x) * 2
    for child in range(2):
        for d, (dy, dz) in enumerate(DIRECTIONS):
            block = ((y + dy) % 4 * 2 + (zl + dz) % 2) * 4
            for k in range(4):
                value = pattern[first + child, block + k].astype(F32)
                out[child : child + 1, (d * 4 + k) * B : (d * 4 + k + 1) * B] = jnp.full((1, B), value)
        out[2 + child : 3 + child, :] = jnp.full((1, WIDE), (widths[first + child] * B).astype(F32))
    out[4:8, :] = jnp.zeros((4, WIDE), F32)


def column_mask(meta, child):
    position = lax.broadcasted_iota(jnp.int32, (SW, B), 0).astype(F32)
    return (position < meta[2 + child : 3 + child, :B]).astype(F32)


def masks(meta, child, d):
    return jnp.concatenate([column_mask(meta, child)] * 4, axis=1) * meta[child : child + 1, d * SW : (d + 1) * SW]


def columns(ids, anc, d):
    dy, dz = DIRECTIONS[d]
    block = (ids[1] + dy) % 4 * 2 + (ids[2] + dz) % 2
    return split(anc[:, pl.ds(pl.multiple_of(block * SW, SW), SW)])


def first_kernel(ids, anc, *refs):
    panels, meta, out = refs[:4], refs[4], refs[5]
    for d, panel in enumerate(panels):
        right = columns(ids, anc, d)
        for child in range(2):
            rows = slice(child * SW, (child + 1) * SW)
            value = dot3(split(panel[rows] * masks(meta, child, d)), right)
            out[rows] = value if d == 0 else out[rows] + value


def second_kernel(ids, anc, total, *refs):
    panels, meta, (out, high, low) = refs[:3], refs[3], refs[4:]
    for d, panel in enumerate(panels, 4):
        right = columns(ids, anc, d)
        for child in range(2):
            rows = slice(child * SW, (child + 1) * SW)
            before = total[rows] if d == 4 else out[rows]
            out[rows] = before + dot3(split(panel[rows] * masks(meta, child, d)), right)
    high[...], low[...] = columns(ids, anc, 7)


def last_kernel(child, total, one, two, three, high, low, panel, meta, *refs):
    off, update = refs[-2:]
    value = jnp.concatenate([one[...], two[...], three[...]], axis=0)
    value = dot3(split(value * masks(meta, child, 7)), (high[...], low[...]))
    mask = masks(meta, child, 0)
    product = (total[...] + value) * mask
    off[...] = -product
    lower_blocks(update, [(split(product), split(panel[...] * mask))])


def lower_blocks(update, pairs):
    at = 0
    for a in range(4):
        value = None
        for left, right in pairs:
            term = dot3([v[a * B : (a + 1) * B] for v in left], [v[: (a + 1) * B] for v in right])
            value = term if value is None else value + term
        for b in range(a + 1):
            update[at * B : (at + 1) * B, :] = value[:, b * B : (b + 1) * B]
            at += 1


def sum_kernel(parts, out):
    total = parts[0]
    for k in range(1, 8):
        total += parts[k]
    for k in range(8):
        out[k] = total


def child_kernel(parts, diag, meta, out):
    at = 0
    for child in range(2):
        across = lax.broadcasted_iota(jnp.int32, (1, SW), 1).astype(F32) < meta[2 + child : 3 + child, :SW]
        across = across.astype(F32)
        mask = column_mask(meta, child)
        for a in range(4):
            for b in range(a + 1):
                block = parts[at]
                at += 1
                for (i, j), value in {(b, a): block.T, (a, b): block}.items():
                    lines = slice(child * SW + i * B, child * SW + (i + 1) * B)
                    lanes = slice(j * B, (j + 1) * B)
                    rows = mask[i * B : (i + 1) * B]
                    out[lines, lanes] = (diag[lines, lanes] + value) * rows * across[:, lanes]


def after(value, *before):
    return lax.optimization_barrier((value, *before))[0]


def local(anc_inverse, panel, diag_inverse, widths, pattern):
    names = ("core", "y", "zl", "zh", "x")
    ids = jnp.stack([lax.axis_index(n) for n in names]).astype(jnp.int32)
    meta = call(meta_kernel, struct((8, WIDE)), [SMEM] * 3)(ids, widths, pattern)
    anc = lax.all_gather(anc_inverse, GROUP, axis=1, tiled=True)

    left, right, across = step(panel, "y", 1), step(panel, "y", -1), step(panel, "zl", 1, 2)
    came, crossed = after(left, right, across), after(across, right, left)
    left_across, right_across, far = step(came, "zl", 1, 2), step(crossed, "y", -1), step(came, "y", 1)
    left_across, right_across, far = lax.optimization_barrier((left_across, right_across, far))
    last = []
    for first in (0, SW):
        one, two, three = (
            value[first + a : first + b]
            for value, a, b in zip((left_across, right_across, far), CUTS[:-1], CUTS[1:])
        )
        last.append((step(one, "y", 1), step(two, "y", -1), step(three, "zl", 1, 2)))
    anc = after(anc, left_across, right_across, far)

    total = struct(panel.shape)
    term = call(first_kernel, total, [SMEM] + [VMEM] * 6)(ids, anc, panel, left, right, across, meta)
    piece = struct((SW, SW), BF16)
    term, high, low = call(second_kernel, (total, piece, piece), [SMEM] + [VMEM] * 6)(
        ids, anc, term, left_across, right_across, far, meta
    )
    off, updates = None, []
    for child in range(2):
        block = pl.BlockSpec((SW, SW), lambda g, child=child: (child, 0))
        off, update = pl.pallas_call(
            functools.partial(last_kernel, child),
            grid=(1,),
            out_shape=(struct(panel.shape), struct((10 * B, B))),
            in_specs=[block] + [VMEM] * 5 + [block, VMEM] + [pl.BlockSpec(memory_space=pl.ANY)] * child,
            out_specs=[block, VMEM],
            input_output_aliases={8: 0} if child else {},
            compiler_params=pltpu.CompilerParams(vmem_limit_bytes=LIMIT),
            cost_estimate=pl.CostEstimate(flops=1024, bytes_accessed=1024, transcendentals=0),
        )(term, *last[child], high, low, panel, meta, *([off] if child else []))
        updates.append(update)

    def swap(value):
        return lax.all_to_all(value, ROW, 0, 0, tiled=True)

    shape = (8, 20 * B // 8, B)
    spread = swap(jnp.concatenate(updates, axis=0).reshape(shape))
    summed = swap(call(sum_kernel, struct(shape), [VMEM])(spread)).reshape(20, B, B)
    out = call(child_kernel, struct(diag_inverse.shape), [VMEM] * 3)(summed, diag_inverse, meta)
    return off, out


def solution(mesh):
    fine = Mesh(mesh.devices.reshape(2, 4, 2, 4, 4), ("core", "y", "zl", "zh", "x"))
    in_specs = (P(ROW, GROUP), P(GROUP, ROW), P(GROUP, None), P(), P())
    out_specs = (P(GROUP, ROW), P(GROUP, None))
    return jax.shard_map(local, mesh=fine, in_specs=in_specs, out_specs=out_specs, check_vma=False)
```

time: 586 us -> 238 us (0.41)
  waiting for transfers between devices: 518 us -> 125 us
  matrix products: 36.6 us -> 0 us
  blocking collectives: 0 us -> 33.1 us
  Pallas kernels: 0 us -> 23.9 us
  starting transfers between devices: 0.11 us -> 21.4 us
  local copies, waits for them, and re-layouts: 0.29 us -> 16.3 us
  other arithmetic: 15.4 us -> 0.09 us
    all_gather x2 -> x1, waiting for transfers between devices: 409 us -> 0.02 us  [local(): anc = lax.all_gather(anc_inverse, GROUP, axis=1, tiled=True)]
    ppermute x0 -> x12, waiting for transfers between devices: none -> 125 us  [step(): return lax.ppermute(value, axis, [(i, (i + k) % n) for i in range(n)])]
    psum x1 -> x0, waiting for transfers between devices: 108 us -> none  [local(): summed = lax.psum(update.reshape(local_rows, SW), 'row')]
    dot_general x2 -> x0, matrix products: 36.6 us -> none  [the longest x1 31.5 us: local(): lax.dot_general(masked, anc_rows, (((1,), (1,)), ((), ())), precision=hig...]
    all_to_all x0 -> x2, blocking collectives: none -> 33.1 us  [swap(): return lax.all_to_all(value, ROW, 0, 0, tiled=True)]
    pallas_call x0 -> x7, Pallas kernels: none -> 23.9 us  [the longest x2 7.47 us: local(): pl.pallas_call(functools.partial(last_kernel, child), grid=(1,), out_shap...]
    ppermute x0 -> x12, starting transfers between devices: none -> 21.4 us  [step(): return lax.ppermute(value, axis, [(i, (i + k) % n) for i in range(n)])]
    mul x3 -> x0, other arithmetic: 15.3 us -> none  [the longest x1 12 us: mask_rows(): values.reshape(slot_count, SW, amount)]
  transfers between devices with their start and end apart: 3 -> 13, of which waited for: 3 -> 3; matrix products, arithmetic and copies ran while one was open for 2% -> 1% of each run, Pallas kernels for 0% -> 8%
where the time goes in v4:
time: 238 us; the launch traced here: 234 us
  waiting for transfers between devices  125 us (53%)
  blocking collectives  33.1 us (14%)
  Pallas kernels  23.9 us (10%)
  starting transfers between devices  21.4 us (9%)
  local copies, waits for them, and re-layouts  16.3 us (7%)
  between operations  14.2 us (6%)
    ppermute x12, waiting for transfers between devices, step(): return lax.ppermute(value, axis, [(i, (i + k) % n) for i in range(n)])  125 us
    all_to_all x2, blocking collectives, swap(): return lax.all_to_all(value, ROW, 0, 0, tiled=True)  33.1 us
    ppermute x12, starting transfers between devices, step(): return lax.ppermute(value, axis, [(i, (i + k) % n) for i in range(n)])  21.4 us
    unnamed x35, local copies, waits for them, and re-layouts  13.6 us
    pallas_call x2, Pallas kernels, local(): pl.pallas_call(functools.partial(last_kernel, child), grid=(1,), out_shap...  7.47 us
    pallas_call x1, Pallas kernels, local(): call(first_kernel, total, [SMEM] + [VMEM] * 6)  7.41 us
    pallas_call x1, Pallas kernels, local(): call(second_kernel, (total, piece, piece), [SMEM] + [VMEM] * 6)  6.02 us
  transfers between devices with their start and end apart: 13, of which 3 were waited for; matrix products, arithmetic and copies ran while one was open for 1% of the time, Pallas kernels for 8%

profile of v4, /device:TPU:6, one launch (start us, length us, event | category | flops | bytes accessed | tf_op | source)
XLA Modules:
  0.0 234.3 jit_solution(8330067277475472714)
XLA Ops:
  7.9 2.0 collective-permute-start.2
  9.9 3.0 %collective-permute-start.1 = (f32[1024,512]{1,0:T(8,128)}, f32[1024,512]{1,0:T(8,128)S(1)}, u32[]{:S(2)}, u32[]{:S(2)}) collective-permute-start(f32[1024,512]{1,0:T(8,128)} %panel.3), channel_id=1, source_target_pairs={{0,96},{32,0},{64,32},{96,64},{1,97},{33,1},{65,33},{97,65},{2,98}... | collective-permute-start | bytes 6291464 | tf_op jit(solution)/shard_map/ppermute | solution.py:44
  13.0 67.6 %collective-permute-done.2.refs_3_ = f32[1024,512]{1,0:T(8,128)S(1)} collective-permute-done((f32[1024,512]{1,0:T(8,128)}, f32[1024,512]{1,0:T(8,128)S(1)}, u32[]{:S(2)}, u32[]{:S(2)}) %collective-permute-start.2) | collective-permute-done | bytes 2097184 | tf_op jit(solution)/shard_map/ppermute | solution.py:44
  80.6 1.3 copy-done.11
  81.9 1.8 collective-permute-start.5
  83.7 2.5 %collective-permute-start.3 = (f32[1024,512]{1,0:T(8,128)S(1)}, f32[1024,512]{1,0:T(8,128)S(1)}, u32[]{:S(2)}, u32[]{:S(2)}) collective-permute-start(f32[1024,512]{1,0:T(8,128)S(1)} %collective-permute-done.refs_1_), channel_id=1, source_target_pairs={{0,16},{16,0},{1,17},{17,1},{2,18},{18,2},{3,19},{19,3},{4,20},{20... | collective-permute-start | bytes 6291464 | tf_op jit(solution)/shard_map/ppermute | solution.py:44
  86.2 1.3 copy-done.13
  87.6 1.6 collective-permute-start.4
  89.2 1.4 copy-done.9
  90.6 33.3 %collective-permute-done.5.refs_2_ = f32[1024,512]{1,0:T(8,128)S(1)} collective-permute-done((f32[1024,512]{1,0:T(8,128)S(1)}, f32[1024,512]{1,0:T(8,128)S(1)}, u32[]{:S(2)}, u32[]{:S(2)}) %collective-permute-start.5) | collective-permute-done | bytes 2097184 | tf_op jit(solution)/shard_map/ppermute | solution.py:44
  123.9 23.6 %collective-permute-done.3.refs_0_ = f32[1024,512]{1,0:T(8,128)S(1)} collective-permute-done((f32[1024,512]{1,0:T(8,128)S(1)}, f32[1024,512]{1,0:T(8,128)S(1)}, u32[]{:S(2)}, u32[]{:S(2)}) %collective-permute-start.3) | collective-permute-done | bytes 2097184 | tf_op jit(solution)/shard_map/ppermute | solution.py:44
  147.5 0.9 fusion
  148.3 0.9 fusion.2
  149.3 1.6 collective-permute-start.9
  150.8 1.6 collective-permute-start.6
  152.4 0.9 fusion.1
  153.3 1.3 copy-done.6
  154.6 1.7 collective-permute-start.10
  156.3 2.0 collective-permute-start.8
  158.3 3.5 %collective-permute-start.7 = (f32[160,512]{1,0:T(8,128)}, f32[160,512]{1,0:T(8,128)}, u32[]{:S(2)}, u32[]{:S(2)}) collective-permute-start(f32[160,512]{1,0:T(8,128)} %get-tuple-element.31), channel_id=1, source_target_pairs={{0,96},{32,0},{64,32},{96,64},{1,97},{33,1},{65,33},{97,65},{2,98}... | collective-permute-start | bytes 983048 | tf_op jit(solution)/shard_map/ppermute | solution.py:44
  162.0 1.3 shard_map.68.refs_4_.refs_3_.meta
  163.3 3.4 %copy-done = f32[512,4096]{1,0:T(8,128)S(1)} copy-done((f32[512,4096]{1,0:T(8,128)S(1)}, f32[512,4096]{1,0:T(8,128)}, u32[]{:S(2)}) %copy-start) | copy-done | bytes 8388632
  166.7 1.6 copy-done.10
  168.3 1.6 copy-done.12
  169.9 1.6 copy-done.14
  171.5 7.4 %shard_map.69.total = f32[1024,512]{1,0:T(8,128)S(1)} custom-call(s32[5]{0:T(128)S(1)} %stack.23.ids, f32[512,4096]{1,0:T(8,128)S(1)} %copy-done, f32[1024,512]{1,0:T(8,128)S(1)} %copy-done.1, f32[1024,512]{1,0:T(8,128)S(1)} %copy-done.14, f32[1024,512]{1,0:T(8,128)S(1)} %copy-done.12, f32[1024,512]{1,0:T(8,128)S(1)} %copy-done.10, ...), custom_call_target="tpu_custom_call" | custom-call | flops 1024 | bytes 1024 | tf_op jit(solution)/shard_map/pallas_call | solution.py:178
  178.9 6.0 %shard_map.70 = (f32[1024,512]{1,0:T(8,128)S(1)}, bf16[512,512]{1,0:T(8,128)(2,1)S(1)}, bf16[512,512]{1,0:T(8,128)(2,1)S(1)}) custom-call(s32[5]{0:T(128)S(1)} %stack.23.ids, f32[512,4096]{1,0:T(8,128)S(1)} %copy-done, f32[1024,512]{1,0:T(8,128)S(1)} %shard_map.69.total, f32[1024,512]{1,0:T(8,128)S(1)} %copy-done.3, f32[1024,512]{1,0:T(8,128)S(1)} %copy-done.7, ...), custom_call_target="tpu_custom_call" | custom-call | flops 1024 | bytes 1024 | tf_op jit(solution)/shard_map/pallas_call | solution.py:180
  185.0 3.6 %shard_map.71 = (f32[1024,512]{1,0:T(8,128)}, f32[1280,128]{1,0:T(8,128)S(1)}) custom-call(f32[1024,512]{1,0:T(8,128)S(1)} %get-tuple-element.21.total, f32[192,512]{1,0:T(8,128)S(1)} %collective-permute-done.9.one, f32[160,512]{1,0:T(8,128)} %collective-permute-done.10.two, f32[160,512]{1,0:T(8,128)S(1)} %collective-permute-done.11.three, ...), custom_call_target="tpu_custom_call" | custom-call | flops 1024 | bytes 1024 | tf_op jit(solution)/shard_map/pallas_call | solution.py:186
  188.6 3.9 %shard_map.72 = (f32[1024,512]{1,0:T(8,128)}, f32[1280,128]{1,0:T(8,128)S(1)}) custom-call(f32[1024,512]{1,0:T(8,128)S(1)} %get-tuple-element.21.total, f32[192,512]{1,0:T(8,128)S(1)} %collective-permute-done.6.one, f32[160,512]{1,0:T(8,128)} %collective-permute-done.7.two, ...), custom_call_target="tpu_custom_call", output_to_operand_aliasing={{0}: (8, {})} | custom-call | flops 1024 | bytes 1024 | tf_op jit(solution)/shard_map/pallas_call | solution.py:186
  192.6 16.9 %all_to_all.10.parts = f32[8,320,128]{2,1,0:T(8,128)S(1)} all-to-all(f32[8,320,128]{2,1,0:T(8,128)S(1)} %bitcast.8), channel_id=1, replica_groups=mesh['core'=2,'y'=4,'zl'=2,'zh'=4,'x'=4] {'y','zl'}, dimensions={0} | all-to-all | bytes 2621440 | tf_op jit(solution)/shard_map/all_to_all | solution.py:199
  209.6 16.2 %all_to_all.11 = f32[8,320,128]{2,1,0:T(8,128)S(1)} all-to-all(f32[8,320,128]{2,1,0:T(8,128)S(1)} %shard_map.73), channel_id=1, replica_groups=mesh['core'=2,'y'=4,'zl'=2,'zh'=4,'x'=4] {'y','zl'}, dimensions={0} | all-to-all | bytes 2621440 | tf_op jit(solution)/shard_map/all_to_all | solution.py:199
  225.8 1.6 shard_map.74
  (44 shorter events, 1.2 us)
Async XLA Ops:
  7.2 156.1 %all-gather.2.cloned.1.call-start = ((), (), s32[]{:S(2)}) async-start(), calls=%async_computation.2 | async-start | bytes 8650752 | tf_op jit(solution)/shard_map/all_gather | solution.py:162
  7.9 153.9 %copy-start.16 = (s32[64,32]{0,1:T(8,128)S(1)}, s32[64,32]{0,1:T(8,128)}, u32[]{:S(2)}) copy-start(s32[64,32]{0,1:T(8,128)} %param.9) | copy-start | bytes 24580
  7.9 154.1 %copy-start.15 = (s32[64]{0:T(128)S(1)}, s32[64]{0:T(128)}, u32[]{:S(2)}) copy-start(s32[64]{0:T(128)} %widths.1) | copy-start | bytes 772
  7.9 155.4 %copy-start.1 = (f32[1024,512]{1,0:T(8,128)S(1)}, f32[1024,512]{1,0:T(8,128)}, u32[]{:S(2)}) copy-start(f32[1024,512]{1,0:T(8,128)} %panel.3) | copy-start | bytes 6291460
  7.9 72.7 %collective-permute-start.2 = (f32[1024,512]{1,0:T(8,128)}, f32[1024,512]{1,0:T(8,128)S(1)}, u32[]{:S(2)}, u32[]{:S(2)}) collective-permute-start(f32[1024,512]{1,0:T(8,128)} %panel.3), channel_id=1, source_target_pairs={{0,16},{16,0},{1,17},{17,1},{2,18},{18,2},{3,19},{19,3},{4,20},{20... | collective-permute-start | bytes 6291464 | tf_op jit(solution)/shard_map/ppermute | solution.py:44
  9.9 70.7 %collective-permute-start.1 = (f32[1024,512]{1,0:T(8,128)}, f32[1024,512]{1,0:T(8,128)S(1)}, u32[]{:S(2)}, u32[]{:S(2)}) collective-permute-start(f32[1024,512]{1,0:T(8,128)} %panel.3), channel_id=1, source_target_pairs={{0,96},{32,0},{64,32},{96,64},{1,97},{33,1},{65,33},{97,65},{2,98}... | collective-permute-start | bytes 6291464 | tf_op jit(solution)/shard_map/ppermute | solution.py:44
  12.9 69.0 %collective-permute-start = (f32[1024,512]{1,0:T(8,128)}, f32[1024,512]{1,0:T(8,128)S(1)}, u32[]{:S(2)}, u32[]{:S(2)}) collective-permute-start(f32[1024,512]{1,0:T(8,128)} %panel.3), channel_id=1, source_target_pairs={{0,32},{32,64},{64,96},{96,0},{1,33},{33,65},{65,97},{97,1},{2,34}... | collective-permute-start | bytes 6291464 | tf_op jit(solution)/shard_map/ppermute | solution.py:44
  80.6 1.3 copy-start.11
  81.9 42.0 %collective-permute-start.5 = (f32[1024,512]{1,0:T(8,128)S(1)}, f32[1024,512]{1,0:T(8,128)S(1)}, u32[]{:S(2)}, u32[]{:S(2)}) collective-permute-start(f32[1024,512]{1,0:T(8,128)S(1)} %collective-permute-done.refs_1_), channel_id=1, source_target_pairs={{0,32},{32,64},{64,96},{96,0},{1,33},{33,65},{65,97},{97,1},{2,34}... | collective-permute-start | bytes 6291464 | tf_op jit(solution)/shard_map/ppermute | solution.py:44
  83.7 63.7 %collective-permute-start.3 = (f32[1024,512]{1,0:T(8,128)S(1)}, f32[1024,512]{1,0:T(8,128)S(1)}, u32[]{:S(2)}, u32[]{:S(2)}) collective-permute-start(f32[1024,512]{1,0:T(8,128)S(1)} %collective-permute-done.refs_1_), channel_id=1, source_target_pairs={{0,16},{16,0},{1,17},{17,1},{2,18},{18,2},{3,19},{19,3},{4,20},{20... | collective-permute-start | bytes 6291464 | tf_op jit(solution)/shard_map/ppermute | solution.py:44
  86.2 1.3 copy-start.13
  87.6 59.9 %collective-permute-start.4 = (f32[1024,512]{1,0:T(8,128)S(1)}, f32[1024,512]{1,0:T(8,128)S(1)}, u32[]{:S(2)}, u32[]{:S(2)}) collective-permute-start(f32[1024,512]{1,0:T(8,128)S(1)} %collective-permute-done.2.refs_3_), channel_id=1, source_target_pairs={{0,96},{32,0},{64,32},{96,64},{1,97},{33,1},{65,33},{97,65},{2,98}... | collective-permute-start | bytes 6291464 | tf_op jit(solution)/shard_map/ppermute | solution.py:44
  89.2 1.4 copy-start.9
  123.9 29.4 %copy-start.4 = (f32[1024,512]{1,0:T(8,128)}, f32[1024,512]{1,0:T(8,128)S(1)}, u32[]{:S(2)}) copy-start(f32[1024,512]{1,0:T(8,128)S(1)} %collective-permute-done.5.refs_2_) | copy-start | bytes 6291460
  147.5 5.9 %copy-start.2 = (f32[1024,512]{1,0:T(8,128)}, f32[1024,512]{1,0:T(8,128)S(1)}, u32[]{:S(2)}) copy-start(f32[1024,512]{1,0:T(8,128)S(1)} %collective-permute-done.3.refs_0_) | copy-start | bytes 6291460
  148.3 10.0 %collective-permute-start.11 = (f32[160,512]{1,0:T(8,128)S(1)}, f32[160,512]{1,0:T(8,128)S(1)}, u32[]{:S(2)}, u32[]{:S(2)}) collective-permute-start(f32[160,512]{1,0:T(8,128)S(1)} %get-tuple-element.28), channel_id=1, source_target_pairs={{0,16},{16,0},{1,17},{17,1},{2,18},{18,2},{3,19},{19,3},{4,20},{20... | collective-permute-start | bytes 983048 | tf_op jit(solution)/shard_map/ppermute | solution.py:44
  149.3 35.7 %collective-permute-start.9 = (f32[192,512]{1,0:T(8,128)}, f32[192,512]{1,0:T(8,128)S(1)}, u32[]{:S(2)}, u32[]{:S(2)}) collective-permute-start(f32[192,512]{1,0:T(8,128)} %get-tuple-element.32), channel_id=1, source_target_pairs={{0,32},{32,64},{64,96},{96,0},{1,33},{33,65},{65,97},{97,1},{2,34}... | collective-permute-start | bytes 1179656 | tf_op jit(solution)/shard_map/ppermute | solution.py:44
  150.8 37.7 %collective-permute-start.6 = (f32[192,512]{1,0:T(8,128)}, f32[192,512]{1,0:T(8,128)S(1)}, u32[]{:S(2)}, u32[]{:S(2)}) collective-permute-start(f32[192,512]{1,0:T(8,128)} %get-tuple-element.33), channel_id=1, source_target_pairs={{0,32},{32,64},{64,96},{96,0},{1,33},{33,65},{65,97},{97,1},{2,34}... | collective-permute-start | bytes 1179656 | tf_op jit(solution)/shard_map/ppermute | solution.py:44
  153.3 1.3 copy-start.6
  154.6 30.3 %collective-permute-start.10 = (f32[160,512]{1,0:T(8,128)}, f32[160,512]{1,0:T(8,128)}, u32[]{:S(2)}, u32[]{:S(2)}) collective-permute-start(f32[160,512]{1,0:T(8,128)} %get-tuple-element.30), channel_id=1, source_target_pairs={{0,96},{32,0},{64,32},{96,64},{1,97},{33,1},{65,33},{97,65},{2,98}... | collective-permute-start | bytes 983048 | tf_op jit(solution)/shard_map/ppermute | solution.py:44
  156.3 32.3 %collective-permute-start.8 = (f32[160,512]{1,0:T(8,128)}, f32[160,512]{1,0:T(8,128)}, u32[]{:S(2)}, u32[]{:S(2)}) collective-permute-start(f32[160,512]{1,0:T(8,128)} %get-tuple-element.29), channel_id=1, source_target_pairs={{0,16},{16,0},{1,17},{17,1},{2,18},{18,2},{3,19},{19,3},{4,20},{20... | collective-permute-start | bytes 983048 | tf_op jit(solution)/shard_map/ppermute | solution.py:44
  158.3 30.2 %collective-permute-start.7 = (f32[160,512]{1,0:T(8,128)}, f32[160,512]{1,0:T(8,128)}, u32[]{:S(2)}, u32[]{:S(2)}) collective-permute-start(f32[160,512]{1,0:T(8,128)} %get-tuple-element.31), channel_id=1, source_target_pairs={{0,96},{32,0},{64,32},{96,64},{1,97},{33,1},{65,33},{97,65},{2,98}... | collective-permute-start | bytes 983048 | tf_op jit(solution)/shard_map/ppermute | solution.py:44
  163.3 3.4 %copy-start = (f32[512,4096]{1,0:T(8,128)S(1)}, f32[512,4096]{1,0:T(8,128)}, u32[]{:S(2)}) copy-start(f32[512,4096]{1,0:T(8,128)} %all-gather.2.cloned.1.call-done.anc) | copy-start | bytes 25165828
  166.7 1.6 copy-start.10
  168.3 1.6 copy-start.12
  169.9 1.6 copy-start.14
  171.5 7.4 %copy-start.3 = (f32[1024,512]{1,0:T(8,128)S(1)}, f32[1024,512]{1,0:T(8,128)}, u32[]{:S(2)}) copy-start(f32[1024,512]{1,0:T(8,128)} %copy-done.2) | copy-start | bytes 6291460
  171.5 7.4 %copy-start.5 = (f32[1024,512]{1,0:T(8,128)S(1)}, f32[1024,512]{1,0:T(8,128)}, u32[]{:S(2)}) copy-start(f32[1024,512]{1,0:T(8,128)} %copy-done.4) | copy-start | bytes 6291460
  171.5 7.4 %copy-start.7 = (f32[1024,512]{1,0:T(8,128)S(1)}, f32[1024,512]{1,0:T(8,128)}, u32[]{:S(2)}) copy-start(f32[1024,512]{1,0:T(8,128)} %copy-done.6) | copy-start | bytes 6291460
  209.4 16.3 %copy-start.8 = (f32[1024,512]{1,0:T(8,128)S(1)}, f32[1024,512]{1,0:T(8,128)}, u32[]{:S(2)}) copy-start(f32[1024,512]{1,0:T(8,128)} %diag.1) | copy-start | bytes 6291460
Sparse Core Ops, SparseCore 0:
  10.5 109.5 all-gather.1

commit v5 on v4

v5 whole, which is shorter than its diff:
```python
import functools

import jax
import jax.numpy as jnp
from jax import lax
from jax.experimental import pallas as pl
from jax.experimental.pallas import tpu as pltpu
from jax.sharding import Mesh, PartitionSpec as P

B = 128
SW = 512
WIDE = 2048
LIMIT = 22 * 2**20
ROW = ("y", "zl")
Z = ("zl", "zh")
DIRECTIONS = (0, 3, 1, 2)

VMEM = pl.BlockSpec(memory_space=pltpu.VMEM)
SMEM = pl.BlockSpec(memory_space=pltpu.SMEM)
F32 = jnp.float32
BF16 = jnp.bfloat16


def call(kernel, out_shape, specs, out_specs=None, scratch=(), aliases=None):
    single = not isinstance(out_shape, (tuple, list))
    return pl.pallas_call(
        kernel,
        out_shape=out_shape,
        in_specs=specs,
        out_specs=out_specs if out_specs is not None else (VMEM if single else [VMEM] * len(out_shape)),
        scratch_shapes=list(scratch),
        input_output_aliases=aliases or {},
        compiler_params=pltpu.CompilerParams(vmem_limit_bytes=LIMIT),
        cost_estimate=pl.CostEstimate(flops=1024, bytes_accessed=1024, transcendentals=0),
    )


def struct(shape, dtype=F32):
    return jax.ShapeDtypeStruct(shape, dtype)


def z_rounds():
    even = [
        {0: 0, 2: 1, 4: 4, 6: 5},
        {6: 0, 0: 1, 2: 4, 4: 5},
        {2: 0, 4: 1, 6: 4, 0: 5},
        {4: 0, 6: 1, 0: 4, 2: 5},
    ]
    rounds = []
    table = {}
    for k, pairs in enumerate(even):
        pairs = {**pairs, **{(3 - t) % 8: (3 - s) % 8 for t, s in pairs.items()}}
        rounds.append([((s % 2) * 4 + s // 2, (t % 2) * 4 + t // 2) for t, s in pairs.items()])
        for t, s in pairs.items():
            table[t, int(s % 2 == t % 2), (s // 2) // 2] = k
    return rounds, table


def step(value, axis, k, n=4):
    return lax.ppermute(value, axis, [(i, (i + k) % n) for i in range(n)])


def split(value):
    high = value.astype(BF16)
    return high, (value - high.astype(F32)).astype(BF16)


def dot3(a, b):
    dims = (((1,), (1,)), ((), ()))
    mul = functools.partial(lax.dot_general, dimension_numbers=dims, preferred_element_type=F32)
    return mul(a[0], b[0]) + (mul(a[0], b[1]) + mul(a[1], b[0]))


def meta_kernel(ids, widths, pattern, out):
    core, y, zl, zh, x = (ids[i] for i in range(5))
    first = ((core * 4 + zh) * 4 + x) * 2
    for child in range(2):
        for d, shift in enumerate(DIRECTIONS):
            block = ((y + shift) % 4 * 2 + zl) * 4
            for k in range(4):
                value = pattern[first + child, block + k].astype(F32)
                out[child : child + 1, (d * 4 + k) * B : (d * 4 + k + 1) * B] = jnp.full((1, B), value)
        out[2 + child : 3 + child, :] = jnp.full((1, WIDE), (widths[first + child] * B).astype(F32))
    out[4:8, :] = jnp.zeros((4, WIDE), F32)


def column_mask(meta, child):
    position = lax.broadcasted_iota(jnp.int32, (SW, B), 0).astype(F32)
    return (position < meta[2 + child : 3 + child, :B]).astype(F32)


def place_of(table, ids, role, half):
    z = ids[3] * 2 + ids[2]
    places = [jnp.int32(0)] * 2
    for k in range(2):
        for at in range(8):
            places[k] = jnp.where(z == at, table[at, role, k], places[k])
    return jnp.where(half == 0, *places)


def each_block(table, ids, role, body):
    @pl.loop(0, 4)
    def _(d):
        block = (ids[1] + jnp.where(d == 0, 0, jnp.where(d == 1, 3, jnp.where(d == 2, 1, 2)))) % 4
        body(d, block // 2 == ids[0], place_of(table, ids, role, block % 2))


def near_kernel(table, ids, *refs):
    for role in range(2):
        high, low = refs[6 + 2 * role : 8 + 2 * role]

        def body(d, here, place):
            for a in range(3):
                lanes = pl.ds(pl.multiple_of((a * 4 + d) * B, B), B)
                for when, ref in ((here, refs[a]), (jnp.logical_not(here), refs[3 + a])):

                    @pl.when(when)
                    def _():
                        high[:, lanes], low[:, lanes] = split(ref[place])

        each_block(table, ids, role, body)


def far_kernel(table, role, ids, *refs):
    high, low = refs[4:]

    def body(d, here, place):
        lanes = pl.ds(pl.multiple_of(d * B, B), B)
        for core, when in ((0, here), (1, jnp.logical_not(here))):
            for side, where in ((0, place < 2), (1, place >= 2)):

                @pl.when(when & where)
                def _():
                    high[:, lanes], low[:, lanes] = split(refs[2 * core + side][place % 2])

    each_block(table, ids, role, body)


def product_kernel(child, ids, own, left, right, top, bottom, *refs):
    high, low, far_high, far_low, meta, out, phigh, plow = refs
    mask = column_mask(meta, child)
    rows = slice(child * SW, (child + 1) * SW)
    for a, away in enumerate((0, 3, 1, 2)):
        k = (ids[4] + away) % 4
        for d, source in enumerate((own, left, right, None)):
            here = pl.ds(pl.multiple_of(k * B, B), B)
            across = pl.ds(pl.multiple_of((d * 4 + k) * B, B), B)
            lanes = slice((a * 4 + d) * B, (a * 4 + d + 1) * B)
            if source is None:
                value = jnp.concatenate([top[:, here], bottom[:, here]], axis=0)
            else:
                value = source[rows, here]
            phigh[:, lanes], plow[:, lanes] = split(value * mask * meta[child : child + 1, across])
    near = 12 * B
    for n in range(0, SW, 256):
        lines = slice(n, n + 256)
        for r in range(0, SW, 256):
            at = slice(r, r + 256)
            value = dot3((phigh[at, :near], plow[at, :near]), (high[lines, :], low[lines, :]))
            value += dot3((phigh[at, near:], plow[at, near:]), (far_high[lines, :], far_low[lines, :]))
            out[at, lines] = value


def lower_blocks(update, left, right):
    at = 0
    for a in range(4):
        value = dot3([v[a * B : (a + 1) * B] for v in left], [v[: (a + 1) * B] for v in right])
        for b in range(a + 1):
            update[at * B : (at + 1) * B, :] = value[:, b * B : (b + 1) * B]
            at += 1


def finish_kernel(child, mine, received, panel, meta, *refs):
    off, update = refs[-2:]
    wide = jnp.concatenate([column_mask(meta, child)] * 4, axis=1)
    masks = wide * meta[child : child + 1, :SW]
    product = (mine[...] + received[...]) * masks
    off[...] = -product
    lower_blocks(update, split(product), split(panel[...] * masks))


def sum_kernel(parts, out):
    total = parts[0]
    for k in range(1, 8):
        total += parts[k]
    for k in range(8):
        out[k] = total


def child_kernel(parts, diag, meta, out):
    at = 0
    for child in range(2):
        across = lax.broadcasted_iota(jnp.int32, (1, SW), 1).astype(F32) < meta[2 + child : 3 + child, :SW]
        across = across.astype(F32)
        mask = column_mask(meta, child)
        for a in range(4):
            for b in range(a + 1):
                block = parts[at]
                at += 1
                for (i, j), value in {(b, a): block.T, (a, b): block}.items():
                    lines = slice(child * SW + i * B, child * SW + (i + 1) * B)
                    lanes = slice(j * B, (j + 1) * B)
                    rows = mask[i * B : (i + 1) * B]
                    out[lines, lanes] = (diag[lines, lanes] + value) * rows * across[:, lanes]


def after(value, *before):
    return lax.optimization_barrier((value, *before))[0]


def local(anc_inverse, panel, diag_inverse, widths, pattern):
    names = ("core", "y", "zl", "zh", "x")
    ids = jnp.stack([lax.axis_index(n) for n in names]).astype(jnp.int32)
    left, right = step(panel, "y", 1), step(panel, "y", -1)
    half = SW // 2
    far = [(step(left[a : a + half], "y", 1), step(right[a + half : a + SW], "y", -1)) for a in (0, SW)]

    rounds, table = z_rounds()
    held = jnp.stack([lax.ppermute(anc_inverse, Z, pairs) for pairs in rounds])
    before, beyond = step(held, "x", 1), step(held, "x", -1)
    near = [held, before, beyond]
    near += [step(value, "core", 1, 2) for value in near]
    ends = step(after(before[:2], *far[0]), "x", 1), step(after(beyond[2:], *far[0]), "x", -1)
    meta = call(meta_kernel, struct((8, WIDE)), [SMEM] * 3)(ids, widths, pattern)
    parts = call(
        functools.partial(near_kernel, table), [struct((SW, 12 * B), BF16)] * 4, [SMEM] + [VMEM] * 6
    )(ids, *near)
    ends = tuple(after(value, parts[0]) for value in ends)
    ends += tuple(step(value, "core", 1, 2) for value in ends)

    def product(role, first):
        pair = [struct((SW, SW), BF16)] * 2
        anc = call(functools.partial(far_kernel, table, role), pair, [SMEM] + [VMEM] * 4)(ids, first, *ends[1:])
        anc = (*parts[2 * role : 2 * role + 2], *anc)
        values = []
        for child in range(2):
            values.append(
                call(
                    functools.partial(product_kernel, child),
                    struct((SW, SW)),
                    [SMEM] + [VMEM] * 10,
                    scratch=[pltpu.VMEM((SW, WIDE), BF16)] * 2,
                )(ids, after(panel, *values) if values else panel, left, right, *far[child], *anc, meta)
            )
        return values

    sent = product(0, ends[0])
    received = [step(value, "zl", 1, 2) for value in sent]
    mine = product(1, after(ends[0], sent[1]))

    off, updates = None, []
    for child in range(2):
        block = pl.BlockSpec((SW, SW), lambda g, child=child: (child, 0))
        off, update = pl.pallas_call(
            functools.partial(finish_kernel, child),
            grid=(1,),
            out_shape=(struct(panel.shape), struct((10 * B, B))),
            in_specs=[VMEM, VMEM, block, VMEM] + [pl.BlockSpec(memory_space=pl.ANY)] * child,
            out_specs=[block, VMEM],
            input_output_aliases={4: 0} if child else {},
            compiler_params=pltpu.CompilerParams(vmem_limit_bytes=LIMIT),
            cost_estimate=pl.CostEstimate(flops=1024, bytes_accessed=1024, transcendentals=0),
        )(mine[child], received[child], panel, meta, *([off] if child else []))
        updates.append(update)

    def swap(value):
        return lax.all_to_all(value, ROW, 0, 0, tiled=True)

    shape = (8, 20 * B // 8, B)
    spread = swap(jnp.concatenate(updates, axis=0).reshape(shape))
    summed = swap(call(sum_kernel, struct(shape), [VMEM])(spread)).reshape(20, B, B)
    out = call(child_kernel, struct(diag_inverse.shape), [VMEM] * 3)(summed, diag_inverse, meta)
    return off, out


def solution(mesh):
    fine = Mesh(mesh.devices.reshape(2, 4, 2, 4, 4), ("core", "y", "zl", "zh", "x"))
    group = ("core", "zh", "x")
    in_specs = (P(ROW, group), P(group, ROW), P(group, None), P(), P())
    out_specs = (P(group, ROW), P(group, None))
    return jax.shard_map(local, mesh=fine, in_specs=in_specs, out_specs=out_specs, check_vma=False)
```

time: 238 us -> 195 us (0.82); the launches traced: 234 us -> 195 us
  waiting for transfers between devices: 125 us -> 74.3 us
  between operations: 14.2 us -> 0.91 us
  Pallas kernels: 23.9 us -> 33.8 us
  blocking collectives: 33.1 us -> 41.3 us
  starting transfers between devices: 21.4 us -> 26.3 us
    ppermute x12 -> x17, waiting for transfers between devices: 125 us -> 41.8 us  [step(): return lax.ppermute(value, axis, [(i, (i + k) % n) for i in range(n)])]
    ppermute x0 -> x4, waiting for transfers between devices: none -> 32.4 us  [local(): held = jnp.stack([lax.ppermute(anc_inverse, Z, pairs) for pairs in rounds])]
    pallas_call x4 -> x9, Pallas kernels: 20.9 us -> 30.9 us  [the longest x4 20.6 us: product(): call(functools.partial(product_kernel, child), struct((SW, SW)), [SMEM] +...]
    ppermute x0 -> x4, starting transfers between devices: none -> 8.79 us  [local(): held = jnp.stack([lax.ppermute(anc_inverse, Z, pairs) for pairs in rounds])]
    all_to_all x2, blocking collectives: 33.1 us -> 41.3 us  [swap(): return lax.all_to_all(value, ROW, 0, 0, tiled=True)]
    ppermute x12 -> x17, starting transfers between devices: 21.4 us -> 17.5 us  [step(): return lax.ppermute(value, axis, [(i, (i + k) % n) for i in range(n)])]
    unnamed x35 -> x49, local copies, waits for them, and re-layouts: 13.6 us -> 14.4 us
  transfers between devices with their start and end apart: 13 -> 21, of which waited for: 3 -> 10; matrix products, arithmetic and copies ran while one was open for 1% -> 2% of each run, Pallas kernels for 8% -> 16%
where the time goes in v5:
time: 195 us
  waiting for transfers between devices  74.3 us (38%)
  blocking collectives  41.3 us (21%)
  Pallas kernels  33.8 us (17%)
  starting transfers between devices  26.3 us (13%)
  local copies, waits for them, and re-layouts  18.2 us (9%)
    ppermute x17, waiting for transfers between devices, step(): return lax.ppermute(value, axis, [(i, (i + k) % n) for i in range(n)])  41.8 us
    all_to_all x2, blocking collectives, swap(): return lax.all_to_all(value, ROW, 0, 0, tiled=True)  41.3 us
    ppermute x4, waiting for transfers between devices, local(): held = jnp.stack([lax.ppermute(anc_inverse, Z, pairs) for pairs in rounds])  32.4 us
    pallas_call x4, Pallas kernels, product(): call(functools.partial(product_kernel, child), struct((SW, SW)), [SMEM] +...  20.6 us
    ppermute x17, starting transfers between devices, step(): return lax.ppermute(value, axis, [(i, (i + k) % n) for i in range(n)])  17.5 us
    unnamed x49, local copies, waits for them, and re-layouts  14.4 us
    ppermute x4, starting transfers between devices, local(): held = jnp.stack([lax.ppermute(anc_inverse, Z, pairs) for pairs in rounds])  8.79 us
  transfers between devices with their start and end apart: 21, of which 10 were waited for; matrix products, arithmetic and copies ran while one was open for 2% of the time, Pallas kernels for 16%

profile of v5, /device:TPU:6, one launch (start us, length us, event | category | flops | bytes accessed | tf_op | source)
XLA Modules:
  0.0 194.8 jit_solution(6646068691205919841)
XLA Ops:
  0.6 3.1 %collective-permute-start.1 = (f32[1024,512]{1,0:T(8,128)}, f32[1024,512]{1,0:T(8,128)S(1)}, u32[]{:S(2)}, u32[]{:S(2)}) collective-permute-start(f32[1024,512]{1,0:T(8,128)} %panel.3), channel_id=1, source_target_pairs={{0,96},{32,0},{64,32},{96,64},{1,97},{33,1},{65,33},{97,65},{2,98}... | collective-permute-start | bytes 6291464 | tf_op jit(solution)/shard_map/ppermute | solution.py:60
  3.7 6.3 %collective-permute-start.5 = (f32[512,128]{1,0:T(8,128)}, f32[512,128]{1,0:T(8,128)S(1)}, u32[]{:S(2)}, u32[]{:S(2)}) collective-permute-start(f32[512,128]{1,0:T(8,128)} %param.5), channel_id=1, source_target_pairs={{0,12},{16,0},{8,4},{24,8},{20,24},{4,20},{28,16},{12,28},{1,13},{... | collective-permute-start | bytes 786440 | tf_op jit(solution)/shard_map/ppermute | solution.py:219
  10.0 1.6 collective-permute-start.4
  12.5 20.0 %collective-permute-done.5 = f32[512,128]{1,0:T(8,128)S(1)} collective-permute-done((f32[512,128]{1,0:T(8,128)}, f32[512,128]{1,0:T(8,128)S(1)}, u32[]{:S(2)}, u32[]{:S(2)}) %collective-permute-start.5) | collective-permute-done | bytes 262176 | tf_op jit(solution)/shard_map/ppermute | solution.py:219
  32.6 12.4 %collective-permute-done.6 = f32[512,128]{1,0:T(8,128)S(1)} collective-permute-done((f32[512,128]{1,0:T(8,128)}, f32[512,128]{1,0:T(8,128)S(1)}, u32[]{:S(2)}, u32[]{:S(2)}) %collective-permute-start.6) | collective-permute-done | bytes 262176 | tf_op jit(solution)/shard_map/ppermute | solution.py:219
  45.9 2.4 %collective-permute-start.8 = (f32[4,512,128]{2,1,0:T(8,128)S(1)}, f32[4,512,128]{2,1,0:T(8,128)S(1)}, u32[]{:S(2)}, u32[]{:S(2)}) collective-permute-start(f32[4,512,128]{2,1,0:T(8,128)S(1)} %pad_maximum_fusion.1.refs_0_), channel_id=1, source_target_pairs={{0,1},{1,2},{2,3},{3,0},{4,5},{5,6},{6,7},{7,4},{8,9},{9,10},{10,1... | collective-permute-start | bytes 3145736 | tf_op jit(solution)/shard_map/ppermute | solution.py:60
  49.9 3.6 %collective-permute-start.3 = (f32[256,512]{1,0:T(8,128)S(1)}, f32[256,512]{1,0:T(8,128)S(1)}, u32[]{:S(2)}, u32[]{:S(2)}) collective-permute-start(f32[256,512]{1,0:T(8,128)S(1)} %get-tuple-element.41), channel_id=1, source_target_pairs={{0,96},{32,0},{64,32},{96,64},{1,97},{33,1},{65,33},{97,65},{2,98}... | collective-permute-start | bytes 1572872 | tf_op jit(solution)/shard_map/ppermute | solution.py:60
  54.5 6.6 %collective-permute-done.9.refs_2_ = f32[4,512,128]{2,1,0:T(8,128)S(1)} collective-permute-done((f32[4,512,128]{2,1,0:T(8,128)S(1)}, f32[4,512,128]{2,1,0:T(8,128)S(1)}, u32[]{:S(2)}, u32[]{:S(2)}) %collective-permute-start.9) | collective-permute-done | bytes 1048608 | tf_op jit(solution)/shard_map/ppermute | solution.py:60
  62.5 1.7 collective-permute-done.3.bottom
  65.0 3.6 %collective-permute-done.2.top = f32[256,512]{1,0:T(8,128)S(1)} collective-permute-done((f32[256,512]{1,0:T(8,128)S(1)}, f32[256,512]{1,0:T(8,128)S(1)}, u32[]{:S(2)}, u32[]{:S(2)}) %collective-permute-start.2) | collective-permute-done | bytes 524320 | tf_op jit(solution)/shard_map/ppermute | solution.py:60
  70.3 1.9 collective-permute-start.14
  72.3 3.4 %shard_map.68 = (bf16[512,1536]{1,0:T(8,128)(2,1)S(1)}, bf16[512,1536]{1,0:T(8,128)(2,1)S(1)}, bf16[512,1536]{1,0:T(8,128)(2,1)S(1)}, bf16[512,1536]{1,0:T(8,128)(2,1)S(1)}) custom-call(s32[5]{0:T(128)S(1)} %stack.38.ids, f32[4,512,128]{2,1,0:T(8,128)S(1)} %pad_maximum_fusion.1.refs_0_, f32[4,512,128]{2,1,0:T(8,128)S(1)} %collective-permute-done.8.refs_1_, ...), custom_call_target="tpu_custom_call" | custom-call | flops 1024 | bytes 1024 | tf_op jit(solution)/shard_map/pallas_call | solution.py:225
  81.6 2.0 %collective-permute-done.14.refs_1_ = f32[2,512,128]{2,1,0:T(8,128)} collective-permute-done((f32[2,512,128]{2,1,0:T(8,128)}, f32[2,512,128]{2,1,0:T(8,128)}, u32[]{:S(2)}, u32[]{:S(2)}) %collective-permute-start.14) | collective-permute-done | bytes 524320 | tf_op jit(solution)/shard_map/ppermute | solution.py:60
  83.7 2.5 %collective-permute-start.18 = (f32[256,512]{1,0:T(8,128)}, f32[256,512]{1,0:T(8,128)S(1)}, u32[]{:S(2)}, u32[]{:S(2)}) collective-permute-start(f32[256,512]{1,0:T(8,128)} %get-tuple-element.40), channel_id=1, source_target_pairs={{0,96},{32,0},{64,32},{96,64},{1,97},{33,1},{65,33},{97,65},{2,98}... | collective-permute-start | bytes 1572872 | tf_op jit(solution)/shard_map/ppermute | solution.py:60
  87.5 1.8 shard_map.69
  89.2 1.6 copy-done.2
  90.8 1.6 copy-done.5
  92.4 1.4 copy-done.12
  93.8 1.4 copy-done.14
  97.3 4.9 %shard_map.71 = f32[512,512]{1,0:T(8,128)S(1)} custom-call(s32[5]{0:T(128)S(1)} %stack.38.ids, f32[1024,512]{1,0:T(8,128)S(1)} %copy-done, f32[1024,512]{1,0:T(8,128)S(1)} %copy-done.5, f32[1024,512]{1,0:T(8,128)S(1)} %copy-done.2, f32[256,512]{1,0:T(8,128)S(1)} %copy-done.19, f32[256,512]{1,0:T(8,128)S(1)} %copy-done.16, bf16[512,1536]{1,0:T(8,128)(2,1)S(1)} %copy-done.12, ...), custom_call_target="tpu_custom_call" | custom-call | flops 1024 | bytes 1024 | tf_op jit(solution)/shard_map/pallas_call | solution.py:238
  103.3 5.5 %shard_map.72 = f32[512,512]{1,0:T(8,128)S(1)} custom-call(s32[5]{0:T(128)S(1)} %stack.38.ids, f32[1024,512]{1,0:T(8,128)S(1)} %copy-done, f32[1024,512]{1,0:T(8,128)S(1)} %copy-done.5, f32[1024,512]{1,0:T(8,128)S(1)} %copy-done.2, f32[256,512]{1,0:T(8,128)} %collective-permute-done.17.top, f32[256,512]{1,0:T(8,128)S(1)} %collective-permute-done.18.bottom, ...), custom_call_target="tpu_custom_call" | custom-call | flops 1024 | bytes 1024 | tf_op jit(solution)/shard_map/pallas_call | solution.py:238
  108.8 1.4 collective-permute-start.19
  110.2 1.8 shard_map.73
  112.0 4.9 %shard_map.74.mine = f32[512,512]{1,0:T(8,128)S(1)} custom-call(s32[5]{0:T(128)S(1)} %stack.38.ids, f32[1024,512]{1,0:T(8,128)S(1)} %copy-done, f32[1024,512]{1,0:T(8,128)S(1)} %copy-done.6, f32[1024,512]{1,0:T(8,128)S(1)} %copy-done.3, f32[256,512]{1,0:T(8,128)S(1)} %copy-done.20, f32[256,512]{1,0:T(8,128)S(1)} %copy-done.17, ...), custom_call_target="tpu_custom_call" | custom-call | flops 1024 | bytes 1024 | tf_op jit(solution)/shard_map/pallas_call | solution.py:238
  116.9 5.4 %shard_map.75.mine = f32[512,512]{1,0:T(8,128)S(1)} custom-call(s32[5]{0:T(128)S(1)} %stack.38.ids, f32[1024,512]{1,0:T(8,128)S(1)} %copy-done, f32[1024,512]{1,0:T(8,128)S(1)} %copy-done.6, f32[1024,512]{1,0:T(8,128)S(1)} %copy-done.3, f32[256,512]{1,0:T(8,128)} %collective-permute-done.17.top, f32[256,512]{1,0:T(8,128)S(1)} %collective-permute-done.18.bottom, ...), custom_call_target="tpu_custom_call" | custom-call | flops 1024 | bytes 1024 | tf_op jit(solution)/shard_map/pallas_call | solution.py:238
  122.2 6.0 %collective-permute-done.20.received = f32[512,512]{1,0:T(8,128)S(1)} collective-permute-done((f32[512,512]{1,0:T(8,128)S(1)}, f32[512,512]{1,0:T(8,128)S(1)}, u32[]{:S(2)}, u32[]{:S(2)}) %collective-permute-start.20) | collective-permute-done | bytes 1048608 | tf_op jit(solution)/shard_map/ppermute | solution.py:60
  128.3 1.7 shard_map.76
  129.9 20.1 %collective-permute-done.19.received = f32[512,512]{1,0:T(8,128)S(1)} collective-permute-done((f32[512,512]{1,0:T(8,128)S(1)}, f32[512,512]{1,0:T(8,128)S(1)}, u32[]{:S(2)}, u32[]{:S(2)}) %collective-permute-start.19) | collective-permute-done | bytes 1048608 | tf_op jit(solution)/shard_map/ppermute | solution.py:60
  150.0 1.7 shard_map.77
  151.8 21.8 %all_to_all.10.parts = f32[8,320,128]{2,1,0:T(8,128)S(1)} all-to-all(f32[8,320,128]{2,1,0:T(8,128)S(1)} %bitcast.12), channel_id=1, replica_groups=mesh['core'=2,'y'=4,'zl'=2,'zh'=4,'x'=4] {'y','zl'}, dimensions={0} | all-to-all | bytes 2621440 | tf_op jit(solution)/shard_map/all_to_all | solution.py:267
  173.7 19.4 %all_to_all.11 = f32[8,320,128]{2,1,0:T(8,128)S(1)} all-to-all(f32[8,320,128]{2,1,0:T(8,128)S(1)} %shard_map.78), channel_id=1, replica_groups=mesh['core'=2,'y'=4,'zl'=2,'zh'=4,'x'=4] {'y','zl'}, dimensions={0} | all-to-all | bytes 2621440 | tf_op jit(solution)/shard_map/all_to_all | solution.py:267
  193.2 1.6 shard_map.79
  (80 shorter events, 19.0 us)
Async XLA Ops:
  0.6 48.3 %collective-permute-start.1 = (f32[1024,512]{1,0:T(8,128)}, f32[1024,512]{1,0:T(8,128)S(1)}, u32[]{:S(2)}, u32[]{:S(2)}) collective-permute-start(f32[1024,512]{1,0:T(8,128)} %panel.3), channel_id=1, source_target_pairs={{0,96},{32,0},{64,32},{96,64},{1,97},{33,1},{65,33},{97,65},{2,98}... | collective-permute-start | bytes 6291464 | tf_op jit(solution)/shard_map/ppermute | solution.py:60
  3.7 49.8 %collective-permute-start = (f32[1024,512]{1,0:T(8,128)}, f32[1024,512]{1,0:T(8,128)S(1)}, u32[]{:S(2)}, u32[]{:S(2)}) collective-permute-start(f32[1024,512]{1,0:T(8,128)} %panel.3), channel_id=1, source_target_pairs={{0,32},{32,64},{64,96},{96,0},{1,33},{33,65},{65,97},{97,1},{2,34}... | collective-permute-start | bytes 6291464 | tf_op jit(solution)/shard_map/ppermute | solution.py:60
  3.7 28.8 %collective-permute-start.5 = (f32[512,128]{1,0:T(8,128)}, f32[512,128]{1,0:T(8,128)S(1)}, u32[]{:S(2)}, u32[]{:S(2)}) collective-permute-start(f32[512,128]{1,0:T(8,128)} %param.5), channel_id=1, source_target_pairs={{0,12},{16,0},{8,4},{24,8},{20,24},{4,20},{28,16},{12,28},{1,13},{... | collective-permute-start | bytes 786440 | tf_op jit(solution)/shard_map/ppermute | solution.py:219
  10.0 22.5 %collective-permute-start.4 = (f32[512,128]{1,0:T(8,128)}, f32[512,128]{1,0:T(8,128)S(1)}, u32[]{:S(2)}, u32[]{:S(2)}) collective-permute-start(f32[512,128]{1,0:T(8,128)} %param.5), channel_id=1, source_target_pairs={{0,0},{16,4},{8,8},{24,12},{20,20},{4,16},{28,28},{12,24},{1,1},{1... | collective-permute-start | bytes 786440 | tf_op jit(solution)/shard_map/ppermute | solution.py:219
  11.6 20.9 %collective-permute-start.7 = (f32[512,128]{1,0:T(8,128)}, f32[512,128]{1,0:T(8,128)S(1)}, u32[]{:S(2)}, u32[]{:S(2)}) collective-permute-start(f32[512,128]{1,0:T(8,128)} %param.5), channel_id=1, source_target_pairs={{0,8},{16,12},{8,0},{24,4},{20,28},{4,24},{28,20},{12,16},{1,9},{1... | collective-permute-start | bytes 786440 | tf_op jit(solution)/shard_map/ppermute | solution.py:219
  32.6 12.4 %collective-permute-start.6 = (f32[512,128]{1,0:T(8,128)}, f32[512,128]{1,0:T(8,128)S(1)}, u32[]{:S(2)}, u32[]{:S(2)}) collective-permute-start(f32[512,128]{1,0:T(8,128)} %param.5), channel_id=1, source_target_pairs={{0,4},{16,8},{8,12},{24,0},{20,16},{4,28},{28,24},{12,20},{1,5},{1... | collective-permute-start | bytes 786440 | tf_op jit(solution)/shard_map/ppermute | solution.py:219
  45.0 16.1 %collective-permute-start.9 = (f32[4,512,128]{2,1,0:T(8,128)S(1)}, f32[4,512,128]{2,1,0:T(8,128)S(1)}, u32[]{:S(2)}, u32[]{:S(2)}) collective-permute-start(f32[4,512,128]{2,1,0:T(8,128)S(1)} %pad_maximum_fusion.1.refs_0_), channel_id=1, source_target_pairs={{0,3},{1,0},{2,1},{3,2},{4,7},{5,4},{6,5},{7,6},{8,11},{9,8},{10,9... | collective-permute-start | bytes 3145736 | tf_op jit(solution)/shard_map/ppermute | solution.py:60
  45.9 15.2 %collective-permute-start.8 = (f32[4,512,128]{2,1,0:T(8,128)S(1)}, f32[4,512,128]{2,1,0:T(8,128)S(1)}, u32[]{:S(2)}, u32[]{:S(2)}) collective-permute-start(f32[4,512,128]{2,1,0:T(8,128)S(1)} %pad_maximum_fusion.1.refs_0_), channel_id=1, source_target_pairs={{0,1},{1,2},{2,3},{3,0},{4,5},{5,6},{6,7},{7,4},{8,9},{9,10},{10,1... | collective-permute-start | bytes 3145736 | tf_op jit(solution)/shard_map/ppermute | solution.py:60
  48.3 24.0 %collective-permute-start.10 = (f32[4,512,128]{2,1,0:T(8,128)S(1)}, f32[4,512,128]{2,1,0:T(8,128)}, u32[]{:S(2)}, u32[]{:S(2)}) collective-permute-start(f32[4,512,128]{2,1,0:T(8,128)S(1)} %pad_maximum_fusion.1.refs_0_), channel_id=1, source_target_pairs={{0,128},{128,0},{1,129},{129,1},{2,130},{130,2},{3,131},{131,3},{4... | collective-permute-start | bytes 3145736 | tf_op jit(solution)/shard_map/ppermute | solution.py:60
  48.9 5.6 %copy-start.1 = (f32[1024,512]{1,0:T(8,128)}, f32[1024,512]{1,0:T(8,128)S(1)}, u32[]{:S(2)}) copy-start(f32[1024,512]{1,0:T(8,128)S(1)} %collective-permute-done.1.right) | copy-start | bytes 6291460
  49.9 14.2 %collective-permute-start.3 = (f32[256,512]{1,0:T(8,128)S(1)}, f32[256,512]{1,0:T(8,128)S(1)}, u32[]{:S(2)}, u32[]{:S(2)}) collective-permute-start(f32[256,512]{1,0:T(8,128)S(1)} %get-tuple-element.41), channel_id=1, source_target_pairs={{0,96},{32,0},{64,32},{96,64},{1,97},{33,1},{65,33},{97,65},{2,98}... | collective-permute-start | bytes 1572872 | tf_op jit(solution)/shard_map/ppermute | solution.py:60
  53.5 9.0 %copy-start.4 = (f32[1024,512]{1,0:T(8,128)}, f32[1024,512]{1,0:T(8,128)S(1)}, u32[]{:S(2)}) copy-start(f32[1024,512]{1,0:T(8,128)S(1)} %collective-permute-done.left) | copy-start | bytes 6291460
  54.5 14.1 %collective-permute-start.2 = (f32[256,512]{1,0:T(8,128)S(1)}, f32[256,512]{1,0:T(8,128)S(1)}, u32[]{:S(2)}, u32[]{:S(2)}) collective-permute-start(f32[256,512]{1,0:T(8,128)S(1)} %get-tuple-element.43), channel_id=1, source_target_pairs={{0,32},{32,64},{64,96},{96,0},{1,33},{33,65},{65,97},{97,1},{2,34}... | collective-permute-start | bytes 1572872 | tf_op jit(solution)/shard_map/ppermute | solution.py:60
  61.1 11.2 %collective-permute-start.12 = (f32[4,512,128]{2,1,0:T(8,128)S(1)}, f32[4,512,128]{2,1,0:T(8,128)}, u32[]{:S(2)}, u32[]{:S(2)}) collective-permute-start(f32[4,512,128]{2,1,0:T(8,128)S(1)} %collective-permute-done.9.refs_2_), channel_id=1, source_target_pairs={{0,128},{128,0},{1,129},{129,1},{2,130},{130,2},{3,131},{131,3},{4... | collective-permute-start | bytes 3145736 | tf_op jit(solution)/shard_map/ppermute | solution.py:60
  61.1 11.2 %collective-permute-start.11 = (f32[4,512,128]{2,1,0:T(8,128)S(1)}, f32[4,512,128]{2,1,0:T(8,128)}, u32[]{:S(2)}, u32[]{:S(2)}) collective-permute-start(f32[4,512,128]{2,1,0:T(8,128)S(1)} %collective-permute-done.8.refs_1_), channel_id=1, source_target_pairs={{0,128},{128,0},{1,129},{129,1},{2,130},{130,2},{3,131},{131,3},{4... | collective-permute-start | bytes 3145736 | tf_op jit(solution)/shard_map/ppermute | solution.py:60
  69.4 12.2 %collective-permute-start.13 = (f32[2,512,128]{2,1,0:T(8,128)}, f32[2,512,128]{2,1,0:T(8,128)}, u32[]{:S(2)}, u32[]{:S(2)}) collective-permute-start(f32[2,512,128]{2,1,0:T(8,128)} %slice.26), channel_id=1, source_target_pairs={{0,1},{1,2},{2,3},{3,0},{4,5},{5,6},{6,7},{7,4},{8,9},{9,10},{10,1... | collective-permute-start | bytes 1572872 | tf_op jit(solution)/shard_map/ppermute | solution.py:60
  70.3 13.3 %collective-permute-start.14 = (f32[2,512,128]{2,1,0:T(8,128)}, f32[2,512,128]{2,1,0:T(8,128)}, u32[]{:S(2)}, u32[]{:S(2)}) collective-permute-start(f32[2,512,128]{2,1,0:T(8,128)} %slice.27), channel_id=1, source_target_pairs={{0,3},{1,0},{2,1},{3,2},{4,7},{5,4},{6,5},{7,6},{8,11},{9,8},{10,9... | collective-permute-start | bytes 1572872 | tf_op jit(solution)/shard_map/ppermute | solution.py:60
  72.3 13.9 %copy-start.23 = (s32[64,32]{0,1:T(8,128)S(1)}, s32[64,32]{0,1:T(8,128)}, u32[]{:S(2)}) copy-start(s32[64,32]{0,1:T(8,128)} %param.9) | copy-start | bytes 24580
  72.3 13.9 %copy-start.22 = (s32[64]{0:T(128)S(1)}, s32[64]{0:T(128)}, u32[]{:S(2)}) copy-start(s32[64]{0:T(128)} %widths.1) | copy-start | bytes 772
  80.4 8.8 %copy-start = (f32[1024,512]{1,0:T(8,128)S(1)}, f32[1024,512]{1,0:T(8,128)}, u32[]{:S(2)}) copy-start(f32[1024,512]{1,0:T(8,128)} %panel.3) | copy-start | bytes 6291460
  81.6 5.8 %collective-permute-start.15 = (f32[2,512,128]{2,1,0:T(8,128)}, f32[2,512,128]{2,1,0:T(8,128)S(1)}, u32[]{:S(2)}, u32[]{:S(2)}) collective-permute-start(f32[2,512,128]{2,1,0:T(8,128)} %collective-permute-done.13.refs_0_), channel_id=1, source_target_pairs={{0,128},{128,0},{1,129},{129,1},{2,130},{130,2},{3,131},{131,3},{4... | collective-permute-start | bytes 1572872 | tf_op jit(solution)/shard_map/ppermute | solution.py:60
  83.7 3.8 %collective-permute-start.16 = (f32[2,512,128]{2,1,0:T(8,128)}, f32[2,512,128]{2,1,0:T(8,128)}, u32[]{:S(2)}, u32[]{:S(2)}) collective-permute-start(f32[2,512,128]{2,1,0:T(8,128)} %collective-permute-done.14.refs_1_), channel_id=1, source_target_pairs={{0,128},{128,0},{1,129},{129,1},{2,130},{130,2},{3,131},{131,3},{4... | collective-permute-start | bytes 1572872 | tf_op jit(solution)/shard_map/ppermute | solution.py:60
  83.7 19.6 %collective-permute-start.18 = (f32[256,512]{1,0:T(8,128)}, f32[256,512]{1,0:T(8,128)S(1)}, u32[]{:S(2)}, u32[]{:S(2)}) collective-permute-start(f32[256,512]{1,0:T(8,128)} %get-tuple-element.40), channel_id=1, source_target_pairs={{0,96},{32,0},{64,32},{96,64},{1,97},{33,1},{65,33},{97,65},{2,98}... | collective-permute-start | bytes 1572872 | tf_op jit(solution)/shard_map/ppermute | solution.py:60
  86.2 17.1 %collective-permute-start.17 = (f32[256,512]{1,0:T(8,128)}, f32[256,512]{1,0:T(8,128)}, u32[]{:S(2)}, u32[]{:S(2)}) collective-permute-start(f32[256,512]{1,0:T(8,128)} %get-tuple-element.42), channel_id=1, source_target_pairs={{0,32},{32,64},{64,96},{96,0},{1,33},{33,65},{65,97},{97,1},{2,34}... | collective-permute-start | bytes 1572872 | tf_op jit(solution)/shard_map/ppermute | solution.py:60
  102.2 26.1 %collective-permute-start.20 = (f32[512,512]{1,0:T(8,128)S(1)}, f32[512,512]{1,0:T(8,128)S(1)}, u32[]{:S(2)}, u32[]{:S(2)}) collective-permute-start(f32[512,512]{1,0:T(8,128)S(1)} %shard_map.71), channel_id=1, source_target_pairs={{0,16},{16,0},{1,17},{17,1},{2,18},{18,2},{3,19},{19,3},{4,20},{20... | collective-permute-start | bytes 3145736 | tf_op jit(solution)/shard_map/ppermute | solution.py:60
  103.2 8.7 %copy-start.6 = (f32[1024,512]{1,0:T(8,128)S(1)}, f32[1024,512]{1,0:T(8,128)}, u32[]{:S(2)}) copy-start(f32[1024,512]{1,0:T(8,128)} %copy-done.4) | copy-start | bytes 6291460
  103.2 8.7 %copy-start.8 = (bf16[512,1536]{1,0:T(8,128)(2,1)S(1)}, bf16[512,1536]{1,0:T(8,128)(2,1)}, u32[]{:S(2)}) copy-start(bf16[512,1536]{1,0:T(8,128)(2,1)} %copy-done.7) | copy-start | bytes 4718596
  103.3 8.7 %copy-start.10 = (bf16[512,1536]{1,0:T(8,128)(2,1)S(1)}, bf16[512,1536]{1,0:T(8,128)(2,1)}, u32[]{:S(2)}) copy-start(bf16[512,1536]{1,0:T(8,128)(2,1)} %copy-done.9) | copy-start | bytes 4718596
  103.3 8.7 %copy-start.17 = (f32[256,512]{1,0:T(8,128)S(1)}, f32[256,512]{1,0:T(8,128)}, u32[]{:S(2)}) copy-start(f32[256,512]{1,0:T(8,128)} %copy-done.15) | copy-start | bytes 1572868
  103.3 8.7 %copy-start.20 = (f32[256,512]{1,0:T(8,128)S(1)}, f32[256,512]{1,0:T(8,128)}, u32[]{:S(2)}) copy-start(f32[256,512]{1,0:T(8,128)} %copy-done.18) | copy-start | bytes 1572868
  108.8 41.2 %collective-permute-start.19 = (f32[512,512]{1,0:T(8,128)S(1)}, f32[512,512]{1,0:T(8,128)S(1)}, u32[]{:S(2)}, u32[]{:S(2)}) collective-permute-start(f32[512,512]{1,0:T(8,128)S(1)} %shard_map.72), channel_id=1, source_target_pairs={{0,16},{16,0},{1,17},{17,1},{2,18},{18,2},{3,19},{19,3},{4,20},{20... | collective-permute-start | bytes 3145736 | tf_op jit(solution)/shard_map/ppermute | solution.py:60
  173.7 19.5 %copy-start.21 = (f32[1024,512]{1,0:T(8,128)S(1)}, f32[1024,512]{1,0:T(8,128)}, u32[]{:S(2)}) copy-start(f32[1024,512]{1,0:T(8,128)} %diag.1) | copy-start | bytes 6291460
  (13 other events, 17.5 us)

commit v6 on v5

--- a/solution.py
+++ b/solution.py
@@ -139,7 +139,6 @@
 def product_kernel(child, ids, own, left, right, top, bottom, *refs):
     high, low, far_high, far_low, meta, out, phigh, plow = refs
     mask = column_mask(meta, child)
-    rows = slice(child * SW, (child + 1) * SW)
     for a, away in enumerate((0, 3, 1, 2)):
         k = (ids[4] + away) % 4
         for d, source in enumerate((own, left, right, None)):
@@ -149,7 +148,7 @@
             if source is None:
                 value = jnp.concatenate([top[:, here], bottom[:, here]], axis=0)
             else:
-                value = source[rows, here]
+                value = source[:, here]
             phigh[:, lanes], plow[:, lanes] = split(value * mask * meta[child : child + 1, across])
     near = 12 * B
     for n in range(0, SW, 256):
@@ -211,17 +210,19 @@
 def local(anc_inverse, panel, diag_inverse, widths, pattern):
     names = ("core", "y", "zl", "zh", "x")
     ids = jnp.stack([lax.axis_index(n) for n in names]).astype(jnp.int32)
+    meta = call(meta_kernel, struct((8, WIDE)), [SMEM] * 3)(ids, widths, pattern)
     left, right = step(panel, "y", 1), step(panel, "y", -1)
     half = SW // 2
     far = [(step(left[a : a + half], "y", 1), step(right[a + half : a + SW], "y", -1)) for a in (0, SW)]
 
     rounds, table = z_rounds()
-    held = jnp.stack([lax.ppermute(anc_inverse, Z, pairs) for pairs in rounds])
+    got = [None if k == 1 else lax.ppermute(anc_inverse, Z, rounds[k]) for k in range(4)]
+    got[1] = lax.ppermute(after(anc_inverse, got[0]), Z, rounds[1])
+    held = jnp.stack(got)
     before, beyond = step(held, "x", 1), step(held, "x", -1)
-    near = [held, before, beyond]
+    near = [after(held, meta), before, beyond]
     near += [step(value, "core", 1, 2) for value in near]
     ends = step(after(before[:2], *far[0]), "x", 1), step(after(beyond[2:], *far[0]), "x", -1)
-    meta = call(meta_kernel, struct((8, WIDE)), [SMEM] * 3)(ids, widths, pattern)
     parts = call(
         functools.partial(near_kernel, table), [struct((SW, 12 * B), BF16)] * 4, [SMEM] + [VMEM] * 6
     )(ids, *near)
@@ -234,12 +235,17 @@
         anc = (*parts[2 * role : 2 * role + 2], *anc)
         values = []
         for child in range(2):
+            block = pl.BlockSpec((SW, SW), lambda g, child=child: (child, 0))
             values.append(
-                call(
+                pl.pallas_call(
                     functools.partial(product_kernel, child),
-                    struct((SW, SW)),
-                    [SMEM] + [VMEM] * 10,
-                    scratch=[pltpu.VMEM((SW, WIDE), BF16)] * 2,
+                    grid=(1,),
+                    out_shape=struct((SW, SW)),
+                    in_specs=[SMEM] + [block] * 3 + [VMEM] * 7,
+                    out_specs=VMEM,
+                    scratch_shapes=[pltpu.VMEM((SW, WIDE), BF16)] * 2,
+                    compiler_params=pltpu.CompilerParams(vmem_limit_bytes=36 * 2**20),
+                    cost_estimate=pl.CostEstimate(flops=1024, bytes_accessed=1024, transcendentals=0),
                 )(ids, after(panel, *values) if values else panel, left, right, *far[child], *anc, meta)
             )
         return values

time: 195 us -> 186 us (0.954)
  starting transfers between devices: 26.3 us -> 44.5 us
  local copies, waits for them, and re-layouts: 18.2 us -> 3.67 us
  waiting for transfers between devices: 74.3 us -> 61.9 us
    ppermute x4, waiting for transfers between devices: 32.4 us -> 6.37 us  [the longest x3 5.07 us: local(): lax.ppermute(anc_inverse, Z, rounds[k])]
    ppermute x4, starting transfers between devices: 8.79 us -> 26.9 us  [the longest x1 15.7 us: local(): got[1] = lax.ppermute(after(anc_inverse, got[0]), Z, rounds[1])]
    unnamed x49 -> x9, local copies, waits for them, and re-layouts: 14.4 us -> 0.1 us
    ppermute x17, waiting for transfers between devices: 41.8 us -> 55.5 us  [step(): return lax.ppermute(value, axis, [(i, (i + k) % n) for i in range(n)])]
  transfers between devices with their start and end apart: 21 -> 21, of which waited for: 10 -> 11; matrix products, arithmetic and copies ran while one was open for 2% -> 2% of each run, Pallas kernels for 16% -> 16%
where the time goes in v6:
time: 186 us
  waiting for transfers between devices  61.9 us (33%)
  starting transfers between devices  44.5 us (24%)
  blocking collectives  41.3 us (22%)
  Pallas kernels  33.4 us (18%)
  local copies, waits for them, and re-layouts  3.67 us (2%)
    ppermute x17, waiting for transfers between devices, step(): return lax.ppermute(value, axis, [(i, (i + k) % n) for i in range(n)])  55.5 us
    all_to_all x2, blocking collectives, swap(): return lax.all_to_all(value, ROW, 0, 0, tiled=True)  41.3 us
    pallas_call x4, Pallas kernels, product(): pl.pallas_call(functools.partial(product_kernel, child), grid=(1,), out_s...  22.2 us
    ppermute x17, starting transfers between devices, step(): return lax.ppermute(value, axis, [(i, (i + k) % n) for i in range(n)])  17.6 us
    ppermute x1, starting transfers between devices, local(): got[1] = lax.ppermute(after(anc_inverse, got[0]), Z, rounds[1])  15.7 us
    ppermute x3, starting transfers between devices, local(): lax.ppermute(anc_inverse, Z, rounds[k])  11.2 us
    ppermute x3, waiting for transfers between devices, local(): lax.ppermute(anc_inverse, Z, rounds[k])  5.07 us
  transfers between devices with their start and end apart: 21, of which 11 were waited for; matrix products, arithmetic and copies ran while one was open for 2% of the time, Pallas kernels for 16%

profile of v6, /device:TPU:6, one launch (start us, length us, event | category | flops | bytes accessed | tf_op | source)
XLA Modules:
  0.0 185.7 jit_solution(9084799229196240505)
XLA Ops:
  0.6 3.1 %collective-permute-start.1 = (f32[1024,512]{1,0:T(8,128)}, f32[1024,512]{1,0:T(8,128)S(1)}, u32[]{:S(2)}, u32[]{:S(2)}) collective-permute-start(f32[1024,512]{1,0:T(8,128)} %panel.3), channel_id=1, source_target_pairs={{0,96},{32,0},{64,32},{96,64},{1,97},{33,1},{65,33},{97,65},{2,98}... | collective-permute-start | bytes 6291464 | tf_op jit(solution)/shard_map/ppermute | solution.py:60
  3.7 1.6 collective-permute-start.4
  5.3 7.2 %collective-permute-start.7 = (f32[512,128]{1,0:T(8,128)}, f32[512,128]{1,0:T(8,128)S(1)}, u32[]{:S(2)}, u32[]{:S(2)}) collective-permute-start(f32[512,128]{1,0:T(8,128)} %param.5), channel_id=1, source_target_pairs={{0,8},{16,12},{8,0},{24,4},{20,28},{4,24},{28,20},{12,16},{1,9},{1... | collective-permute-start | bytes 786440 | tf_op jit(solution)/shard_map/ppermute | solution.py:219
  12.5 2.4 %collective-permute-start.6 = (f32[512,128]{1,0:T(8,128)}, f32[512,128]{1,0:T(8,128)S(1)}, u32[]{:S(2)}, u32[]{:S(2)}) collective-permute-start(f32[512,128]{1,0:T(8,128)} %param.5), channel_id=1, source_target_pairs={{0,4},{16,8},{8,12},{24,0},{20,16},{4,28},{28,24},{12,20},{1,5},{1... | collective-permute-start | bytes 786440 | tf_op jit(solution)/shard_map/ppermute | solution.py:219
  15.0 15.7 %collective-permute-start.5 = (f32[512,128]{1,0:T(8,128)}, f32[512,128]{1,0:T(8,128)S(1)}, u32[]{:S(2)}, u32[]{:S(2)}) collective-permute-start(f32[512,128]{1,0:T(8,128)} %param.5), channel_id=1, source_target_pairs={{0,12},{16,0},{8,4},{24,8},{20,24},{4,20},{28,16},{12,28},{1,13},{... | collective-permute-start | bytes 786440 | tf_op jit(solution)/shard_map/ppermute | solution.py:220
  30.7 5.0 %collective-permute-done.6 = f32[512,128]{1,0:T(8,128)S(1)} collective-permute-done((f32[512,128]{1,0:T(8,128)}, f32[512,128]{1,0:T(8,128)S(1)}, u32[]{:S(2)}, u32[]{:S(2)}) %collective-permute-start.6) | collective-permute-done | bytes 262176 | tf_op jit(solution)/shard_map/ppermute | solution.py:219
  35.7 1.3 collective-permute-done.5
  38.0 2.4 %collective-permute-start.8 = (f32[4,512,128]{2,1,0:T(8,128)S(1)}, f32[4,512,128]{2,1,0:T(8,128)}, u32[]{:S(2)}, u32[]{:S(2)}) collective-permute-start(f32[4,512,128]{2,1,0:T(8,128)S(1)} %pad_maximum_fusion.1.refs_0_), channel_id=1, source_target_pairs={{0,1},{1,2},{2,3},{3,0},{4,5},{5,6},{6,7},{7,4},{8,9},{9,10},{10,1... | collective-permute-start | bytes 3145736 | tf_op jit(solution)/shard_map/ppermute | solution.py:60
  40.6 1.2 shard_map.68.refs_4_.meta
  41.9 7.1 %collective-permute-done.1.right = f32[1024,512]{1,0:T(8,128)S(1)} collective-permute-done((f32[1024,512]{1,0:T(8,128)}, f32[1024,512]{1,0:T(8,128)S(1)}, u32[]{:S(2)}, u32[]{:S(2)}) %collective-permute-start.1) | collective-permute-done | bytes 2097184 | tf_op jit(solution)/shard_map/ppermute | solution.py:60
  49.0 3.7 %collective-permute-start.3 = (f32[256,512]{1,0:T(8,128)S(1)}, f32[256,512]{1,0:T(8,128)S(1)}, u32[]{:S(2)}, u32[]{:S(2)}) collective-permute-start(f32[256,512]{1,0:T(8,128)S(1)} %get-tuple-element.45), channel_id=1, source_target_pairs={{0,96},{32,0},{64,32},{96,64},{1,97},{33,1},{65,33},{97,65},{2,98}... | collective-permute-start | bytes 1572872 | tf_op jit(solution)/shard_map/ppermute | solution.py:60
  52.7 1.3 fusion.1
  54.0 9.0 %collective-permute-done.9.refs_2_ = f32[4,512,128]{2,1,0:T(8,128)} collective-permute-done((f32[4,512,128]{2,1,0:T(8,128)S(1)}, f32[4,512,128]{2,1,0:T(8,128)}, u32[]{:S(2)}, u32[]{:S(2)}) %collective-permute-start.9) | collective-permute-done | bytes 1048608 | tf_op jit(solution)/shard_map/ppermute | solution.py:60
  64.6 3.2 %collective-permute-done.2.top = f32[256,512]{1,0:T(8,128)S(1)} collective-permute-done((f32[256,512]{1,0:T(8,128)S(1)}, f32[256,512]{1,0:T(8,128)S(1)}, u32[]{:S(2)}, u32[]{:S(2)}) %collective-permute-start.2) | collective-permute-done | bytes 524320 | tf_op jit(solution)/shard_map/ppermute | solution.py:60
  68.3 1.1 slice.27
  69.4 1.6 collective-permute-start.14
  71.1 3.1 %shard_map.69 = (bf16[512,1536]{1,0:T(8,128)(2,1)S(1)}, bf16[512,1536]{1,0:T(8,128)(2,1)S(1)}, bf16[512,1536]{1,0:T(8,128)(2,1)S(1)}, bf16[512,1536]{1,0:T(8,128)(2,1)S(1)}) custom-call(s32[5]{0:T(128)S(1)} %stack.38.ids, f32[4,512,128]{2,1,0:T(8,128)S(1)} %pad_maximum_fusion.1.refs_0_, f32[4,512,128]{2,1,0:T(8,128)} %collective-permute-done.8.refs_1_, ...), custom_call_target="tpu_custom_call" | custom-call | flops 1024 | bytes 1024 | tf_op jit(solution)/shard_map/pallas_call | solution.py:226
  74.2 5.4 %collective-permute-done.13.refs_0_ = f32[2,512,128]{2,1,0:T(8,128)S(1)} collective-permute-done((f32[2,512,128]{2,1,0:T(8,128)S(1)}, f32[2,512,128]{2,1,0:T(8,128)S(1)}, u32[]{:S(2)}, u32[]{:S(2)}) %collective-permute-start.13) | collective-permute-done | bytes 524320 | tf_op jit(solution)/shard_map/ppermute | solution.py:60
  79.6 4.0 %collective-permute-done.14.refs_1_ = f32[2,512,128]{2,1,0:T(8,128)S(1)} collective-permute-done((f32[2,512,128]{2,1,0:T(8,128)S(1)}, f32[2,512,128]{2,1,0:T(8,128)S(1)}, u32[]{:S(2)}, u32[]{:S(2)}) %collective-permute-start.14) | collective-permute-done | bytes 524320 | tf_op jit(solution)/shard_map/ppermute | solution.py:60
  83.6 3.0 %collective-permute-start.18 = (f32[256,512]{1,0:T(8,128)S(1)}, f32[256,512]{1,0:T(8,128)S(1)}, u32[]{:S(2)}, u32[]{:S(2)}) collective-permute-start(f32[256,512]{1,0:T(8,128)S(1)} %get-tuple-element.44), channel_id=1, source_target_pairs={{0,96},{32,0},{64,32},{96,64},{1,97},{33,1},{65,33},{97,65},{2,98}... | collective-permute-start | bytes 1572872 | tf_op jit(solution)/shard_map/ppermute | solution.py:60
  87.5 5.5 %shard_map.71 = f32[512,512]{1,0:T(8,128)S(1)} custom-call(s32[5]{0:T(128)S(1)} %stack.38.ids, f32[1024,512]{1,0:T(8,128)S(1)} %copy-done, f32[1024,512]{1,0:T(8,128)} %collective-permute-done.left, f32[1024,512]{1,0:T(8,128)S(1)} %collective-permute-done.1.right, f32[256,512]{1,0:T(8,128)S(1)} %collective-permute-done.2.top, ...), custom_call_target="tpu_custom_call" | custom-call | flops 1024 | bytes 1024 | tf_op jit(solution)/shard_map/pallas_call | solution.py:240
  93.8 4.6 %collective-permute-done.18.bottom = f32[256,512]{1,0:T(8,128)S(1)} collective-permute-done((f32[256,512]{1,0:T(8,128)S(1)}, f32[256,512]{1,0:T(8,128)S(1)}, u32[]{:S(2)}, u32[]{:S(2)}) %collective-permute-start.18) | collective-permute-done | bytes 524320 | tf_op jit(solution)/shard_map/ppermute | solution.py:60
  98.4 3.4 %collective-permute-done.17.top = f32[256,512]{1,0:T(8,128)S(1)} collective-permute-done((f32[256,512]{1,0:T(8,128)S(1)}, f32[256,512]{1,0:T(8,128)S(1)}, u32[]{:S(2)}, u32[]{:S(2)}) %collective-permute-start.17) | collective-permute-done | bytes 524320 | tf_op jit(solution)/shard_map/ppermute | solution.py:60
  101.8 5.5 %shard_map.72 = f32[512,512]{1,0:T(8,128)S(1)} custom-call(s32[5]{0:T(128)S(1)} %stack.38.ids, f32[1024,512]{1,0:T(8,128)S(1)} %copy-done, f32[1024,512]{1,0:T(8,128)} %collective-permute-done.left, f32[1024,512]{1,0:T(8,128)S(1)} %collective-permute-done.1.right, f32[256,512]{1,0:T(8,128)S(1)} %collective-permute-done.17.top, ...), custom_call_target="tpu_custom_call" | custom-call | flops 1024 | bytes 1024 | tf_op jit(solution)/shard_map/pallas_call | solution.py:240
  109.3 5.5 %shard_map.74.mine = f32[512,512]{1,0:T(8,128)S(1)} custom-call(s32[5]{0:T(128)S(1)} %stack.38.ids, f32[1024,512]{1,0:T(8,128)S(1)} %copy-done, f32[1024,512]{1,0:T(8,128)} %collective-permute-done.left, f32[1024,512]{1,0:T(8,128)S(1)} %collective-permute-done.1.right, f32[256,512]{1,0:T(8,128)S(1)} %collective-permute-done.2.top, ...), custom_call_target="tpu_custom_call" | custom-call | flops 1024 | bytes 1024 | tf_op jit(solution)/shard_map/pallas_call | solution.py:240
  114.8 5.5 %shard_map.75.mine = f32[512,512]{1,0:T(8,128)S(1)} custom-call(s32[5]{0:T(128)S(1)} %stack.38.ids, f32[1024,512]{1,0:T(8,128)S(1)} %copy-done, f32[1024,512]{1,0:T(8,128)} %collective-permute-done.left, f32[1024,512]{1,0:T(8,128)S(1)} %collective-permute-done.1.right, f32[256,512]{1,0:T(8,128)S(1)} %collective-permute-done.17.top, ...), custom_call_target="tpu_custom_call" | custom-call | flops 1024 | bytes 1024 | tf_op jit(solution)/shard_map/pallas_call | solution.py:240
  120.4 1.7 shard_map.76
  122.1 18.8 %collective-permute-done.19.received = f32[512,512]{1,0:T(8,128)S(1)} collective-permute-done((f32[512,512]{1,0:T(8,128)S(1)}, f32[512,512]{1,0:T(8,128)S(1)}, u32[]{:S(2)}, u32[]{:S(2)}) %collective-permute-start.19) | collective-permute-done | bytes 1048608 | tf_op jit(solution)/shard_map/ppermute | solution.py:60
  140.9 1.7 shard_map.77
  142.7 21.9 %all_to_all.10.parts = f32[8,320,128]{2,1,0:T(8,128)S(1)} all-to-all(f32[8,320,128]{2,1,0:T(8,128)S(1)} %bitcast.12), channel_id=1, replica_groups=mesh['core'=2,'y'=4,'zl'=2,'zh'=4,'x'=4] {'y','zl'}, dimensions={0} | all-to-all | bytes 2621440 | tf_op jit(solution)/shard_map/all_to_all | solution.py:273
  164.7 19.4 %all_to_all.11 = f32[8,320,128]{2,1,0:T(8,128)S(1)} all-to-all(f32[8,320,128]{2,1,0:T(8,128)S(1)} %shard_map.78), channel_id=1, replica_groups=mesh['core'=2,'y'=4,'zl'=2,'zh'=4,'x'=4] {'y','zl'}, dimensions={0} | all-to-all | bytes 2621440 | tf_op jit(solution)/shard_map/all_to_all | solution.py:273
  184.1 1.6 shard_map.79
  (40 shorter events, 7.4 us)
Async XLA Ops:
  0.6 39.8 %copy-start.3 = (s32[64,32]{0,1:T(8,128)S(1)}, s32[64,32]{0,1:T(8,128)}, u32[]{:S(2)}) copy-start(s32[64,32]{0,1:T(8,128)} %param.9) | copy-start | bytes 24580
  0.6 39.9 %copy-start.2 = (s32[64]{0:T(128)S(1)}, s32[64]{0:T(128)}, u32[]{:S(2)}) copy-start(s32[64]{0:T(128)} %widths.1) | copy-start | bytes 772
  0.6 48.3 %collective-permute-start.1 = (f32[1024,512]{1,0:T(8,128)}, f32[1024,512]{1,0:T(8,128)S(1)}, u32[]{:S(2)}, u32[]{:S(2)}) collective-permute-start(f32[1024,512]{1,0:T(8,128)} %panel.3), channel_id=1, source_target_pairs={{0,96},{32,0},{64,32},{96,64},{1,97},{33,1},{65,33},{97,65},{2,98}... | collective-permute-start | bytes 6291464 | tf_op jit(solution)/shard_map/ppermute | solution.py:60
  3.7 48.9 %collective-permute-start = (f32[1024,512]{1,0:T(8,128)}, f32[1024,512]{1,0:T(8,128)}, u32[]{:S(2)}, u32[]{:S(2)}) collective-permute-start(f32[1024,512]{1,0:T(8,128)} %panel.3), channel_id=1, source_target_pairs={{0,32},{32,64},{64,96},{96,0},{1,33},{33,65},{65,97},{97,1},{2,34}... | collective-permute-start | bytes 6291464 | tf_op jit(solution)/shard_map/ppermute | solution.py:60
  3.7 11.2 %collective-permute-start.4 = (f32[512,128]{1,0:T(8,128)}, f32[512,128]{1,0:T(8,128)S(1)}, u32[]{:S(2)}, u32[]{:S(2)}) collective-permute-start(f32[512,128]{1,0:T(8,128)} %param.5), channel_id=1, source_target_pairs={{0,0},{16,4},{8,8},{24,12},{20,20},{4,16},{28,28},{12,24},{1,1},{1... | collective-permute-start | bytes 786440 | tf_op jit(solution)/shard_map/ppermute | solution.py:219
  5.3 25.4 %collective-permute-start.7 = (f32[512,128]{1,0:T(8,128)}, f32[512,128]{1,0:T(8,128)S(1)}, u32[]{:S(2)}, u32[]{:S(2)}) collective-permute-start(f32[512,128]{1,0:T(8,128)} %param.5), channel_id=1, source_target_pairs={{0,8},{16,12},{8,0},{24,4},{20,28},{4,24},{28,20},{12,16},{1,9},{1... | collective-permute-start | bytes 786440 | tf_op jit(solution)/shard_map/ppermute | solution.py:219
  12.5 23.2 %collective-permute-start.6 = (f32[512,128]{1,0:T(8,128)}, f32[512,128]{1,0:T(8,128)S(1)}, u32[]{:S(2)}, u32[]{:S(2)}) collective-permute-start(f32[512,128]{1,0:T(8,128)} %param.5), channel_id=1, source_target_pairs={{0,4},{16,8},{8,12},{24,0},{20,16},{4,28},{28,24},{12,20},{1,5},{1... | collective-permute-start | bytes 786440 | tf_op jit(solution)/shard_map/ppermute | solution.py:219
  15.0 22.1 %collective-permute-start.5 = (f32[512,128]{1,0:T(8,128)}, f32[512,128]{1,0:T(8,128)S(1)}, u32[]{:S(2)}, u32[]{:S(2)}) collective-permute-start(f32[512,128]{1,0:T(8,128)} %param.5), channel_id=1, source_target_pairs={{0,12},{16,0},{8,4},{24,8},{20,24},{4,20},{28,16},{12,28},{1,13},{... | collective-permute-start | bytes 786440 | tf_op jit(solution)/shard_map/ppermute | solution.py:220
  37.1 25.9 %collective-permute-start.9 = (f32[4,512,128]{2,1,0:T(8,128)S(1)}, f32[4,512,128]{2,1,0:T(8,128)}, u32[]{:S(2)}, u32[]{:S(2)}) collective-permute-start(f32[4,512,128]{2,1,0:T(8,128)S(1)} %pad_maximum_fusion.1.refs_0_), channel_id=1, source_target_pairs={{0,3},{1,0},{2,1},{3,2},{4,7},{5,4},{6,5},{7,6},{8,11},{9,8},{10,9... | collective-permute-start | bytes 3145736 | tf_op jit(solution)/shard_map/ppermute | solution.py:60
  38.0 25.0 %collective-permute-start.8 = (f32[4,512,128]{2,1,0:T(8,128)S(1)}, f32[4,512,128]{2,1,0:T(8,128)}, u32[]{:S(2)}, u32[]{:S(2)}) collective-permute-start(f32[4,512,128]{2,1,0:T(8,128)S(1)} %pad_maximum_fusion.1.refs_0_), channel_id=1, source_target_pairs={{0,1},{1,2},{2,3},{3,0},{4,5},{5,6},{6,7},{7,4},{8,9},{9,10},{10,1... | collective-permute-start | bytes 3145736 | tf_op jit(solution)/shard_map/ppermute | solution.py:60
  41.8 29.3 %collective-permute-start.10 = (f32[4,512,128]{2,1,0:T(8,128)S(1)}, f32[4,512,128]{2,1,0:T(8,128)S(1)}, u32[]{:S(2)}, u32[]{:S(2)}) collective-permute-start(f32[4,512,128]{2,1,0:T(8,128)S(1)} %pad_maximum_fusion.1.refs_0_), channel_id=1, source_target_pairs={{0,128},{128,0},{1,129},{129,1},{2,130},{130,2},{3,131},{131,3},{4... | collective-permute-start | bytes 3145736 | tf_op jit(solution)/shard_map/ppermute | solution.py:60
  49.0 15.6 %collective-permute-start.3 = (f32[256,512]{1,0:T(8,128)S(1)}, f32[256,512]{1,0:T(8,128)S(1)}, u32[]{:S(2)}, u32[]{:S(2)}) collective-permute-start(f32[256,512]{1,0:T(8,128)S(1)} %get-tuple-element.45), channel_id=1, source_target_pairs={{0,96},{32,0},{64,32},{96,64},{1,97},{33,1},{65,33},{97,65},{2,98}... | collective-permute-start | bytes 1572872 | tf_op jit(solution)/shard_map/ppermute | solution.py:60
  54.0 13.9 %collective-permute-start.2 = (f32[256,512]{1,0:T(8,128)S(1)}, f32[256,512]{1,0:T(8,128)S(1)}, u32[]{:S(2)}, u32[]{:S(2)}) collective-permute-start(f32[256,512]{1,0:T(8,128)S(1)} %get-tuple-element.47), channel_id=1, source_target_pairs={{0,32},{32,64},{64,96},{96,0},{1,33},{33,65},{65,97},{97,1},{2,34}... | collective-permute-start | bytes 1572872 | tf_op jit(solution)/shard_map/ppermute | solution.py:60
  63.0 8.0 %collective-permute-start.12 = (f32[4,512,128]{2,1,0:T(8,128)}, f32[4,512,128]{2,1,0:T(8,128)S(1)}, u32[]{:S(2)}, u32[]{:S(2)}) collective-permute-start(f32[4,512,128]{2,1,0:T(8,128)} %collective-permute-done.9.refs_2_), channel_id=1, source_target_pairs={{0,128},{128,0},{1,129},{129,1},{2,130},{130,2},{3,131},{131,3},{4... | collective-permute-start | bytes 3145736 | tf_op jit(solution)/shard_map/ppermute | solution.py:60
  63.0 8.0 %collective-permute-start.11 = (f32[4,512,128]{2,1,0:T(8,128)}, f32[4,512,128]{2,1,0:T(8,128)S(1)}, u32[]{:S(2)}, u32[]{:S(2)}) collective-permute-start(f32[4,512,128]{2,1,0:T(8,128)} %collective-permute-done.8.refs_1_), channel_id=1, source_target_pairs={{0,128},{128,0},{1,129},{129,1},{2,130},{130,2},{3,131},{131,3},{4... | collective-permute-start | bytes 3145736 | tf_op jit(solution)/shard_map/ppermute | solution.py:60
  67.9 11.7 %collective-permute-start.13 = (f32[2,512,128]{2,1,0:T(8,128)S(1)}, f32[2,512,128]{2,1,0:T(8,128)S(1)}, u32[]{:S(2)}, u32[]{:S(2)}) collective-permute-start(f32[2,512,128]{2,1,0:T(8,128)S(1)} %slice.26), channel_id=1, source_target_pairs={{0,1},{1,2},{2,3},{3,0},{4,5},{5,6},{6,7},{7,4},{8,9},{9,10},{10,1... | collective-permute-start | bytes 1572872 | tf_op jit(solution)/shard_map/ppermute | solution.py:60
  69.4 14.2 %collective-permute-start.14 = (f32[2,512,128]{2,1,0:T(8,128)S(1)}, f32[2,512,128]{2,1,0:T(8,128)S(1)}, u32[]{:S(2)}, u32[]{:S(2)}) collective-permute-start(f32[2,512,128]{2,1,0:T(8,128)S(1)} %slice.27), channel_id=1, source_target_pairs={{0,3},{1,0},{2,1},{3,2},{4,7},{5,4},{6,5},{7,6},{8,11},{9,8},{10,9... | collective-permute-start | bytes 1572872 | tf_op jit(solution)/shard_map/ppermute | solution.py:60
  74.2 13.3 %copy-start = (f32[1024,512]{1,0:T(8,128)S(1)}, f32[1024,512]{1,0:T(8,128)}, u32[]{:S(2)}) copy-start(f32[1024,512]{1,0:T(8,128)} %panel.3) | copy-start | bytes 6291460
  79.6 7.0 %collective-permute-start.15 = (f32[2,512,128]{2,1,0:T(8,128)S(1)}, f32[2,512,128]{2,1,0:T(8,128)S(1)}, u32[]{:S(2)}, u32[]{:S(2)}) collective-permute-start(f32[2,512,128]{2,1,0:T(8,128)S(1)} %collective-permute-done.13.refs_0_), channel_id=1, source_target_pairs={{0,128},{128,0},{1,129},{129,1},{2,130},{130,2},{3,131},{131,3},{4... | collective-permute-start | bytes 1572872 | tf_op jit(solution)/shard_map/ppermute | solution.py:60
  83.6 3.0 %collective-permute-start.16 = (f32[2,512,128]{2,1,0:T(8,128)S(1)}, f32[2,512,128]{2,1,0:T(8,128)S(1)}, u32[]{:S(2)}, u32[]{:S(2)}) collective-permute-start(f32[2,512,128]{2,1,0:T(8,128)S(1)} %collective-permute-done.14.refs_1_), channel_id=1, source_target_pairs={{0,128},{128,0},{1,129},{129,1},{2,130},{130,2},{3,131},{131,3},{4... | collective-permute-start | bytes 1572872 | tf_op jit(solution)/shard_map/ppermute | solution.py:60
  83.6 14.8 %collective-permute-start.18 = (f32[256,512]{1,0:T(8,128)S(1)}, f32[256,512]{1,0:T(8,128)S(1)}, u32[]{:S(2)}, u32[]{:S(2)}) collective-permute-start(f32[256,512]{1,0:T(8,128)S(1)} %get-tuple-element.44), channel_id=1, source_target_pairs={{0,96},{32,0},{64,32},{96,64},{1,97},{33,1},{65,33},{97,65},{2,98}... | collective-permute-start | bytes 1572872 | tf_op jit(solution)/shard_map/ppermute | solution.py:60
  86.6 15.3 %collective-permute-start.17 = (f32[256,512]{1,0:T(8,128)S(1)}, f32[256,512]{1,0:T(8,128)S(1)}, u32[]{:S(2)}, u32[]{:S(2)}) collective-permute-start(f32[256,512]{1,0:T(8,128)S(1)} %get-tuple-element.46), channel_id=1, source_target_pairs={{0,32},{32,64},{64,96},{96,0},{1,33},{33,65},{65,97},{97,1},{2,34}... | collective-permute-start | bytes 1572872 | tf_op jit(solution)/shard_map/ppermute | solution.py:60
  93.1 27.3 %collective-permute-start.20 = (f32[512,512]{1,0:T(8,128)S(1)}, f32[512,512]{1,0:T(8,128)S(1)}, u32[]{:S(2)}, u32[]{:S(2)}) collective-permute-start(f32[512,512]{1,0:T(8,128)S(1)} %shard_map.71), channel_id=1, source_target_pairs={{0,16},{16,0},{1,17},{17,1},{2,18},{18,2},{3,19},{19,3},{4,20},{20... | collective-permute-start | bytes 3145736 | tf_op jit(solution)/shard_map/ppermute | solution.py:60
  107.4 33.5 %collective-permute-start.19 = (f32[512,512]{1,0:T(8,128)S(1)}, f32[512,512]{1,0:T(8,128)S(1)}, u32[]{:S(2)}, u32[]{:S(2)}) collective-permute-start(f32[512,512]{1,0:T(8,128)S(1)} %shard_map.72), channel_id=1, source_target_pairs={{0,16},{16,0},{1,17},{17,1},{2,18},{18,2},{3,19},{19,3},{4,20},{20... | collective-permute-start | bytes 3145736 | tf_op jit(solution)/shard_map/ppermute | solution.py:60
  164.7 19.4 %copy-start.1 = (f32[1024,512]{1,0:T(8,128)S(1)}, f32[1024,512]{1,0:T(8,128)}, u32[]{:S(2)}) copy-start(f32[1024,512]{1,0:T(8,128)} %diag.1) | copy-start | bytes 6291460

commit v7 on v6

--- a/solution.py
+++ b/solution.py
@@ -211,22 +211,22 @@
     names = ("core", "y", "zl", "zh", "x")
     ids = jnp.stack([lax.axis_index(n) for n in names]).astype(jnp.int32)
     meta = call(meta_kernel, struct((8, WIDE)), [SMEM] * 3)(ids, widths, pattern)
-    left, right = step(panel, "y", 1), step(panel, "y", -1)
+    rounds, table = z_rounds()
+    got = [lax.ppermute(anc_inverse, Z, pairs) for pairs in rounds]
+    held = jnp.stack(got)
+
+    left, right = step(panel, "y", 1), step(after(panel, got[0]), "y", -1)
     half = SW // 2
     far = [(step(left[a : a + half], "y", 1), step(right[a + half : a + SW], "y", -1)) for a in (0, SW)]
 
-    rounds, table = z_rounds()
-    got = [None if k == 1 else lax.ppermute(anc_inverse, Z, rounds[k]) for k in range(4)]
-    got[1] = lax.ppermute(after(anc_inverse, got[0]), Z, rounds[1])
-    held = jnp.stack(got)
     before, beyond = step(held, "x", 1), step(held, "x", -1)
     near = [after(held, meta), before, beyond]
     near += [step(value, "core", 1, 2) for value in near]
-    ends = step(after(before[:2], *far[0]), "x", 1), step(after(beyond[2:], *far[0]), "x", -1)
+    ends = step(before[:2], "x", 1), step(beyond[2:], "x", -1)
     parts = call(
         functools.partial(near_kernel, table), [struct((SW, 12 * B), BF16)] * 4, [SMEM] + [VMEM] * 6
     )(ids, *near)
-    ends = tuple(after(value, parts[0]) for value in ends)
+    ends = tuple(after(value, parts[0], *far[0]) for value in ends)
     ends += tuple(step(value, "core", 1, 2) for value in ends)
 
     def product(role, first):

time: 186 us -> 186 us (level); the launches traced: 186 us -> 183 us
  starting transfers between devices: 44.5 us -> 37.5 us
  waiting for transfers between devices: 61.9 us -> 66.2 us
    ppermute x4, starting transfers between devices: 26.9 us -> 11.3 us  [local(): got = [lax.ppermute(anc_inverse, Z, pairs) for pairs in rounds]]
    ppermute x17, starting transfers between devices: 17.6 us -> 26.2 us  [step(): return lax.ppermute(value, axis, [(i, (i + k) % n) for i in range(n)])]
    ppermute x4, waiting for transfers between devices: 6.37 us -> 14.8 us  [local(): got = [lax.ppermute(anc_inverse, Z, pairs) for pairs in rounds]]
    ppermute x17, waiting for transfers between devices: 55.5 us -> 51.4 us  [step(): return lax.ppermute(value, axis, [(i, (i + k) % n) for i in range(n)])]
  transfers between devices with their start and end apart: 21 -> 21, of which waited for: 11 -> 10; matrix products, arithmetic and copies ran while one was open for 2% -> 2% of each run, Pallas kernels for 16% -> 16%
where the time goes in v7:
time: 186 us; the launch traced here: 183 us
  waiting for transfers between devices  66.2 us (36%)
  blocking collectives  41.2 us (22%)
  starting transfers between devices  37.5 us (20%)
  Pallas kernels  33.4 us (18%)
  local copies, waits for them, and re-layouts  3.67 us (2%)
    ppermute x17, waiting for transfers between devices, step(): return lax.ppermute(value, axis, [(i, (i + k) % n) for i in range(n)])  51.4 us
    all_to_all x2, blocking collectives, swap(): return lax.all_to_all(value, ROW, 0, 0, tiled=True)  41.2 us
    ppermute x17, starting transfers between devices, step(): return lax.ppermute(value, axis, [(i, (i + k) % n) for i in range(n)])  26.2 us
    pallas_call x4, Pallas kernels, product(): pl.pallas_call(functools.partial(product_kernel, child), grid=(1,), out_s...  22.2 us
    ppermute x4, waiting for transfers between devices, local(): got = [lax.ppermute(anc_inverse, Z, pairs) for pairs in rounds]  14.8 us
    ppermute x4, starting transfers between devices, local(): got = [lax.ppermute(anc_inverse, Z, pairs) for pairs in rounds]  11.3 us
  transfers between devices with their start and end apart: 21, of which 10 were waited for; matrix products, arithmetic and copies ran while one was open for 2% of the time, Pallas kernels for 16%

profile of v7, /device:TPU:6, one launch (start us, length us, event | category | flops | bytes accessed | tf_op | source)
XLA Modules:
  0.0 183.0 jit_solution(4856721372541976609)
XLA Ops:
  0.6 1.7 collective-permute-start
  2.3 1.6 collective-permute-start.1
  3.9 7.7 %collective-permute-start.5 = (f32[512,128]{1,0:T(8,128)}, f32[512,128]{1,0:T(8,128)S(1)}, u32[]{:S(2)}, u32[]{:S(2)}) collective-permute-start(f32[512,128]{1,0:T(8,128)} %param.5), channel_id=1, source_target_pairs={{0,12},{16,0},{8,4},{24,8},{20,24},{4,20},{28,16},{12,28},{1,13},{... | collective-permute-start | bytes 786440 | tf_op jit(solution)/shard_map/ppermute | solution.py:215
  11.6 2.0 %collective-permute-start.6 = (f32[512,128]{1,0:T(8,128)}, f32[512,128]{1,0:T(8,128)S(1)}, u32[]{:S(2)}, u32[]{:S(2)}) collective-permute-start(f32[512,128]{1,0:T(8,128)} %param.5), channel_id=1, source_target_pairs={{0,4},{16,8},{8,12},{24,0},{20,16},{4,28},{28,24},{12,20},{1,5},{1... | collective-permute-start | bytes 786440 | tf_op jit(solution)/shard_map/ppermute | solution.py:215
  13.6 1.7 collective-permute-start.2
  15.3 13.9 %collective-permute-done.5 = f32[512,128]{1,0:T(8,128)S(1)} collective-permute-done((f32[512,128]{1,0:T(8,128)}, f32[512,128]{1,0:T(8,128)S(1)}, u32[]{:S(2)}, u32[]{:S(2)}) %collective-permute-start.5) | collective-permute-done | bytes 262176 | tf_op jit(solution)/shard_map/ppermute | solution.py:215
  31.1 2.4 %collective-permute-start.8 = (f32[4,512,128]{2,1,0:T(8,128)S(1)}, f32[4,512,128]{2,1,0:T(8,128)}, u32[]{:S(2)}, u32[]{:S(2)}) collective-permute-start(f32[4,512,128]{2,1,0:T(8,128)S(1)} %pad_maximum_fusion.1.refs_0_), channel_id=1, source_target_pairs={{0,1},{1,2},{2,3},{3,0},{4,5},{5,6},{6,7},{7,4},{8,9},{9,10},{10,1... | collective-permute-start | bytes 3145736 | tf_op jit(solution)/shard_map/ppermute | solution.py:60
  33.6 1.2 shard_map.68.refs_4_.meta
  34.9 20.2 %collective-permute-done.9.refs_2_ = f32[4,512,128]{2,1,0:T(8,128)} collective-permute-done((f32[4,512,128]{2,1,0:T(8,128)S(1)}, f32[4,512,128]{2,1,0:T(8,128)}, u32[]{:S(2)}, u32[]{:S(2)}) %collective-permute-start.9) | collective-permute-done | bytes 1048608 | tf_op jit(solution)/shard_map/ppermute | solution.py:60
  55.2 1.1 slice.27
  57.0 3.2 %collective-permute-done.2.right = f32[1024,512]{1,0:T(8,128)} collective-permute-done((f32[1024,512]{1,0:T(8,128)}, f32[1024,512]{1,0:T(8,128)}, u32[]{:S(2)}, u32[]{:S(2)}) %collective-permute-start.2) | collective-permute-done | bytes 2097184 | tf_op jit(solution)/shard_map/ppermute | solution.py:60
  60.2 1.6 collective-permute-start.3
  61.8 1.3 fusion
  63.0 1.7 collective-permute-start.4
  66.4 3.1 %shard_map.69 = (bf16[512,1536]{1,0:T(8,128)(2,1)S(1)}, bf16[512,1536]{1,0:T(8,128)(2,1)S(1)}, bf16[512,1536]{1,0:T(8,128)(2,1)S(1)}, bf16[512,1536]{1,0:T(8,128)(2,1)S(1)}) custom-call(s32[5]{0:T(128)S(1)} %stack.38.ids, f32[4,512,128]{2,1,0:T(8,128)S(1)} %pad_maximum_fusion.1.refs_0_, f32[4,512,128]{2,1,0:T(8,128)} %collective-permute-done.8.refs_1_, ...), custom_call_target="tpu_custom_call" | custom-call | flops 1024 | bytes 1024 | tf_op jit(solution)/shard_map/pallas_call | solution.py:226
  69.5 2.3 %collective-permute-done.14.refs_1_ = f32[2,512,128]{2,1,0:T(8,128)S(1)} collective-permute-done((f32[2,512,128]{2,1,0:T(8,128)S(1)}, f32[2,512,128]{2,1,0:T(8,128)S(1)}, u32[]{:S(2)}, u32[]{:S(2)}) %collective-permute-start.14) | collective-permute-done | bytes 524320 | tf_op jit(solution)/shard_map/ppermute | solution.py:60
  71.9 1.2 collective-permute-done.3.top
  73.1 1.4 collective-permute-done.4.bottom
  74.5 2.6 %collective-permute-done.13.refs_0_ = f32[2,512,128]{2,1,0:T(8,128)S(1)} collective-permute-done((f32[2,512,128]{2,1,0:T(8,128)S(1)}, f32[2,512,128]{2,1,0:T(8,128)S(1)}, u32[]{:S(2)}, u32[]{:S(2)}) %collective-permute-start.13) | collective-permute-done | bytes 524320 | tf_op jit(solution)/shard_map/ppermute | solution.py:60
  77.9 3.0 %collective-permute-start.18 = (f32[256,512]{1,0:T(8,128)S(1)}, f32[256,512]{1,0:T(8,128)S(1)}, u32[]{:S(2)}, u32[]{:S(2)}) collective-permute-start(f32[256,512]{1,0:T(8,128)S(1)} %get-tuple-element.40), channel_id=1, source_target_pairs={{0,96},{32,0},{64,32},{96,64},{1,97},{33,1},{65,33},{97,65},{2,98}... | collective-permute-start | bytes 1572872 | tf_op jit(solution)/shard_map/ppermute | solution.py:60
  81.8 5.5 %shard_map.71 = f32[512,512]{1,0:T(8,128)S(1)} custom-call(s32[5]{0:T(128)S(1)} %stack.38.ids, f32[1024,512]{1,0:T(8,128)S(1)} %copy-done, f32[1024,512]{1,0:T(8,128)S(1)} %collective-permute-done.left, f32[1024,512]{1,0:T(8,128)} %collective-permute-done.2.right, f32[256,512]{1,0:T(8,128)S(1)} %collective-permute-done.3.top, ...), custom_call_target="tpu_custom_call" | custom-call | flops 1024 | bytes 1024 | tf_op jit(solution)/shard_map/pallas_call | solution.py:240
  87.4 5.7 %collective-permute-start.20 = (f32[512,512]{1,0:T(8,128)S(1)}, f32[512,512]{1,0:T(8,128)S(1)}, u32[]{:S(2)}, u32[]{:S(2)}) collective-permute-start(f32[512,512]{1,0:T(8,128)S(1)} %shard_map.71), channel_id=1, source_target_pairs={{0,16},{16,0},{1,17},{17,1},{2,18},{18,2},{3,19},{19,3},{4,20},{20... | collective-permute-start | bytes 3145736 | tf_op jit(solution)/shard_map/ppermute | solution.py:60
  93.0 5.5 %shard_map.72 = f32[512,512]{1,0:T(8,128)S(1)} custom-call(s32[5]{0:T(128)S(1)} %stack.38.ids, f32[1024,512]{1,0:T(8,128)S(1)} %copy-done, f32[1024,512]{1,0:T(8,128)S(1)} %collective-permute-done.left, f32[1024,512]{1,0:T(8,128)} %collective-permute-done.2.right, f32[256,512]{1,0:T(8,128)S(1)} %collective-permute-done.17.top, ...), custom_call_target="tpu_custom_call" | custom-call | flops 1024 | bytes 1024 | tf_op jit(solution)/shard_map/pallas_call | solution.py:240
  98.6 5.5 %collective-permute-start.19 = (f32[512,512]{1,0:T(8,128)S(1)}, f32[512,512]{1,0:T(8,128)S(1)}, u32[]{:S(2)}, u32[]{:S(2)}) collective-permute-start(f32[512,512]{1,0:T(8,128)S(1)} %shard_map.72), channel_id=1, source_target_pairs={{0,16},{16,0},{1,17},{17,1},{2,18},{18,2},{3,19},{19,3},{4,20},{20... | collective-permute-start | bytes 3145736 | tf_op jit(solution)/shard_map/ppermute | solution.py:60
  105.0 5.5 %shard_map.74.mine = f32[512,512]{1,0:T(8,128)S(1)} custom-call(s32[5]{0:T(128)S(1)} %stack.38.ids, f32[1024,512]{1,0:T(8,128)S(1)} %copy-done, f32[1024,512]{1,0:T(8,128)S(1)} %collective-permute-done.left, f32[1024,512]{1,0:T(8,128)} %collective-permute-done.2.right, f32[256,512]{1,0:T(8,128)S(1)} %collective-permute-done.3.top, ...), custom_call_target="tpu_custom_call" | custom-call | flops 1024 | bytes 1024 | tf_op jit(solution)/shard_map/pallas_call | solution.py:240
  110.6 5.5 %shard_map.75.mine = f32[512,512]{1,0:T(8,128)S(1)} custom-call(s32[5]{0:T(128)S(1)} %stack.38.ids, f32[1024,512]{1,0:T(8,128)S(1)} %copy-done, f32[1024,512]{1,0:T(8,128)S(1)} %collective-permute-done.left, f32[1024,512]{1,0:T(8,128)} %collective-permute-done.2.right, f32[256,512]{1,0:T(8,128)S(1)} %collective-permute-done.17.top, ...), custom_call_target="tpu_custom_call" | custom-call | flops 1024 | bytes 1024 | tf_op jit(solution)/shard_map/pallas_call | solution.py:240
  117.1 1.7 shard_map.76
  118.7 19.5 %collective-permute-done.19.received = f32[512,512]{1,0:T(8,128)S(1)} collective-permute-done((f32[512,512]{1,0:T(8,128)S(1)}, f32[512,512]{1,0:T(8,128)S(1)}, u32[]{:S(2)}, u32[]{:S(2)}) %collective-permute-start.19) | collective-permute-done | bytes 1048608 | tf_op jit(solution)/shard_map/ppermute | solution.py:60
  138.3 1.7 shard_map.77
  140.0 21.5 %all_to_all.10.parts = f32[8,320,128]{2,1,0:T(8,128)S(1)} all-to-all(f32[8,320,128]{2,1,0:T(8,128)S(1)} %bitcast.12), channel_id=1, replica_groups=mesh['core'=2,'y'=4,'zl'=2,'zh'=4,'x'=4] {'y','zl'}, dimensions={0} | all-to-all | bytes 2621440 | tf_op jit(solution)/shard_map/all_to_all | solution.py:273
  161.6 19.7 %all_to_all.11 = f32[8,320,128]{2,1,0:T(8,128)S(1)} all-to-all(f32[8,320,128]{2,1,0:T(8,128)S(1)} %shard_map.78), channel_id=1, replica_groups=mesh['core'=2,'y'=4,'zl'=2,'zh'=4,'x'=4] {'y','zl'}, dimensions={0} | all-to-all | bytes 2621440 | tf_op jit(solution)/shard_map/all_to_all | solution.py:273
  181.4 1.6 shard_map.79
  (40 shorter events, 8.3 us)
Async XLA Ops:
  0.6 32.8 %copy-start.3 = (s32[64,32]{0,1:T(8,128)S(1)}, s32[64,32]{0,1:T(8,128)}, u32[]{:S(2)}) copy-start(s32[64,32]{0,1:T(8,128)} %param.9) | copy-start | bytes 24580
  0.6 33.0 %copy-start.2 = (s32[64]{0:T(128)S(1)}, s32[64]{0:T(128)}, u32[]{:S(2)}) copy-start(s32[64]{0:T(128)} %widths.1) | copy-start | bytes 772
  0.6 55.7 %collective-permute-start = (f32[1024,512]{1,0:T(8,128)}, f32[1024,512]{1,0:T(8,128)S(1)}, u32[]{:S(2)}, u32[]{:S(2)}) collective-permute-start(f32[1024,512]{1,0:T(8,128)} %panel.3), channel_id=1, source_target_pairs={{0,32},{32,64},{64,96},{96,0},{1,33},{33,65},{65,97},{97,1},{2,34}... | collective-permute-start | bytes 6291464 | tf_op jit(solution)/shard_map/ppermute | solution.py:60
  2.3 11.3 %collective-permute-start.1 = (f32[512,128]{1,0:T(8,128)}, f32[512,128]{1,0:T(8,128)S(1)}, u32[]{:S(2)}, u32[]{:S(2)}) collective-permute-start(f32[512,128]{1,0:T(8,128)} %param.5), channel_id=1, source_target_pairs={{0,0},{16,4},{8,8},{24,12},{20,20},{4,16},{28,28},{12,24},{1,1},{1... | collective-permute-start | bytes 786440 | tf_op jit(solution)/shard_map/ppermute | solution.py:215
  3.9 25.3 %collective-permute-start.5 = (f32[512,128]{1,0:T(8,128)}, f32[512,128]{1,0:T(8,128)S(1)}, u32[]{:S(2)}, u32[]{:S(2)}) collective-permute-start(f32[512,128]{1,0:T(8,128)} %param.5), channel_id=1, source_target_pairs={{0,12},{16,0},{8,4},{24,8},{20,24},{4,20},{28,16},{12,28},{1,13},{... | collective-permute-start | bytes 786440 | tf_op jit(solution)/shard_map/ppermute | solution.py:215
  11.6 17.6 %collective-permute-start.7 = (f32[512,128]{1,0:T(8,128)}, f32[512,128]{1,0:T(8,128)S(1)}, u32[]{:S(2)}, u32[]{:S(2)}) collective-permute-start(f32[512,128]{1,0:T(8,128)} %param.5), channel_id=1, source_target_pairs={{0,8},{16,12},{8,0},{24,4},{20,28},{4,24},{28,20},{12,16},{1,9},{1... | collective-permute-start | bytes 786440 | tf_op jit(solution)/shard_map/ppermute | solution.py:215
  11.6 18.5 %collective-permute-start.6 = (f32[512,128]{1,0:T(8,128)}, f32[512,128]{1,0:T(8,128)S(1)}, u32[]{:S(2)}, u32[]{:S(2)}) collective-permute-start(f32[512,128]{1,0:T(8,128)} %param.5), channel_id=1, source_target_pairs={{0,4},{16,8},{8,12},{24,0},{20,16},{4,28},{28,24},{12,20},{1,5},{1... | collective-permute-start | bytes 786440 | tf_op jit(solution)/shard_map/ppermute | solution.py:215
  13.6 46.6 %collective-permute-start.2 = (f32[1024,512]{1,0:T(8,128)}, f32[1024,512]{1,0:T(8,128)}, u32[]{:S(2)}, u32[]{:S(2)}) collective-permute-start(f32[1024,512]{1,0:T(8,128)} %panel.3), channel_id=1, source_target_pairs={{0,96},{32,0},{64,32},{96,64},{1,97},{33,1},{65,33},{97,65},{2,98}... | collective-permute-start | bytes 6291464 | tf_op jit(solution)/shard_map/ppermute | solution.py:60
  30.1 25.0 %collective-permute-start.9 = (f32[4,512,128]{2,1,0:T(8,128)S(1)}, f32[4,512,128]{2,1,0:T(8,128)}, u32[]{:S(2)}, u32[]{:S(2)}) collective-permute-start(f32[4,512,128]{2,1,0:T(8,128)S(1)} %pad_maximum_fusion.1.refs_0_), channel_id=1, source_target_pairs={{0,3},{1,0},{2,1},{3,2},{4,7},{5,4},{6,5},{7,6},{8,11},{9,8},{10,9... | collective-permute-start | bytes 3145736 | tf_op jit(solution)/shard_map/ppermute | solution.py:60
  31.1 25.2 %collective-permute-start.8 = (f32[4,512,128]{2,1,0:T(8,128)S(1)}, f32[4,512,128]{2,1,0:T(8,128)}, u32[]{:S(2)}, u32[]{:S(2)}) collective-permute-start(f32[4,512,128]{2,1,0:T(8,128)S(1)} %pad_maximum_fusion.1.refs_0_), channel_id=1, source_target_pairs={{0,1},{1,2},{2,3},{3,0},{4,5},{5,6},{6,7},{7,4},{8,9},{9,10},{10,1... | collective-permute-start | bytes 3145736 | tf_op jit(solution)/shard_map/ppermute | solution.py:60
  34.8 28.2 %collective-permute-start.10 = (f32[4,512,128]{2,1,0:T(8,128)S(1)}, f32[4,512,128]{2,1,0:T(8,128)S(1)}, u32[]{:S(2)}, u32[]{:S(2)}) collective-permute-start(f32[4,512,128]{2,1,0:T(8,128)S(1)} %pad_maximum_fusion.1.refs_0_), channel_id=1, source_target_pairs={{0,128},{128,0},{1,129},{129,1},{2,130},{130,2},{3,131},{131,3},{4... | collective-permute-start | bytes 3145736 | tf_op jit(solution)/shard_map/ppermute | solution.py:60
  55.1 10.7 %collective-permute-start.12 = (f32[4,512,128]{2,1,0:T(8,128)}, f32[4,512,128]{2,1,0:T(8,128)S(1)}, u32[]{:S(2)}, u32[]{:S(2)}) collective-permute-start(f32[4,512,128]{2,1,0:T(8,128)} %collective-permute-done.9.refs_2_), channel_id=1, source_target_pairs={{0,128},{128,0},{1,129},{129,1},{2,130},{130,2},{3,131},{131,3},{4... | collective-permute-start | bytes 3145736 | tf_op jit(solution)/shard_map/ppermute | solution.py:60
  56.2 15.6 %collective-permute-start.14 = (f32[2,512,128]{2,1,0:T(8,128)S(1)}, f32[2,512,128]{2,1,0:T(8,128)S(1)}, u32[]{:S(2)}, u32[]{:S(2)}) collective-permute-start(f32[2,512,128]{2,1,0:T(8,128)S(1)} %slice.27), channel_id=1, source_target_pairs={{0,3},{1,0},{2,1},{3,2},{4,7},{5,4},{6,5},{7,6},{8,11},{9,8},{10,9... | collective-permute-start | bytes 1572872 | tf_op jit(solution)/shard_map/ppermute | solution.py:60
  56.3 10.1 %collective-permute-start.11 = (f32[4,512,128]{2,1,0:T(8,128)}, f32[4,512,128]{2,1,0:T(8,128)S(1)}, u32[]{:S(2)}, u32[]{:S(2)}) collective-permute-start(f32[4,512,128]{2,1,0:T(8,128)} %collective-permute-done.8.refs_1_), channel_id=1, source_target_pairs={{0,128},{128,0},{1,129},{129,1},{2,130},{130,2},{3,131},{131,3},{4... | collective-permute-start | bytes 3145736 | tf_op jit(solution)/shard_map/ppermute | solution.py:60
  60.2 12.9 %collective-permute-start.3 = (f32[256,512]{1,0:T(8,128)S(1)}, f32[256,512]{1,0:T(8,128)S(1)}, u32[]{:S(2)}, u32[]{:S(2)}) collective-permute-start(f32[256,512]{1,0:T(8,128)S(1)} %get-tuple-element.43), channel_id=1, source_target_pairs={{0,32},{32,64},{64,96},{96,0},{1,33},{33,65},{65,97},{97,1},{2,34}... | collective-permute-start | bytes 1572872 | tf_op jit(solution)/shard_map/ppermute | solution.py:60
  63.0 11.4 %collective-permute-start.4 = (f32[256,512]{1,0:T(8,128)S(1)}, f32[256,512]{1,0:T(8,128)S(1)}, u32[]{:S(2)}, u32[]{:S(2)}) collective-permute-start(f32[256,512]{1,0:T(8,128)S(1)} %get-tuple-element.41), channel_id=1, source_target_pairs={{0,96},{32,0},{64,32},{96,64},{1,97},{33,1},{65,33},{97,65},{2,98}... | collective-permute-start | bytes 1572872 | tf_op jit(solution)/shard_map/ppermute | solution.py:60
  65.9 11.2 %collective-permute-start.13 = (f32[2,512,128]{2,1,0:T(8,128)S(1)}, f32[2,512,128]{2,1,0:T(8,128)S(1)}, u32[]{:S(2)}, u32[]{:S(2)}) collective-permute-start(f32[2,512,128]{2,1,0:T(8,128)S(1)} %slice.26), channel_id=1, source_target_pairs={{0,1},{1,2},{2,3},{3,0},{4,5},{5,6},{6,7},{7,4},{8,9},{9,10},{10,1... | collective-permute-start | bytes 1572872 | tf_op jit(solution)/shard_map/ppermute | solution.py:60
  69.5 12.3 %copy-start = (f32[1024,512]{1,0:T(8,128)S(1)}, f32[1024,512]{1,0:T(8,128)}, u32[]{:S(2)}) copy-start(f32[1024,512]{1,0:T(8,128)} %panel.3) | copy-start | bytes 6291460
  77.1 3.8 %collective-permute-start.15 = (f32[2,512,128]{2,1,0:T(8,128)S(1)}, f32[2,512,128]{2,1,0:T(8,128)S(1)}, u32[]{:S(2)}, u32[]{:S(2)}) collective-permute-start(f32[2,512,128]{2,1,0:T(8,128)S(1)} %collective-permute-done.13.refs_0_), channel_id=1, source_target_pairs={{0,128},{128,0},{1,129},{129,1},{2,130},{130,2},{3,131},{131,3},{4... | collective-permute-start | bytes 1572872 | tf_op jit(solution)/shard_map/ppermute | solution.py:60
  77.1 3.8 %collective-permute-start.16 = (f32[2,512,128]{2,1,0:T(8,128)S(1)}, f32[2,512,128]{2,1,0:T(8,128)S(1)}, u32[]{:S(2)}, u32[]{:S(2)}) collective-permute-start(f32[2,512,128]{2,1,0:T(8,128)S(1)} %collective-permute-done.14.refs_1_), channel_id=1, source_target_pairs={{0,128},{128,0},{1,129},{129,1},{2,130},{130,2},{3,131},{131,3},{4... | collective-permute-start | bytes 1572872 | tf_op jit(solution)/shard_map/ppermute | solution.py:60
  77.6 15.4 %collective-permute-start.17 = (f32[256,512]{1,0:T(8,128)S(1)}, f32[256,512]{1,0:T(8,128)S(1)}, u32[]{:S(2)}, u32[]{:S(2)}) collective-permute-start(f32[256,512]{1,0:T(8,128)S(1)} %get-tuple-element.42), channel_id=1, source_target_pairs={{0,32},{32,64},{64,96},{96,0},{1,33},{33,65},{65,97},{97,1},{2,34}... | collective-permute-start | bytes 1572872 | tf_op jit(solution)/shard_map/ppermute | solution.py:60
  77.9 15.1 %collective-permute-start.18 = (f32[256,512]{1,0:T(8,128)S(1)}, f32[256,512]{1,0:T(8,128)S(1)}, u32[]{:S(2)}, u32[]{:S(2)}) collective-permute-start(f32[256,512]{1,0:T(8,128)S(1)} %get-tuple-element.40), channel_id=1, source_target_pairs={{0,96},{32,0},{64,32},{96,64},{1,97},{33,1},{65,33},{97,65},{2,98}... | collective-permute-start | bytes 1572872 | tf_op jit(solution)/shard_map/ppermute | solution.py:60
  87.4 29.7 %collective-permute-start.20 = (f32[512,512]{1,0:T(8,128)S(1)}, f32[512,512]{1,0:T(8,128)S(1)}, u32[]{:S(2)}, u32[]{:S(2)}) collective-permute-start(f32[512,512]{1,0:T(8,128)S(1)} %shard_map.71), channel_id=1, source_target_pairs={{0,16},{16,0},{1,17},{17,1},{2,18},{18,2},{3,19},{19,3},{4,20},{20... | collective-permute-start | bytes 3145736 | tf_op jit(solution)/shard_map/ppermute | solution.py:60
  98.6 39.7 %collective-permute-start.19 = (f32[512,512]{1,0:T(8,128)S(1)}, f32[512,512]{1,0:T(8,128)S(1)}, u32[]{:S(2)}, u32[]{:S(2)}) collective-permute-start(f32[512,512]{1,0:T(8,128)S(1)} %shard_map.72), channel_id=1, source_target_pairs={{0,16},{16,0},{1,17},{17,1},{2,18},{18,2},{3,19},{19,3},{4,20},{20... | collective-permute-start | bytes 3145736 | tf_op jit(solution)/shard_map/ppermute | solution.py:60
  161.6 19.7 %copy-start.1 = (f32[1024,512]{1,0:T(8,128)S(1)}, f32[1024,512]{1,0:T(8,128)}, u32[]{:S(2)}) copy-start(f32[1024,512]{1,0:T(8,128)} %diag.1) | copy-start | bytes 6291460

commit v8 on v7

--- a/solution.py
+++ b/solution.py
@@ -10,6 +10,7 @@
 B = 128
 SW = 512
 WIDE = 2048
+PACKED = 1056
 LIMIT = 22 * 2**20
 ROW = ("y", "zl")
 Z = ("zl", "zh")
@@ -160,13 +161,25 @@
             out[at, lines] = value
 
 
-def lower_blocks(update, left, right):
+def lower_blocks(update, pairs):
     at = 0
+    diagonal = []
     for a in range(4):
-        value = dot3([v[a * B : (a + 1) * B] for v in left], [v[: (a + 1) * B] for v in right])
-        for b in range(a + 1):
+        value = None
+        for left, right in pairs:
+            term = dot3([v[a * B : (a + 1) * B] for v in left], [v[: (a + 1) * B] for v in right])
+            value = term if value is None else value + term
+        for b in range(a):
             update[at * B : (at + 1) * B, :] = value[:, b * B : (b + 1) * B]
             at += 1
+        diagonal.append(value[:, a * B :])
+    line, lane = (lax.broadcasted_iota(jnp.int32, (B, B), axis) for axis in range(2))
+    update[8 * B :, :] = jnp.zeros((PACKED - 8 * B, B), F32)
+    for k in range(2):
+        first, second = diagonal[2 * k : 2 * k + 2]
+        update[at * B : (at + 1) * B, :] = jnp.where(line >= lane, first, second)
+        update[8 * B + k : 8 * B + k + 1, :] = jnp.sum(jnp.where(line == lane, second, 0.0), axis=0, keepdims=True)
+        at += 1
 
 
 def finish_kernel(child, mine, received, panel, meta, *refs):
@@ -175,7 +188,7 @@
     masks = wide * meta[child : child + 1, :SW]
     product = (mine[...] + received[...]) * masks
     off[...] = -product
-    lower_blocks(update, split(product), split(panel[...] * masks))
+    lower_blocks(update, [(split(product), split(panel[...] * masks))])
 
 
 def sum_kernel(parts, out):
@@ -187,20 +200,32 @@
 
 
 def child_kernel(parts, diag, meta, out):
-    at = 0
+    line, lane = (lax.broadcasted_iota(jnp.int32, (B, B), axis) for axis in range(2))
     for child in range(2):
+        base = child * PACKED
         across = lax.broadcasted_iota(jnp.int32, (1, SW), 1).astype(F32) < meta[2 + child : 3 + child, :SW]
         across = across.astype(F32)
         mask = column_mask(meta, child)
+
+        def put(i, j, value):
+            lines = slice(child * SW + i * B, child * SW + (i + 1) * B)
+            lanes = slice(j * B, (j + 1) * B)
+            out[lines, lanes] = (diag[lines, lanes] + value) * mask[i * B : (i + 1) * B] * across[:, lanes]
+
+        at = base
         for a in range(4):
-            for b in range(a + 1):
-                block = parts[at]
-                at += 1
-                for (i, j), value in {(b, a): block.T, (a, b): block}.items():
-                    lines = slice(child * SW + i * B, child * SW + (i + 1) * B)
-                    lanes = slice(j * B, (j + 1) * B)
-                    rows = mask[i * B : (i + 1) * B]
-                    out[lines, lanes] = (diag[lines, lanes] + value) * rows * across[:, lanes]
+            for b in range(a):
+                block = parts[at : at + B, :]
+                put(a, b, block)
+                put(b, a, block.T)
+                at += B
+        for k in range(2):
+            block = parts[at : at + B, :]
+            turned = block.T
+            row = parts[base + 8 * B + k : base + 8 * B + k + 1, :]
+            put(2 * k, 2 * k, jnp.where(line >= lane, block, turned))
+            put(2 * k + 1, 2 * k + 1, jnp.where(line < lane, block, jnp.where(line > lane, turned, row)))
+            at += B
 
 
 def after(value, *before):
@@ -260,7 +285,7 @@
         off, update = pl.pallas_call(
             functools.partial(finish_kernel, child),
             grid=(1,),
-            out_shape=(struct(panel.shape), struct((10 * B, B))),
+            out_shape=(struct(panel.shape), struct((PACKED, B))),
             in_specs=[VMEM, VMEM, block, VMEM] + [pl.BlockSpec(memory_space=pl.ANY)] * child,
             out_specs=[block, VMEM],
             input_output_aliases={4: 0} if child else {},
@@ -272,9 +297,9 @@
     def swap(value):
         return lax.all_to_all(value, ROW, 0, 0, tiled=True)
 
-    shape = (8, 20 * B // 8, B)
+    shape = (8, 2 * PACKED // 8, B)
     spread = swap(jnp.concatenate(updates, axis=0).reshape(shape))
-    summed = swap(call(sum_kernel, struct(shape), [VMEM])(spread)).reshape(20, B, B)
+    summed = swap(call(sum_kernel, struct(shape), [VMEM])(spread)).reshape(2 * PACKED, B)
     out = call(child_kernel, struct(diag_inverse.shape), [VMEM] * 3)(summed, diag_inverse, meta)
     return off, out
 

time: 186 us -> 181 us (0.973)
  blocking collectives: 41.2 us -> 36.5 us
    all_to_all x2, blocking collectives: 41.2 us -> 36.5 us  [swap(): return lax.all_to_all(value, ROW, 0, 0, tiled=True)]
  transfers between devices with their start and end apart: 21 -> 21, of which waited for: 10 -> 10; matrix products, arithmetic and copies ran while one was open for 2% -> 2% of each run, Pallas kernels for 16% -> 17%
where the time goes in v8:
time: 181 us; the launch traced here: 178 us
  waiting for transfers between devices  66.2 us (37%)
  starting transfers between devices  37.5 us (21%)
  blocking collectives  36.5 us (20%)
  Pallas kernels  33.5 us (19%)
  local copies, waits for them, and re-layouts  3.67 us (2%)
    ppermute x17, waiting for transfers between devices, step(): return lax.ppermute(value, axis, [(i, (i + k) % n) for i in range(n)])  51.4 us
    all_to_all x2, blocking collectives, swap(): return lax.all_to_all(value, ROW, 0, 0, tiled=True)  36.5 us
    ppermute x17, starting transfers between devices, step(): return lax.ppermute(value, axis, [(i, (i + k) % n) for i in range(n)])  26.2 us
    pallas_call x4, Pallas kernels, product(): pl.pallas_call(functools.partial(product_kernel, child), grid=(1,), out_s...  22.2 us
    ppermute x4, waiting for transfers between devices, local(): got = [lax.ppermute(anc_inverse, Z, pairs) for pairs in rounds]  14.8 us
    ppermute x4, starting transfers between devices, local(): got = [lax.ppermute(anc_inverse, Z, pairs) for pairs in rounds]  11.3 us
  transfers between devices with their start and end apart: 21, of which 10 were waited for; matrix products, arithmetic and copies ran while one was open for 2% of the time, Pallas kernels for 17%

profile of v8, /device:TPU:6, one launch (start us, length us, event | category | flops | bytes accessed | tf_op | source)
XLA Modules:
  0.0 178.3 jit_solution(10973081154283512990)
XLA Ops:
  0.6 1.7 collective-permute-start
  2.3 1.6 collective-permute-start.1
  3.9 7.7 %collective-permute-start.5 = (f32[512,128]{1,0:T(8,128)}, f32[512,128]{1,0:T(8,128)S(1)}, u32[]{:S(2)}, u32[]{:S(2)}) collective-permute-start(f32[512,128]{1,0:T(8,128)} %param.5), channel_id=1, source_target_pairs={{0,12},{16,0},{8,4},{24,8},{20,24},{4,20},{28,16},{12,28},{1,13},{... | collective-permute-start | bytes 786440 | tf_op jit(solution)/shard_map/ppermute | solution.py:240
  11.6 2.0 %collective-permute-start.6 = (f32[512,128]{1,0:T(8,128)}, f32[512,128]{1,0:T(8,128)S(1)}, u32[]{:S(2)}, u32[]{:S(2)}) collective-permute-start(f32[512,128]{1,0:T(8,128)} %param.5), channel_id=1, source_target_pairs={{0,4},{16,8},{8,12},{24,0},{20,16},{4,28},{28,24},{12,20},{1,5},{1... | collective-permute-start | bytes 786440 | tf_op jit(solution)/shard_map/ppermute | solution.py:240
  13.6 1.7 collective-permute-start.2
  15.3 13.9 %collective-permute-done.5 = f32[512,128]{1,0:T(8,128)S(1)} collective-permute-done((f32[512,128]{1,0:T(8,128)}, f32[512,128]{1,0:T(8,128)S(1)}, u32[]{:S(2)}, u32[]{:S(2)}) %collective-permute-start.5) | collective-permute-done | bytes 262176 | tf_op jit(solution)/shard_map/ppermute | solution.py:240
  31.1 2.4 %collective-permute-start.8 = (f32[4,512,128]{2,1,0:T(8,128)S(1)}, f32[4,512,128]{2,1,0:T(8,128)}, u32[]{:S(2)}, u32[]{:S(2)}) collective-permute-start(f32[4,512,128]{2,1,0:T(8,128)S(1)} %pad_maximum_fusion.1.refs_0_), channel_id=1, source_target_pairs={{0,1},{1,2},{2,3},{3,0},{4,5},{5,6},{6,7},{7,4},{8,9},{9,10},{10,1... | collective-permute-start | bytes 3145736 | tf_op jit(solution)/shard_map/ppermute | solution.py:61
  33.6 1.2 shard_map.68.refs_4_.meta
  34.9 20.2 %collective-permute-done.9.refs_2_ = f32[4,512,128]{2,1,0:T(8,128)} collective-permute-done((f32[4,512,128]{2,1,0:T(8,128)S(1)}, f32[4,512,128]{2,1,0:T(8,128)}, u32[]{:S(2)}, u32[]{:S(2)}) %collective-permute-start.9) | collective-permute-done | bytes 1048608 | tf_op jit(solution)/shard_map/ppermute | solution.py:61
  55.2 1.1 slice.27
  57.0 3.2 %collective-permute-done.2.right = f32[1024,512]{1,0:T(8,128)} collective-permute-done((f32[1024,512]{1,0:T(8,128)}, f32[1024,512]{1,0:T(8,128)}, u32[]{:S(2)}, u32[]{:S(2)}) %collective-permute-start.2) | collective-permute-done | bytes 2097184 | tf_op jit(solution)/shard_map/ppermute | solution.py:61
  60.2 1.6 collective-permute-start.3
  61.8 1.3 fusion
  63.0 1.7 collective-permute-start.4
  66.4 3.1 %shard_map.69 = (bf16[512,1536]{1,0:T(8,128)(2,1)S(1)}, bf16[512,1536]{1,0:T(8,128)(2,1)S(1)}, bf16[512,1536]{1,0:T(8,128)(2,1)S(1)}, bf16[512,1536]{1,0:T(8,128)(2,1)S(1)}) custom-call(s32[5]{0:T(128)S(1)} %stack.38.ids, f32[4,512,128]{2,1,0:T(8,128)S(1)} %pad_maximum_fusion.1.refs_0_, f32[4,512,128]{2,1,0:T(8,128)} %collective-permute-done.8.refs_1_, ...), custom_call_target="tpu_custom_call" | custom-call | flops 1024 | bytes 1024 | tf_op jit(solution)/shard_map/pallas_call | solution.py:251
  69.5 2.3 %collective-permute-done.14.refs_1_ = f32[2,512,128]{2,1,0:T(8,128)S(1)} collective-permute-done((f32[2,512,128]{2,1,0:T(8,128)S(1)}, f32[2,512,128]{2,1,0:T(8,128)S(1)}, u32[]{:S(2)}, u32[]{:S(2)}) %collective-permute-start.14) | collective-permute-done | bytes 524320 | tf_op jit(solution)/shard_map/ppermute | solution.py:61
  71.9 1.2 collective-permute-done.3.top
  73.1 1.4 collective-permute-done.4.bottom
  74.5 2.6 %collective-permute-done.13.refs_0_ = f32[2,512,128]{2,1,0:T(8,128)S(1)} collective-permute-done((f32[2,512,128]{2,1,0:T(8,128)S(1)}, f32[2,512,128]{2,1,0:T(8,128)S(1)}, u32[]{:S(2)}, u32[]{:S(2)}) %collective-permute-start.13) | collective-permute-done | bytes 524320 | tf_op jit(solution)/shard_map/ppermute | solution.py:61
  77.9 3.0 %collective-permute-start.18 = (f32[256,512]{1,0:T(8,128)S(1)}, f32[256,512]{1,0:T(8,128)S(1)}, u32[]{:S(2)}, u32[]{:S(2)}) collective-permute-start(f32[256,512]{1,0:T(8,128)S(1)} %get-tuple-element.40), channel_id=1, source_target_pairs={{0,96},{32,0},{64,32},{96,64},{1,97},{33,1},{65,33},{97,65},{2,98}... | collective-permute-start | bytes 1572872 | tf_op jit(solution)/shard_map/ppermute | solution.py:61
  81.8 5.5 %shard_map.71 = f32[512,512]{1,0:T(8,128)S(1)} custom-call(s32[5]{0:T(128)S(1)} %stack.38.ids, f32[1024,512]{1,0:T(8,128)S(1)} %copy-done, f32[1024,512]{1,0:T(8,128)S(1)} %collective-permute-done.left, f32[1024,512]{1,0:T(8,128)} %collective-permute-done.2.right, f32[256,512]{1,0:T(8,128)S(1)} %collective-permute-done.3.top, ...), custom_call_target="tpu_custom_call" | custom-call | flops 1024 | bytes 1024 | tf_op jit(solution)/shard_map/pallas_call | solution.py:265
  87.4 5.7 %collective-permute-start.20 = (f32[512,512]{1,0:T(8,128)S(1)}, f32[512,512]{1,0:T(8,128)S(1)}, u32[]{:S(2)}, u32[]{:S(2)}) collective-permute-start(f32[512,512]{1,0:T(8,128)S(1)} %shard_map.71), channel_id=1, source_target_pairs={{0,16},{16,0},{1,17},{17,1},{2,18},{18,2},{3,19},{19,3},{4,20},{20... | collective-permute-start | bytes 3145736 | tf_op jit(solution)/shard_map/ppermute | solution.py:61
  93.0 5.5 %shard_map.72 = f32[512,512]{1,0:T(8,128)S(1)} custom-call(s32[5]{0:T(128)S(1)} %stack.38.ids, f32[1024,512]{1,0:T(8,128)S(1)} %copy-done, f32[1024,512]{1,0:T(8,128)S(1)} %collective-permute-done.left, f32[1024,512]{1,0:T(8,128)} %collective-permute-done.2.right, f32[256,512]{1,0:T(8,128)S(1)} %collective-permute-done.17.top, ...), custom_call_target="tpu_custom_call" | custom-call | flops 1024 | bytes 1024 | tf_op jit(solution)/shard_map/pallas_call | solution.py:265
  98.6 5.5 %collective-permute-start.19 = (f32[512,512]{1,0:T(8,128)S(1)}, f32[512,512]{1,0:T(8,128)S(1)}, u32[]{:S(2)}, u32[]{:S(2)}) collective-permute-start(f32[512,512]{1,0:T(8,128)S(1)} %shard_map.72), channel_id=1, source_target_pairs={{0,16},{16,0},{1,17},{17,1},{2,18},{18,2},{3,19},{19,3},{4,20},{20... | collective-permute-start | bytes 3145736 | tf_op jit(solution)/shard_map/ppermute | solution.py:61
  105.0 5.5 %shard_map.74.mine = f32[512,512]{1,0:T(8,128)S(1)} custom-call(s32[5]{0:T(128)S(1)} %stack.38.ids, f32[1024,512]{1,0:T(8,128)S(1)} %copy-done, f32[1024,512]{1,0:T(8,128)S(1)} %collective-permute-done.left, f32[1024,512]{1,0:T(8,128)} %collective-permute-done.2.right, f32[256,512]{1,0:T(8,128)S(1)} %collective-permute-done.3.top, ...), custom_call_target="tpu_custom_call" | custom-call | flops 1024 | bytes 1024 | tf_op jit(solution)/shard_map/pallas_call | solution.py:265
  110.6 5.5 %shard_map.75.mine = f32[512,512]{1,0:T(8,128)S(1)} custom-call(s32[5]{0:T(128)S(1)} %stack.38.ids, f32[1024,512]{1,0:T(8,128)S(1)} %copy-done, f32[1024,512]{1,0:T(8,128)S(1)} %collective-permute-done.left, f32[1024,512]{1,0:T(8,128)} %collective-permute-done.2.right, f32[256,512]{1,0:T(8,128)S(1)} %collective-permute-done.17.top, ...), custom_call_target="tpu_custom_call" | custom-call | flops 1024 | bytes 1024 | tf_op jit(solution)/shard_map/pallas_call | solution.py:265
  117.1 1.7 shard_map.76
  118.7 19.5 %collective-permute-done.19.received = f32[512,512]{1,0:T(8,128)S(1)} collective-permute-done((f32[512,512]{1,0:T(8,128)S(1)}, f32[512,512]{1,0:T(8,128)S(1)}, u32[]{:S(2)}, u32[]{:S(2)}) %collective-permute-start.19) | collective-permute-done | bytes 1048608 | tf_op jit(solution)/shard_map/ppermute | solution.py:61
  138.3 1.7 shard_map.77
  140.0 19.3 %all_to_all.10.parts = f32[8,264,128]{2,1,0:T(8,128)S(1)} all-to-all(f32[8,264,128]{2,1,0:T(8,128)S(1)} %bitcast.12), channel_id=1, replica_groups=mesh['core'=2,'y'=4,'zl'=2,'zh'=4,'x'=4] {'y','zl'}, dimensions={0} | all-to-all | bytes 2162688 | tf_op jit(solution)/shard_map/all_to_all | solution.py:298
  159.4 17.2 %all_to_all.11 = f32[8,264,128]{2,1,0:T(8,128)S(1)} all-to-all(f32[8,264,128]{2,1,0:T(8,128)S(1)} %shard_map.78), channel_id=1, replica_groups=mesh['core'=2,'y'=4,'zl'=2,'zh'=4,'x'=4] {'y','zl'}, dimensions={0} | all-to-all | bytes 2162688 | tf_op jit(solution)/shard_map/all_to_all | solution.py:298
  176.6 1.7 shard_map.79
  (40 shorter events, 8.3 us)
Async XLA Ops:
  0.6 32.8 %copy-start.3 = (s32[64,32]{0,1:T(8,128)S(1)}, s32[64,32]{0,1:T(8,128)}, u32[]{:S(2)}) copy-start(s32[64,32]{0,1:T(8,128)} %param.9) | copy-start | bytes 24580
  0.6 33.0 %copy-start.2 = (s32[64]{0:T(128)S(1)}, s32[64]{0:T(128)}, u32[]{:S(2)}) copy-start(s32[64]{0:T(128)} %widths.1) | copy-start | bytes 772
  0.6 55.7 %collective-permute-start = (f32[1024,512]{1,0:T(8,128)}, f32[1024,512]{1,0:T(8,128)S(1)}, u32[]{:S(2)}, u32[]{:S(2)}) collective-permute-start(f32[1024,512]{1,0:T(8,128)} %panel.3), channel_id=1, source_target_pairs={{0,32},{32,64},{64,96},{96,0},{1,33},{33,65},{65,97},{97,1},{2,34}... | collective-permute-start | bytes 6291464 | tf_op jit(solution)/shard_map/ppermute | solution.py:61
  2.3 11.3 %collective-permute-start.1 = (f32[512,128]{1,0:T(8,128)}, f32[512,128]{1,0:T(8,128)S(1)}, u32[]{:S(2)}, u32[]{:S(2)}) collective-permute-start(f32[512,128]{1,0:T(8,128)} %param.5), channel_id=1, source_target_pairs={{0,0},{16,4},{8,8},{24,12},{20,20},{4,16},{28,28},{12,24},{1,1},{1... | collective-permute-start | bytes 786440 | tf_op jit(solution)/shard_map/ppermute | solution.py:240
  3.9 25.3 %collective-permute-start.5 = (f32[512,128]{1,0:T(8,128)}, f32[512,128]{1,0:T(8,128)S(1)}, u32[]{:S(2)}, u32[]{:S(2)}) collective-permute-start(f32[512,128]{1,0:T(8,128)} %param.5), channel_id=1, source_target_pairs={{0,12},{16,0},{8,4},{24,8},{20,24},{4,20},{28,16},{12,28},{1,13},{... | collective-permute-start | bytes 786440 | tf_op jit(solution)/shard_map/ppermute | solution.py:240
  11.6 17.6 %collective-permute-start.7 = (f32[512,128]{1,0:T(8,128)}, f32[512,128]{1,0:T(8,128)S(1)}, u32[]{:S(2)}, u32[]{:S(2)}) collective-permute-start(f32[512,128]{1,0:T(8,128)} %param.5), channel_id=1, source_target_pairs={{0,8},{16,12},{8,0},{24,4},{20,28},{4,24},{28,20},{12,16},{1,9},{1... | collective-permute-start | bytes 786440 | tf_op jit(solution)/shard_map/ppermute | solution.py:240
  11.6 18.5 %collective-permute-start.6 = (f32[512,128]{1,0:T(8,128)}, f32[512,128]{1,0:T(8,128)S(1)}, u32[]{:S(2)}, u32[]{:S(2)}) collective-permute-start(f32[512,128]{1,0:T(8,128)} %param.5), channel_id=1, source_target_pairs={{0,4},{16,8},{8,12},{24,0},{20,16},{4,28},{28,24},{12,20},{1,5},{1... | collective-permute-start | bytes 786440 | tf_op jit(solution)/shard_map/ppermute | solution.py:240
  13.6 46.6 %collective-permute-start.2 = (f32[1024,512]{1,0:T(8,128)}, f32[1024,512]{1,0:T(8,128)}, u32[]{:S(2)}, u32[]{:S(2)}) collective-permute-start(f32[1024,512]{1,0:T(8,128)} %panel.3), channel_id=1, source_target_pairs={{0,96},{32,0},{64,32},{96,64},{1,97},{33,1},{65,33},{97,65},{2,98}... | collective-permute-start | bytes 6291464 | tf_op jit(solution)/shard_map/ppermute | solution.py:61
  30.1 25.0 %collective-permute-start.9 = (f32[4,512,128]{2,1,0:T(8,128)S(1)}, f32[4,512,128]{2,1,0:T(8,128)}, u32[]{:S(2)}, u32[]{:S(2)}) collective-permute-start(f32[4,512,128]{2,1,0:T(8,128)S(1)} %pad_maximum_fusion.1.refs_0_), channel_id=1, source_target_pairs={{0,3},{1,0},{2,1},{3,2},{4,7},{5,4},{6,5},{7,6},{8,11},{9,8},{10,9... | collective-permute-start | bytes 3145736 | tf_op jit(solution)/shard_map/ppermute | solution.py:61
  31.1 25.2 %collective-permute-start.8 = (f32[4,512,128]{2,1,0:T(8,128)S(1)}, f32[4,512,128]{2,1,0:T(8,128)}, u32[]{:S(2)}, u32[]{:S(2)}) collective-permute-start(f32[4,512,128]{2,1,0:T(8,128)S(1)} %pad_maximum_fusion.1.refs_0_), channel_id=1, source_target_pairs={{0,1},{1,2},{2,3},{3,0},{4,5},{5,6},{6,7},{7,4},{8,9},{9,10},{10,1... | collective-permute-start | bytes 3145736 | tf_op jit(solution)/shard_map/ppermute | solution.py:61
  34.8 28.2 %collective-permute-start.10 = (f32[4,512,128]{2,1,0:T(8,128)S(1)}, f32[4,512,128]{2,1,0:T(8,128)S(1)}, u32[]{:S(2)}, u32[]{:S(2)}) collective-permute-start(f32[4,512,128]{2,1,0:T(8,128)S(1)} %pad_maximum_fusion.1.refs_0_), channel_id=1, source_target_pairs={{0,128},{128,0},{1,129},{129,1},{2,130},{130,2},{3,131},{131,3},{4... | collective-permute-start | bytes 3145736 | tf_op jit(solution)/shard_map/ppermute | solution.py:61
  55.1 10.7 %collective-permute-start.12 = (f32[4,512,128]{2,1,0:T(8,128)}, f32[4,512,128]{2,1,0:T(8,128)S(1)}, u32[]{:S(2)}, u32[]{:S(2)}) collective-permute-start(f32[4,512,128]{2,1,0:T(8,128)} %collective-permute-done.9.refs_2_), channel_id=1, source_target_pairs={{0,128},{128,0},{1,129},{129,1},{2,130},{130,2},{3,131},{131,3},{4... | collective-permute-start | bytes 3145736 | tf_op jit(solution)/shard_map/ppermute | solution.py:61
  56.2 15.6 %collective-permute-start.14 = (f32[2,512,128]{2,1,0:T(8,128)S(1)}, f32[2,512,128]{2,1,0:T(8,128)S(1)}, u32[]{:S(2)}, u32[]{:S(2)}) collective-permute-start(f32[2,512,128]{2,1,0:T(8,128)S(1)} %slice.27), channel_id=1, source_target_pairs={{0,3},{1,0},{2,1},{3,2},{4,7},{5,4},{6,5},{7,6},{8,11},{9,8},{10,9... | collective-permute-start | bytes 1572872 | tf_op jit(solution)/shard_map/ppermute | solution.py:61
  56.3 10.1 %collective-permute-start.11 = (f32[4,512,128]{2,1,0:T(8,128)}, f32[4,512,128]{2,1,0:T(8,128)S(1)}, u32[]{:S(2)}, u32[]{:S(2)}) collective-permute-start(f32[4,512,128]{2,1,0:T(8,128)} %collective-permute-done.8.refs_1_), channel_id=1, source_target_pairs={{0,128},{128,0},{1,129},{129,1},{2,130},{130,2},{3,131},{131,3},{4... | collective-permute-start | bytes 3145736 | tf_op jit(solution)/shard_map/ppermute | solution.py:61
  60.2 12.9 %collective-permute-start.3 = (f32[256,512]{1,0:T(8,128)S(1)}, f32[256,512]{1,0:T(8,128)S(1)}, u32[]{:S(2)}, u32[]{:S(2)}) collective-permute-start(f32[256,512]{1,0:T(8,128)S(1)} %get-tuple-element.43), channel_id=1, source_target_pairs={{0,32},{32,64},{64,96},{96,0},{1,33},{33,65},{65,97},{97,1},{2,34}... | collective-permute-start | bytes 1572872 | tf_op jit(solution)/shard_map/ppermute | solution.py:61
  63.0 11.4 %collective-permute-start.4 = (f32[256,512]{1,0:T(8,128)S(1)}, f32[256,512]{1,0:T(8,128)S(1)}, u32[]{:S(2)}, u32[]{:S(2)}) collective-permute-start(f32[256,512]{1,0:T(8,128)S(1)} %get-tuple-element.41), channel_id=1, source_target_pairs={{0,96},{32,0},{64,32},{96,64},{1,97},{33,1},{65,33},{97,65},{2,98}... | collective-permute-start | bytes 1572872 | tf_op jit(solution)/shard_map/ppermute | solution.py:61
  65.9 11.2 %collective-permute-start.13 = (f32[2,512,128]{2,1,0:T(8,128)S(1)}, f32[2,512,128]{2,1,0:T(8,128)S(1)}, u32[]{:S(2)}, u32[]{:S(2)}) collective-permute-start(f32[2,512,128]{2,1,0:T(8,128)S(1)} %slice.26), channel_id=1, source_target_pairs={{0,1},{1,2},{2,3},{3,0},{4,5},{5,6},{6,7},{7,4},{8,9},{9,10},{10,1... | collective-permute-start | bytes 1572872 | tf_op jit(solution)/shard_map/ppermute | solution.py:61
  69.5 12.3 %copy-start = (f32[1024,512]{1,0:T(8,128)S(1)}, f32[1024,512]{1,0:T(8,128)}, u32[]{:S(2)}) copy-start(f32[1024,512]{1,0:T(8,128)} %panel.3) | copy-start | bytes 6291460
  77.1 3.8 %collective-permute-start.15 = (f32[2,512,128]{2,1,0:T(8,128)S(1)}, f32[2,512,128]{2,1,0:T(8,128)S(1)}, u32[]{:S(2)}, u32[]{:S(2)}) collective-permute-start(f32[2,512,128]{2,1,0:T(8,128)S(1)} %collective-permute-done.13.refs_0_), channel_id=1, source_target_pairs={{0,128},{128,0},{1,129},{129,1},{2,130},{130,2},{3,131},{131,3},{4... | collective-permute-start | bytes 1572872 | tf_op jit(solution)/shard_map/ppermute | solution.py:61
  77.1 3.8 %collective-permute-start.16 = (f32[2,512,128]{2,1,0:T(8,128)S(1)}, f32[2,512,128]{2,1,0:T(8,128)S(1)}, u32[]{:S(2)}, u32[]{:S(2)}) collective-permute-start(f32[2,512,128]{2,1,0:T(8,128)S(1)} %collective-permute-done.14.refs_1_), channel_id=1, source_target_pairs={{0,128},{128,0},{1,129},{129,1},{2,130},{130,2},{3,131},{131,3},{4... | collective-permute-start | bytes 1572872 | tf_op jit(solution)/shard_map/ppermute | solution.py:61
  77.6 15.4 %collective-permute-start.17 = (f32[256,512]{1,0:T(8,128)S(1)}, f32[256,512]{1,0:T(8,128)S(1)}, u32[]{:S(2)}, u32[]{:S(2)}) collective-permute-start(f32[256,512]{1,0:T(8,128)S(1)} %get-tuple-element.42), channel_id=1, source_target_pairs={{0,32},{32,64},{64,96},{96,0},{1,33},{33,65},{65,97},{97,1},{2,34}... | collective-permute-start | bytes 1572872 | tf_op jit(solution)/shard_map/ppermute | solution.py:61
  77.9 15.1 %collective-permute-start.18 = (f32[256,512]{1,0:T(8,128)S(1)}, f32[256,512]{1,0:T(8,128)S(1)}, u32[]{:S(2)}, u32[]{:S(2)}) collective-permute-start(f32[256,512]{1,0:T(8,128)S(1)} %get-tuple-element.40), channel_id=1, source_target_pairs={{0,96},{32,0},{64,32},{96,64},{1,97},{33,1},{65,33},{97,65},{2,98}... | collective-permute-start | bytes 1572872 | tf_op jit(solution)/shard_map/ppermute | solution.py:61
  87.4 29.7 %collective-permute-start.20 = (f32[512,512]{1,0:T(8,128)S(1)}, f32[512,512]{1,0:T(8,128)S(1)}, u32[]{:S(2)}, u32[]{:S(2)}) collective-permute-start(f32[512,512]{1,0:T(8,128)S(1)} %shard_map.71), channel_id=1, source_target_pairs={{0,16},{16,0},{1,17},{17,1},{2,18},{18,2},{3,19},{19,3},{4,20},{20... | collective-permute-start | bytes 3145736 | tf_op jit(solution)/shard_map/ppermute | solution.py:61
  98.6 39.7 %collective-permute-start.19 = (f32[512,512]{1,0:T(8,128)S(1)}, f32[512,512]{1,0:T(8,128)S(1)}, u32[]{:S(2)}, u32[]{:S(2)}) collective-permute-start(f32[512,512]{1,0:T(8,128)S(1)} %shard_map.72), channel_id=1, source_target_pairs={{0,16},{16,0},{1,17},{17,1},{2,18},{18,2},{3,19},{19,3},{4,20},{20... | collective-permute-start | bytes 3145736 | tf_op jit(solution)/shard_map/ppermute | solution.py:61
  159.4 17.3 %copy-start.1 = (f32[1024,512]{1,0:T(8,128)S(1)}, f32[1024,512]{1,0:T(8,128)}, u32[]{:S(2)}) copy-start(f32[1024,512]{1,0:T(8,128)} %diag.1) | copy-start | bytes 6291460
